TPU v7x, 32 devices: a whole 2x2x4 slice. The times are simulated.
32 devices in a mesh: dp: 4 (over y, core), seq: 8 (over z, x).
Axes of the slice: x: 2, y: 2, z: 4, core: 2. Of those that a mesh axis runs over, the one named last changes fastest.
Arguments:
- tok_ids: int32 [4, 2048], P('dp'), may hold values from 0 to 31999, as said below
- targets: int32 [4, 512], P('dp'), may hold values from 0 to 31999
- positions: int32 [4, 512], P('dp'), may hold values from 0 to 2047, as said below
- answer_mask: int32 [4, 512], replicated, may hold values from 0 to 1, as said below
- emb: float32 [32000, 2048], P('dp', 'seq'), may hold values from -6 to 6
- head: float32 [32000, 2048], P('seq', 'dp'), may hold values from -0.5745243 to 0.5745243
- attn_w: float32 [2048, 4608], P(('dp', 'seq')), may hold values from -1.06066017 to 1.06066017
- mlp_w: float32 [2048, 16896], P(('dp', 'seq')), may hold values from -0.13258252 to 0.13258252
- gains: float32 [3, 2048], P(None, ('dp', 'seq')), may hold values from 0.48 to 2.16
- emb_row: float32 [32000], P('dp'), may hold values from 7.45284975e-11 to 9.9868187e-09
- emb_col: float32 [2048], P('seq'), may hold values from 4.47171e-10 to 3.8754819e-09
- head_row: float32 [32000], P('seq'), may hold values from 1.5258789e-09 to 2.0446777e-07
- head_col: float32 [2048], P('dp'), may hold values from 9.15527344e-09 to 7.93457e-08
- attn_row: float32 [2048], P(('dp', 'seq')), may hold values from 6.2421453e-06 to 5.4098593e-05
- attn_col: float32 [4608], replicated, may hold values from 6.2421453e-06 to 5.4098593e-05
- mlp_row: float32 [2048], P(('dp', 'seq')), may hold values from 5.78706915e-08 to 5.0154599e-07
- mlp_col: float32 [16896], replicated, may hold values from 5.78706915e-08 to 5.0154599e-07
- gains_moment: float32 [3, 2048], P(None, ('dp', 'seq')), may hold values from 1.31607056e-07 to 7.8037691e-05
Outputs:
- loss_sum: float32 [], replicated
- valid_count: float32 [], replicated
- emb_grad: float32 [32000, 2048], P('dp', 'seq')
- emb_new: float32 [32000, 2048], P('dp', 'seq')
- emb_row_new: float32 [32000], P('dp')
- emb_col_new: float32 [2048], P('seq')
- head_grad: float32 [32000, 2048], P('seq', 'dp')
- head_new: float32 [32000, 2048], P('seq', 'dp')
- head_row_new: float32 [32000], P('seq')
- head_col_new: float32 [2048], P('dp')
- attn_grad: float32 [2048, 4608], P(('dp', 'seq'))
- attn_new: float32 [2048, 4608], P(('dp', 'seq'))
- attn_row_new: float32 [2048], P(('dp', 'seq'))
- attn_col_new: float32 [4608], replicated
- mlp_grad: float32 [2048, 16896], P(('dp', 'seq'))
- mlp_new: float32 [2048, 16896], P(('dp', 'seq'))
- mlp_row_new: float32 [2048], P(('dp', 'seq'))
- mlp_col_new: float32 [16896], replicated
- gains_grad: float32 [3, 2048], P(None, ('dp', 'seq'))
- gains_moment_new: float32 [3, 2048], P(None, ('dp', 'seq'))
- gains_new: float32 [3, 2048], P(None, ('dp', 'seq'))
Inputs may be any that keep to these rules, and one draw needn't show every extreme that they name: `positions`: distinct and increasing within a row; the first is 0 and the last 2047. `answer_mask`: every row has a 1 in its first place. `tok_ids`: at each answer position the token equals the target there.
All inputs are finite; a program needn't handle non-finite values.
Results may differ from a plain program's by a relative error of at most 0.025.
The roundings to bfloat16 on the way count: a program that leaves them out, or rounds other values in their place, can miss the bound.
Values may be sent and summed in bfloat16 or wider, within the bound.
A program may use at most 640 MiB of HBM per device.

v0:
```python
import math

import jax
import jax.numpy as jnp
from jax import lax
from jax.sharding import PartitionSpec as P

D = 2048
HEADS = 32
KVH = 4
HD = 64
FF = 5632
VOCAB = 32000
QKV = 2560


eps_norm = 1e-05
eps_square = 1e-30
decay_rate = 0.5
learn_rate = 1.0
zloss_weight = 0.0001
orig_context = 2048.0
yarn_factor = 4.0
highest = lax.Precision.HIGHEST


def combined_all(value, axis, combine):
    everything = jax.tree.map(lambda part: lax.all_gather(part, axis), value)
    leading = jax.tree.map(lambda part: part[0], everything)

    def lap(k, so_far):
        return combine(so_far, jax.tree.map(lambda part: part[k], everything))

    return lax.fori_loop(1, lax.axis_size(axis), lap, leading)


def yarn_tables(places):
    halves = jnp.arange(HD // 2, dtype=jnp.float32)
    inverse = jnp.power(10000.0, -2.0 * halves / HD)
    ratio = orig_context * inverse / (2.0 * math.pi)
    ramp_part = jnp.clip((ratio - 1.0) / 31.0, 0.0, 1.0)
    frequency = inverse / yarn_factor * (1.0 - ramp_part) + inverse * ramp_part
    angles = places[:, None] * frequency[None, :]
    magnitude = 0.1 * math.log(yarn_factor) + 1.0
    return (jnp.cos(angles) * magnitude, jnp.sin(angles) * magnitude)


def rotate(values, cosine, sine):
    first = values[..., : HD // 2]
    second = values[..., HD // 2 :]
    cosine_row = cosine[:, None, :]
    sine_row = sine[:, None, :]
    return jnp.concatenate(
        [first * cosine_row - second * sine_row, second * cosine_row + first * sine_row], -1
    )


def unrotate(values, cosine, sine):
    first = values[..., : HD // 2]
    second = values[..., HD // 2 :]
    cosine_row = cosine[:, None, :]
    sine_row = sine[:, None, :]
    return jnp.concatenate(
        [first * cosine_row + second * sine_row, second * cosine_row - first * sine_row], -1
    )


def rms_norm(values, gain_row):
    return values * lax.rsqrt(jnp.mean(values * values, -1, keepdims=True) + eps_norm) * gain_row


def norm_back(values, gain_row, upstream):
    factor = lax.rsqrt(jnp.mean(values * values, -1, keepdims=True) + eps_norm)
    normed = values * factor
    gain_grad = jnp.sum(upstream * normed, 0)
    inner = upstream * gain_row
    return (factor * (inner - normed * jnp.mean(inner * normed, -1, keepdims=True)), gain_grad)


def matmul(left, right):
    return jnp.dot(left, right, preferred_element_type=jnp.float32)


def matmul_nt(left, right):
    return lax.dot_general(
        left, right, (((1,), (1,)), ((), ())), preferred_element_type=jnp.float32
    )


def matmul_tn(left, right):
    return lax.dot_general(
        left, right, (((0,), (0,)), ((), ())), preferred_element_type=jnp.float32
    )


def combine_stats(first, second):
    larger = jnp.maximum(first[0], second[0])
    summed = first[1] * jnp.exp(first[0] - larger) + second[1] * jnp.exp(second[0] - larger)
    return (larger, summed, first[2] + second[2])


def gather_layer(attn_w, mlp_w, gains):
    return (
        lax.all_gather(attn_w.astype(jnp.bfloat16), ("dp", "seq"), axis=0, tiled=True),
        lax.all_gather(mlp_w.astype(jnp.bfloat16), ("dp", "seq"), axis=0, tiled=True),
        lax.all_gather(gains.astype(jnp.bfloat16), ("dp", "seq"), axis=1, tiled=True),
    )


def gather_keys(keys, values):
    return (
        lax.all_gather(keys, "seq", axis=0, tiled=True),
        lax.all_gather(values, "seq", axis=0, tiled=True),
    )


def attend_piece(carry, piece, start, queries, query_first):
    keys, values = piece
    total = keys.shape[0]
    block = math.gcd(total, 512)
    tokens = queries.shape[0]
    query_last = query_first + tokens - 1
    key_blocks = keys.reshape(total // block, block, KVH, HD)
    value_blocks = values.reshape(total // block, block, KVH, HD)
    starts = start + jnp.arange(total // block, dtype=jnp.int32) * block
    query_pos = query_first + jnp.arange(tokens, dtype=jnp.int32)

    def one_step(state, blocks):
        key_block, value_block, block_start = blocks

        def compute(inner):
            running, highest_seen, denominator = inner
            scores = jnp.einsum(
                "qgho,kgo->ghqk", queries, key_block, preferred_element_type=jnp.float32
            ) * HD ** (-0.5)
            allowed = (block_start + jnp.arange(block, dtype=jnp.int32))[None, :] <= query_pos[
                :, None
            ]
            scores = jnp.where(allowed, scores, -1e30)
            new_high = jnp.maximum(highest_seen, jnp.max(scores, -1))
            fade = jnp.exp(highest_seen - new_high)
            weights = jnp.where(allowed, jnp.exp(scores - new_high[..., None]), 0.0)
            denominator = fade * denominator + jnp.sum(weights, -1)
            running = fade[..., None] * running + jnp.einsum(
                "ghqk,kgo->ghqo",
                weights.astype(jnp.bfloat16),
                value_block,
                preferred_element_type=jnp.float32,
            )
            return (running, new_high, denominator)

        return (lax.cond(block_start <= query_last, compute, lambda inner: inner, state), None)

    carry, unused = lax.scan(one_step, carry, (key_blocks, value_blocks, starts))
    return carry


def attend_back(queries, grad_out, log_total, delta, key_all, value_all, query_first):
    total = key_all.shape[0]
    block = math.gcd(total, 512)
    tokens = queries.shape[0]
    query_last = query_first + tokens - 1
    key_blocks = key_all.reshape(total // block, block, KVH, HD)
    value_blocks = value_all.reshape(total // block, block, KVH, HD)
    starts = jnp.arange(total // block, dtype=jnp.int32) * block
    query_pos = query_first + jnp.arange(tokens, dtype=jnp.int32)
    scale = HD ** (-0.5)

    def one_step(query_grad, blocks):
        key_block, value_block, block_start = blocks

        def compute(unused):
            scores = (
                jnp.einsum("qgho,kgo->ghqk", queries, key_block, preferred_element_type=jnp.float32)
                * scale
            )
            allowed = (block_start + jnp.arange(block, dtype=jnp.int32))[None, :] <= query_pos[
                :, None
            ]
            weights = jnp.where(allowed, jnp.exp(scores - log_total[..., None]), 0.0)
            weight_grad = jnp.einsum(
                "qgho,kgo->ghqk", grad_out, value_block, preferred_element_type=jnp.float32
            )
            score_grad = (weights * (weight_grad - delta[..., None])).astype(jnp.bfloat16)
            add_query = (
                jnp.einsum(
                    "ghqk,kgo->qgho", score_grad, key_block, preferred_element_type=jnp.float32
                )
                * scale
            )
            key_grad = (
                jnp.einsum(
                    "ghqk,qgho->kgo", score_grad, queries, preferred_element_type=jnp.float32
                )
                * scale
            )
            value_grad = jnp.einsum(
                "ghqk,qgho->kgo",
                weights.astype(jnp.bfloat16),
                grad_out,
                preferred_element_type=jnp.float32,
            )
            return (add_query, key_grad, value_grad)

        def skipped(unused):
            empty = jnp.zeros((block, KVH, HD), jnp.float32)
            return (jnp.zeros_like(query_grad), empty, empty)

        add_query, key_grad, value_grad = lax.cond(
            block_start <= query_last, compute, skipped, None
        )
        return (query_grad + add_query, (key_grad, value_grad))

    start_grad = jnp.zeros((tokens, KVH, HEADS // KVH, HD), jnp.float32)
    query_grad, stacked = lax.scan(one_step, start_grad, (key_blocks, value_blocks, starts))
    return (query_grad, stacked[0].reshape(total, KVH * HD), stacked[1].reshape(total, KVH * HD))


def finish(weight, update, weight_square, entries):
    return weight - learn_rate * jnp.maximum(0.001, jnp.sqrt(weight_square / entries)) * update


def on_device(
    tok_ids,
    targets,
    positions,
    answer_mask,
    emb,
    head,
    attn_w,
    mlp_w,
    gains,
    emb_row,
    emb_col,
    head_row,
    head_col,
    attn_row,
    attn_col,
    mlp_row,
    mlp_col,
    gains_moment,
):
    seq_size = lax.axis_size("seq")
    seq_rank = lax.axis_index("seq")
    dp_rank = lax.axis_index("dp")
    seqlen = tok_ids.shape[1]
    tokens = seqlen // seq_size
    group = HEADS // KVH
    kv_width = KVH * HD
    attn_full, mlp_full, gain_low = gather_layer(attn_w, mlp_w, gains)
    gain_float = gain_low.astype(jnp.float32)
    emb_cols, head_rows = (
        lax.all_gather(emb.astype(jnp.bfloat16), "dp", axis=0, tiled=True),
        lax.all_gather(head.astype(jnp.bfloat16), "dp", axis=1, tiled=True),
    )
    token_row = tok_ids[0]
    looked = jnp.take(emb_cols, token_row, axis=0)
    start_x = lax.all_to_all(looked, "seq", split_axis=0, concat_axis=1, tiled=True).astype(
        jnp.float32
    )
    query_first = seq_rank * tokens
    query_pos = query_first + jnp.arange(tokens, dtype=jnp.int32)
    cosine, sine = yarn_tables(query_pos.astype(jnp.float32))
    normed = rms_norm(start_x, gain_float[0]).astype(jnp.bfloat16)
    projected = matmul(normed, attn_full[:, :QKV])
    queries = (
        rotate(projected[:, :D].reshape(tokens, HEADS, HD), cosine, sine)
        .astype(jnp.bfloat16)
        .reshape(tokens, KVH, group, HD)
    )
    keys = (
        rotate(projected[:, D : D + kv_width].reshape(tokens, KVH, HD), cosine, sine)
        .astype(jnp.bfloat16)
        .reshape(tokens, kv_width)
    )
    values = projected[:, D + kv_width :].astype(jnp.bfloat16)
    initial = (
        jnp.zeros((KVH, group, tokens, HD), jnp.float32),
        jnp.full((KVH, group, tokens), -1e30, jnp.float32),
        jnp.zeros((KVH, group, tokens), jnp.float32),
    )
    key_all, value_all = gather_keys(keys, values)
    running, highest_seen, denominator = attend_piece(
        initial, (key_all, value_all), 0, queries, query_first
    )
    log_total = highest_seen + jnp.log(denominator)
    attended = jnp.transpose(running / denominator[..., None], (2, 0, 1, 3))
    attended_low = attended.reshape(tokens, D).astype(jnp.bfloat16)
    middle = start_x + matmul_nt(attended_low, attn_full[:, QKV:])
    normed_two = rms_norm(middle, gain_float[1]).astype(jnp.bfloat16)
    gate_up = matmul(normed_two, mlp_full[:, : 2 * FF])
    gate = gate_up[:, :FF]
    upward = gate_up[:, FF:]
    mixed = (jax.nn.silu(gate) * upward).astype(jnp.bfloat16)
    ending = middle + matmul_nt(mixed, mlp_full[:, 2 * FF :])
    final = rms_norm(ending, gain_float[2]).astype(jnp.bfloat16)
    select = positions[0][:, None] == query_pos[None, :]
    picked = matmul(select.astype(jnp.bfloat16), final)
    chosen = lax.psum(picked.astype(jnp.bfloat16), "seq")
    logits = matmul_nt(chosen, head_rows)
    vocab_part = head_rows.shape[0]
    target_hit = (
        targets[0][:, None]
        == seq_rank * vocab_part + jnp.arange(vocab_part, dtype=jnp.int32)[None, :]
    )
    part_high = jnp.max(logits, 1)
    part_sum = jnp.sum(jnp.exp(logits - part_high[:, None]), 1)
    part_target = jnp.sum(jnp.where(target_hit, logits, 0.0), 1)
    all_high, all_sum_exp, target_logit = combined_all(
        (part_high, part_sum, part_target), "seq", combine_stats
    )
    row_total = all_high + jnp.log(all_sum_exp)
    mask_float = answer_mask.astype(jnp.float32)
    count = jnp.sum(mask_float)
    own_mask = lax.dynamic_slice_in_dim(mask_float, dp_rank, 1, 0)[0]
    loss_part = jnp.where(
        seq_rank == 0,
        jnp.sum(own_mask * (row_total - target_logit + zloss_weight * row_total * row_total)),
        0.0,
    )
    probs = jnp.exp(logits - row_total[:, None])
    logit_grad = (
        (own_mask / count)[:, None]
        * (probs * (1.0 + 2.0 * zloss_weight * row_total)[:, None] - target_hit.astype(jnp.float32))
    ).astype(jnp.bfloat16)
    head_rows_grad = matmul_tn(logit_grad, chosen)
    chosen_grad = lax.psum(matmul(logit_grad, head_rows).astype(jnp.bfloat16), "seq").astype(
        jnp.float32
    )
    final_grad = jnp.dot(select.astype(jnp.float32).T, chosen_grad, precision=highest)
    ending_grad, final_gain_grad = norm_back(ending, gain_float[2], final_grad)
    branch_grad = ending_grad.astype(jnp.bfloat16)
    down_grad = matmul_tn(branch_grad, mixed)
    mixed_grad = matmul(branch_grad, mlp_full[:, 2 * FF :])
    sigmoid_gate = jax.nn.sigmoid(gate)
    gate_grad = mixed_grad * upward * sigmoid_gate * (1.0 + gate * (1.0 - sigmoid_gate))
    upward_grad = mixed_grad * gate * sigmoid_gate
    gate_up_grad = jnp.concatenate([gate_grad, upward_grad], 1).astype(jnp.bfloat16)
    mlp_term = jnp.concatenate([matmul_tn(normed_two, gate_up_grad), down_grad], 1)
    middle_part, middle_gain_grad = norm_back(
        middle, gain_float[1], matmul_nt(gate_up_grad, mlp_full[:, : 2 * FF])
    )
    middle_grad = ending_grad + middle_part
    attn_branch_grad = middle_grad.astype(jnp.bfloat16)
    output_proj_grad = matmul_tn(attn_branch_grad, attended_low)
    attended_grad = matmul(attn_branch_grad, attn_full[:, QKV:]).astype(jnp.bfloat16)
    grad_out = attended_grad.reshape(tokens, KVH, group, HD)
    delta = jnp.einsum("qgho,qgho->ghq", grad_out.astype(jnp.float32), attended)
    query_grad, key_term, value_term = attend_back(
        queries, grad_out, log_total, delta, key_all, value_all, query_first
    )
    key_grad, value_grad = (
        lax.psum_scatter(
            key_term.astype(jnp.bfloat16), "seq", scatter_dimension=0, tiled=True
        ).astype(jnp.float32),
        lax.psum_scatter(
            value_term.astype(jnp.bfloat16), "seq", scatter_dimension=0, tiled=True
        ).astype(jnp.float32),
    )
    query_raw = unrotate(query_grad.reshape(tokens, HEADS, HD), cosine, sine).reshape(tokens, D)
    key_raw = unrotate(key_grad.reshape(tokens, KVH, HD), cosine, sine).reshape(tokens, kv_width)
    projected_grad = jnp.concatenate([query_raw, key_raw, value_grad], 1).astype(jnp.bfloat16)
    attn_term = jnp.concatenate([matmul_tn(normed, projected_grad), output_proj_grad], 1)
    start_part, start_gain_grad = norm_back(
        start_x, gain_float[0], matmul_nt(projected_grad, attn_full[:, :QKV])
    )
    start_grad = middle_grad + start_part
    gains_term = jnp.stack([start_gain_grad, middle_gain_grad, final_gain_grad])
    attn_grad, mlp_grad, gains_grad = (
        lax.psum_scatter(attn_term, ("dp", "seq"), scatter_dimension=0, tiled=True),
        lax.psum_scatter(mlp_term, ("dp", "seq"), scatter_dimension=0, tiled=True),
        lax.psum_scatter(gains_term, ("dp", "seq"), scatter_dimension=1, tiled=True),
    )
    back_rows = lax.all_to_all(
        start_grad.astype(jnp.bfloat16), "seq", split_axis=1, concat_axis=0, tiled=True
    ).astype(start_grad.dtype)
    emb_cols_grad = (
        jnp.zeros((emb_cols.shape[0], back_rows.shape[1]), jnp.float32).at[token_row].add(back_rows)
    )
    emb_grad, head_grad = (
        lax.psum_scatter(
            emb_cols_grad.astype(jnp.bfloat16), "dp", scatter_dimension=0, tiled=True
        ).astype(jnp.float32),
        lax.psum_scatter(
            head_rows_grad.astype(jnp.bfloat16), "dp", scatter_dimension=1, tiled=True
        ).astype(jnp.float32),
    )
    attn_square = attn_grad * attn_grad + eps_square
    mlp_square = mlp_grad * mlp_grad + eps_square
    emb_square = emb_grad * emb_grad + eps_square
    head_square = head_grad * head_grad + eps_square
    attn_row_new = decay_rate * attn_row + (1.0 - decay_rate) * jnp.mean(attn_square, 1)
    mlp_row_new = decay_rate * mlp_row + (1.0 - decay_rate) * jnp.mean(mlp_square, 1)
    emb_rows_n = emb.shape[0]
    emb_cols_n = emb.shape[1]
    head_rows_n = head.shape[0]
    head_cols_n = head.shape[1]
    emb_row_part = lax.dynamic_update_slice(
        jnp.zeros((VOCAB,), jnp.float32), jnp.sum(emb_square, 1), (dp_rank * emb_rows_n,)
    )
    emb_col_part = lax.dynamic_update_slice(
        jnp.zeros((D,), jnp.float32), jnp.sum(emb_square, 0), (seq_rank * emb_cols_n,)
    )
    head_row_part = lax.dynamic_update_slice(
        jnp.zeros((VOCAB,), jnp.float32), jnp.sum(head_square, 1), (seq_rank * head_rows_n,)
    )
    head_col_part = lax.dynamic_update_slice(
        jnp.zeros((D,), jnp.float32), jnp.sum(head_square, 0), (dp_rank * head_cols_n,)
    )
    scalars = jnp.stack(
        [
            loss_part,
            jnp.sum(attn_row_new),
            jnp.sum(attn_w * attn_w),
            jnp.sum(mlp_row_new),
            jnp.sum(mlp_w * mlp_w),
            jnp.where(seq_rank == 0, jnp.sum(emb_row), 0.0),
            jnp.sum(emb * emb),
            jnp.where(dp_rank == 0, jnp.sum(head_row), 0.0),
            jnp.sum(head * head),
            jnp.sum(gains * gains),
        ]
    )
    attn_cols_sum, mlp_cols_sum, emb_row_sum, emb_col_sum, head_row_sum, head_col_sum, totals = (
        lax.psum(
            (
                jnp.sum(attn_square, 0),
                jnp.sum(mlp_square, 0),
                emb_row_part,
                emb_col_part,
                head_row_part,
                head_col_part,
                scalars,
            ),
            ("dp", "seq"),
        )
    )
    attn_col_new = decay_rate * attn_col + (1.0 - decay_rate) * attn_cols_sum / D
    mlp_col_new = decay_rate * mlp_col + (1.0 - decay_rate) * mlp_cols_sum / D
    attn_update = attn_grad * lax.rsqrt(
        attn_row_new[:, None] * attn_col_new[None, :] / (totals[1] / D)
    )
    mlp_update = mlp_grad * lax.rsqrt(mlp_row_new[:, None] * mlp_col_new[None, :] / (totals[3] / D))
    emb_row_new = (
        decay_rate * emb_row
        + (1.0 - decay_rate)
        * lax.dynamic_slice_in_dim(emb_row_sum, dp_rank * emb_rows_n, emb_rows_n)
        / D
    )
    emb_col_new = (
        decay_rate * emb_col
        + (1.0 - decay_rate)
        * lax.dynamic_slice_in_dim(emb_col_sum, seq_rank * emb_cols_n, emb_cols_n)
        / VOCAB
    )
    emb_mean = (decay_rate * totals[5] + (1.0 - decay_rate) * jnp.sum(emb_row_sum) / D) / VOCAB
    emb_update = emb_grad * lax.rsqrt(emb_row_new[:, None] * emb_col_new[None, :] / emb_mean)
    head_row_new = (
        decay_rate * head_row
        + (1.0 - decay_rate)
        * lax.dynamic_slice_in_dim(head_row_sum, seq_rank * head_rows_n, head_rows_n)
        / D
    )
    head_col_new = (
        decay_rate * head_col
        + (1.0 - decay_rate)
        * lax.dynamic_slice_in_dim(head_col_sum, dp_rank * head_cols_n, head_cols_n)
        / VOCAB
    )
    head_mean = (decay_rate * totals[7] + (1.0 - decay_rate) * jnp.sum(head_row_sum) / D) / VOCAB
    head_update = head_grad * lax.rsqrt(head_row_new[:, None] * head_col_new[None, :] / head_mean)
    moment_new = decay_rate * gains_moment + (1.0 - decay_rate) * (
        gains_grad * gains_grad + eps_square
    )
    gains_update = gains_grad * lax.rsqrt(moment_new)
    attn_new = finish(attn_w, attn_update, totals[2], D * (QKV + D))
    mlp_new = finish(mlp_w, mlp_update, totals[4], D * 3 * FF)
    emb_new = finish(emb, emb_update, totals[6], VOCAB * D)
    head_new = finish(head, head_update, totals[8], VOCAB * D)
    gains_new = finish(gains, gains_update, totals[9], 3 * D)
    return (
        totals[0],
        count,
        emb_grad,
        emb_new,
        emb_row_new,
        emb_col_new,
        head_grad,
        head_new,
        head_row_new,
        head_col_new,
        attn_grad,
        attn_new,
        attn_row_new,
        attn_col_new,
        mlp_grad,
        mlp_new,
        mlp_row_new,
        mlp_col_new,
        gains_grad,
        moment_new,
        gains_new,
    )


def solution(mesh):
    return jax.shard_map(
        on_device,
        mesh=mesh,
        in_specs=(
            P("dp", None),
            P("dp", None),
            P("dp", None),
            P(),
            P("dp", "seq"),
            P("seq", "dp"),
            P(("dp", "seq"), None),
            P(("dp", "seq"), None),
            P(None, ("dp", "seq")),
            P("dp"),
            P("seq"),
            P("seq"),
            P("dp"),
            P(("dp", "seq")),
            P(),
            P(("dp", "seq")),
            P(),
            P(None, ("dp", "seq")),
        ),
        out_specs=(
            P(),
            P(),
            P("dp", "seq"),
            P("dp", "seq"),
            P("dp"),
            P("seq"),
            P("seq", "dp"),
            P("seq", "dp"),
            P("seq"),
            P("dp"),
            P(("dp", "seq"), None),
            P(("dp", "seq"), None),
            P(("dp", "seq")),
            P(),
            P(("dp", "seq"), None),
            P(("dp", "seq"), None),
            P(("dp", "seq")),
            P(),
            P(None, ("dp", "seq")),
            P(None, ("dp", "seq")),
            P(None, ("dp", "seq")),
        ),
        check_vma=False,
    )
```

profile of v0, /device:TPU:0, one launch (start us, length us, event | category | flops | bytes accessed | tf_op | source)
XLA Modules:
  0.0 3665.4 jit_solution(7017499080139646577)
XLA Ops:
  22.4 101.7 %all-gather.14.cloned.1.call-done = bf16[32000,256]{1,0:T(8,128)(2,1)} async-done(((bf16[8000,256]{1,0:T(8,128)(2,1)}), bf16[32000,256]{1,0:T(8,128)(2,1)}) %all-gather.14.cloned.1.call-update) | async-done | bytes 16384016 | tf_op jit(solution)/shard_map/all_gather | solution.py:253
  145.9 97.5 %all-gather.3 = bf16[32,64,3]{1,2,0:T(4,128)(2,1)S(1)} all-gather(bf16[1,64,3]{1,2,0:T(4,128)(2,1)S(1)} %get-tuple-element.794), channel_id=1, replica_groups=mesh['dp'=4,'seq'=8] {'dp','seq'}, dimensions={0}, use_global_device_ids=true | all-gather | bytes 12672 | tf_op jit(solution)/shard_map/all_gather | solution.py:106
  313.4 39.6 %all-gather.20.cloned.1.call-done = bf16[2048,256]{1,0:T(8,128)(2,1)} async-done(((bf16[256,256]{1,0:T(8,128)(2,1)}), bf16[2048,256]{1,0:T(8,128)(2,1)}) %all-gather.20.cloned.1.call-update) | async-done | bytes 1048592 | tf_op jit(solution)/shard_map/all_gather | solution.py:113
  393.3 328.1 %all-gather.22.cloned.1.call-done = bf16[2048,16896]{1,0:T(8,128)(2,1)} async-done(((bf16[64,16896]{1,0:T(8,128)(2,1)}), bf16[2048,16896]{1,0:T(8,128)(2,1)}) %all-gather.22.cloned.1.call-update) | async-done | bytes 69206032 | tf_op jit(solution)/shard_map/all_gather | solution.py:105
  721.4 29.0 fusion.49
  772.0 53.3 %all-gather.24.cloned.1.call-done = bf16[4000,2048]{1,0:T(8,128)(2,1)} async-done(((bf16[4000,512]{1,0:T(8,128)(2,1)}), bf16[4000,2048]{1,0:T(8,128)(2,1)}) %all-gather.24.cloned.1.call-update) | async-done | bytes 16384016 | tf_op jit(solution)/shard_map/all_gather | solution.py:254
  825.3 106.1 %all-reduce.7.cloned.1.call-done = bf16[512,2048]{1,0:T(8,128)(2,1)} async-done(((bf16[512,2048]{1,0:T(8,128)(2,1)}), bf16[512,2048]{1,0:T(8,128)(2,1)}) %all-reduce.7.cloned.1.call-update) | async-done | bytes 2097168 | tf_op jit(solution)/shard_map/psum | solution.py:299
  949.8 26.0 all-gather.5
  975.8 26.0 all-gather.6
  1001.8 26.0 all-gather.4
  1049.3 99.2 %all-reduce.9.cloned.1.call-done = bf16[512,2048]{1,0:T(8,128)(2,1)} async-done(((bf16[512,2048]{1,0:T(8,128)(2,1)}), bf16[512,2048]{1,0:T(8,128)(2,1)}) %all-reduce.9.cloned.1.call-update) | async-done | bytes 2097168 | tf_op jit(solution)/shard_map/psum | solution.py:327
  1209.0 58.8 %while.51 = (s32[]{:T(128)}, f32[256,4,8,64]{0,3,2,1:T(8,128)}, bf16[4,512,4,64]{1,3,2,0:T(8,128)(2,1)}, bf16[4,512,4,64]{1,3,2,0:T(8,128)(2,1)}, s32[4]{0:T(128...) while((s32[]{:T(128)}, f32[256,4,8,64]{0,3,2,1:T(8,128)}, ...), condition=%wide.region_23.24_spmd.clone, body=%wide.region_20.23_spmd.clone.sunk | while | flops 2728264448 | bytes 95136064 | solution.py:215
  1210.6 31.9 conditional.7
  1274.2 153.3 %reduce-scatter.12.cloned.1.call-done = bf16[256,256]{0,1:T(8,128)(2,1)} async-done(((bf16[2048,256]{0,1:T(8,128)(2,1)}), bf16[256,256]{0,1:T(8,128)(2,1)}) %reduce-scatter.12.cloned.1.call-update) | async-done | bytes 131088 | tf_op jit(solution)/shard_map/reduce_scatter | solution.py:353
  1428.4 66.2 %reduce-scatter.14.cloned.1.call-done = bf16[256,256]{0,1:T(8,128)(2,1)} async-done(((bf16[2048,256]{0,1:T(8,128)(2,1)}), bf16[256,256]{0,1:T(8,128)(2,1)}) %reduce-scatter.14.cloned.1.call-update) | async-done | bytes 131088 | tf_op jit(solution)/shard_map/reduce_scatter | solution.py:356
  1525.8 30.0 all_to_all.23
  1646.3 25.7 fusion.98
  1672.0 36.8 %fusion.75 = f32[2048,11264]{1,0:T(8,128)} fusion(bf16[256,5632]{1,0:T(8,128)(2,1)} %get-tuple-element.769, bf16[256,5632]{1,0:T(8,128)(2,1)} %get-tuple-element.768, f32[256,2048]{1,0:T(8,128)} %get-tuple-element.810, f32[2048]{0:T(1024)S(1)} %bitcast.247, f32[256]{0:T(256)S(1)} %copy-done.34), kind=kOutput, calls=%fused_computation.111 | convolution fusion | flops 11824267264 | bytes 100148224 | tf_op jit(solution)/shard_map/dot_general | solution.py:91
  1708.8 94.8 %pad_maximum_fusion = f32[2048,16896]{1,0:T(8,128)} fusion(f32[2048,5632]{1,0:T(8,128)} %fusion.98, f32[2048,11264]{1,0:T(8,128)} %fusion.75), kind=kLoop, calls=%fused_computation.63 | loop fusion | flops 34603008 | bytes 276824064 | tf_op jit(solution)/shard_map/concatenate | solution.py:339
  1813.3 76.6 %reduce-scatter.18.cloned.1.call-done = bf16[8000,256]{1,0:T(8,128)(2,1)} async-done(((bf16[32000,256]{1,0:T(8,128)(2,1)}), bf16[8000,256]{1,0:T(8,128)(2,1)}) %reduce-scatter.18.cloned.1.call-update) | async-done | bytes 4096016 | tf_op jit(solution)/shard_map/reduce_scatter | solution.py:381
  1897.8 348.9 %reduce-scatter.16.cloned.1.call-done = f32[64,4608]{1,0:T(8,128)} async-done(((f32[2048,4608]{1,0:T(8,128)}), f32[64,4608]{1,0:T(8,128)}) %reduce-scatter.16.cloned.1.call-update) | async-done | bytes 1179664 | tf_op jit(solution)/shard_map/reduce_scatter | solution.py:370
  2248.8 1188.6 %reduce-scatter.24.cloned.1.call-done = f32[64,16896]{1,0:T(8,128)} async-done(((f32[2048,16896]{1,0:T(8,128)}), f32[64,16896]{1,0:T(8,128)}) %reduce-scatter.24.cloned.1.call-update) | async-done | bytes 4325392
  3441.6 130.3 %all-reduce.11.cloned.1.call-done = (f32[32000]{0:T(1024)}, f32[32000]{0:T(1024)}, f32[16896]{0:T(1024)}) async-done(((f32[32000]{0:T(1024)}, f32[32000]{0:T(1024)}, f32[16896]{0:T(1024)}), (f32[32000]{0:T(1024)}, f32[32000]{0:T(1024)}, f32[16896]{0:T(1024)})) %all-reduce.11.cloned.1.call-update) | async-done | bytes 323600 | tf_op jit(solution)/shard_map/psum | solution.py:425
  3585.1 41.9 %all-reduce.1 = (f32[10]{0:T(128)S(1)}, f32[2048]{0:T(1024)S(1)}, f32[2048]{0:T(1024)S(1)}, f32[4608]{0:T(1024)S(1)}) all-reduce(f32[10]{0:T(128)S(1)} %stack.55, f32[2048]{0:T(1024)S(1)} %dynamic_update_slice.20, f32[2048]{0:T(1024)S(1)} %dynamic_update_slice.22, ...), channel_id=1, replica_groups=mesh['dp'=4,'seq'=8] {'dp','seq'}, use_global_device_ids=true, to_apply=%region_39.40 | all-reduce | flops 8714 | bytes 69712 | tf_op jit(solution)/shard_map/psum | solution.py:425
  (435 shorter events, 546.2 us)
Async XLA Ops:
  7.2 116.9 %all-gather.14.cloned.1.call-start = ((), (), s32[]{:S(2)}) async-start(), calls=%async_computation.9 | async-start | bytes 20480000 | tf_op jit(solution)/shard_map/all_gather | solution.py:253
  17.5 247.8 %all-gather.16.cloned.1.call-start = ((), (), s32[]{:S(2)}) async-start(), calls=%async_computation.10 | async-start | bytes 19464192 | tf_op jit(solution)/shard_map/all_gather | solution.py:104
  139.7 104.7 %all-to-all-start = ((bf16[8,256,256]{2,1,0:T(8,128)(2,1)}), bf16[8,256,256]{2,1,0:T(8,128)(2,1)S(1)}, u32[]{:S(2)}, u32[]{:S(2)}) async-start(bf16[8,256,256]{2,1,0:T(8,128)(2,1)} %broadcast_select_fusion), calls=%async_computation | async-start | bytes 2097152 | tf_op jit(solution)/shard_map/all_to_all | solution.py:258
  145.2 166.1 %all-gather.18.cloned.1.call-start = ((), (), s32[]{:S(2)}) async-start(), calls=%async_computation.11 | async-start | bytes 1179648 | tf_op jit(solution)/shard_map/all_gather | solution.py:112
  273.4 79.5 %all-gather.20.cloned.1.call-start = ((), (), s32[]{:S(2)}) async-start(), calls=%async_computation.12 | async-start | bytes 1179648 | tf_op jit(solution)/shard_map/all_gather | solution.py:113
  275.1 446.3 %all-gather.22.cloned.1.call-start = ((), (), s32[]{:S(2)}) async-start(), calls=%async_computation.13 | async-start | bytes 71368704 | tf_op jit(solution)/shard_map/all_gather | solution.py:105
  281.7 543.6 %all-gather.24.cloned.1.call-start = ((), (), s32[]{:S(2)}) async-start(), calls=%async_computation.15 | async-start | bytes 20480000 | tf_op jit(solution)/shard_map/all_gather | solution.py:254
  292.2 639.3 %all-reduce.7.cloned.1.call-start = ((), (), s32[]{:S(2)}) async-start(), calls=%async_computation.14 | async-start | bytes 4194304 | tf_op jit(solution)/shard_map/psum | solution.py:299
  771.3 377.1 %all-reduce.9.cloned.1.call-start = ((), (), s32[]{:S(2)}) async-start(), calls=%async_computation.16 | async-start | bytes 4194304 | tf_op jit(solution)/shard_map/psum | solution.py:327
  1049.2 378.2 %reduce-scatter.12.cloned.1.call-start = ((), (), s32[]{:S(2)}) async-start(), calls=%async_computation.17 | async-start | bytes 1179648 | tf_op jit(solution)/shard_map/reduce_scatter | solution.py:353
  1271.3 223.3 %reduce-scatter.14.cloned.1.call-start = ((), (), s32[]{:S(2)}) async-start(), calls=%async_computation.18 | async-start | bytes 1179648 | tf_op jit(solution)/shard_map/reduce_scatter | solution.py:356
  1273.5 531.1 %reduce-scatter.22.cloned.1.call-start = ((), (), s32[]{:S(2)}) async-start(), calls=%async_computation.22 | async-start | bytes 1081344
  1505.2 300.1 %reduce-scatter.20.cloned.1.call-start = ((), (), s32[]{:S(2)}) async-start(), calls=%async_computation.21 | async-start | bytes 20480000 | tf_op jit(solution)/shard_map/reduce_scatter | solution.py:384
  1521.4 368.5 %reduce-scatter.18.cloned.1.call-start = ((), (), s32[]{:S(2)}) async-start(), calls=%async_computation.20 | async-start | bytes 20480000 | tf_op jit(solution)/shard_map/reduce_scatter | solution.py:381
  1599.1 647.6 %reduce-scatter.16.cloned.1.call-start = ((), (), s32[]{:S(2)}) async-start(), calls=%async_computation.19 | async-start | bytes 38928384 | tf_op jit(solution)/shard_map/reduce_scatter | solution.py:370
  1644.2 1793.3 %reduce-scatter.24.cloned.1.call-start = ((), (), s32[]{:S(2)}) async-start(), calls=%async_computation.23 | async-start | bytes 142737408
  1803.6 1768.3 %all-reduce.11.cloned.1.call-start = ((), (), s32[]{:S(2)}) async-start(), calls=%async_computation.24 | async-start | bytes 663552 | tf_op jit(solution)/shard_map/psum | solution.py:425
  1805.4 1829.5 %copy-start.60 = (f32[3,64]{1,0:T(4,128)}, f32[3,64]{1,0:T(4,128)S(1)}, u32[]{:S(2)}) copy-start(f32[3,64]{1,0:T(4,128)S(1)} %copy.129) | copy-start | bytes 2308
  1896.8 1736.9 %copy-start.42 = (f32[16896]{0:T(1024)S(1)}, f32[16896]{0:T(1024)}, u32[]{:S(2)}) copy-start(f32[16896]{0:T(1024)} %param.44) | copy-start | bytes 202756
  1896.8 1737.8 %copy-start.75 = (f32[256]{0:T(256)S(1)}, f32[256]{0:T(256)}, u32[]{:S(2)}) copy-start(f32[256]{0:T(256)} %param.38) | copy-start | bytes 3076
  1896.8 1737.9 %copy-start.69 = (f32[512]{0:T(512)S(1)}, f32[512]{0:T(512)}, u32[]{:S(2)}) copy-start(f32[512]{0:T(512)} %param.40) | copy-start | bytes 6148
  1896.8 1738.0 %copy-start.53 = (f32[4608]{0:T(1024)S(1)}, f32[4608]{0:T(1024)}, u32[]{:S(2)}) copy-start(f32[4608]{0:T(1024)} %param.42) | copy-start | bytes 55300
  1896.8 1738.0 %copy-start.59 = (f32[3,64]{1,0:T(4,128)S(1)}, f32[3,64]{1,0:T(4,128)}, u32[]{:S(2)}) copy-start(f32[3,64]{1,0:T(4,128)} %param.36) | copy-start | bytes 2308
  1896.9 1738.0 %copy-start.70 = (f32[3,64]{1,0:T(4,128)S(1)}, f32[3,64]{1,0:T(4,128)}, u32[]{:S(2)}) copy-start(f32[3,64]{1,0:T(4,128)} %param.45) | copy-start | bytes 2308
  (81 other events, 12807.3 us)
Sparse Core Ops, SparseCore 0:
  17.6 106.3 all-gather.13
  127.6 137.6 all-gather.15
  273.5 37.7 all-gather.17
  313.8 39.0 all-gather.19
  356.3 365.0 all-gather.21
  723.4 101.8 all-gather.23
  829.5 101.8 all-reduce.6
  1049.3 99.0 all-reduce.8
  1271.4 155.9 reduce-scatter.11
  1431.6 62.9 reduce-scatter.13
  1505.3 135.0 reduce-scatter.21
  1643.1 120.3 reduce-scatter.19
  1766.1 123.7 reduce-scatter.17
  1897.9 348.6 reduce-scatter.15
  2253.5 1183.8 reduce-scatter.23
  3445.2 126.6 all-reduce.10
where the time goes:
time: 3680 us; the launch traced here: 3670 us
  waiting for transfers between devices  2730 us (74%)
  other arithmetic  285 us (8%)
  matrix products  285 us (8%)
  blocking collectives  247 us (7%)
  local copies, waits for them, and re-layouts  83.5 us (2%)
    unnamed x18, waiting for transfers between devices  1190 us
    reduce_scatter x1, waiting for transfers between devices, on_device(): lax.psum_scatter(attn_term, ('dp', 'seq'), scatter_dimension=0, tiled=True)  349 us
    all_gather x1, waiting for transfers between devices, gather_layer(): lax.all_gather(mlp_w.astype(jnp.bfloat16), ('dp', 'seq'), axis=0, tiled=T...  328 us
    reduce_scatter x1, waiting for transfers between devices, on_device(): lax.psum_scatter(key_term.astype(jnp.bfloat16), 'seq', scatter_dimension=...  153 us
    psum x1, waiting for transfers between devices, on_device(): lax.psum((jnp.sum(attn_square, 0), jnp.sum(mlp_square, 0), emb_row_part,...  130 us
    psum x1, waiting for transfers between devices, on_device(): chosen = lax.psum(picked.astype(jnp.bfloat16), 'seq')  106 us
    all_gather x1, waiting for transfers between devices, on_device(): lax.all_gather(emb.astype(jnp.bfloat16), 'dp', axis=0, tiled=True)  102 us
    psum x1, waiting for transfers between devices, on_device(): lax.psum(matmul(logit_grad, head_rows).astype(jnp.bfloat16), 'seq')  99.2 us
  transfers between devices with their start and end apart: 17, of which 14 were waited for; matrix products, arithmetic and copies ran while one was open for 11% of the time, Pallas kernels for 0%

commit v1 on v0

v1 whole, which is shorter than its diff:
```python
import math

import jax
import jax.numpy as jnp
from jax import lax
from jax.sharding import PartitionSpec as P

D = 2048
HEADS = 32
KVH = 4
HD = 64
FF = 5632
VOCAB = 32000
QKV = 2560


eps_norm = 1e-05
eps_square = 1e-30
decay_rate = 0.5
learn_rate = 1.0
zloss_weight = 0.0001
orig_context = 2048.0
yarn_factor = 4.0
highest = lax.Precision.HIGHEST


def yarn_tables(places):
    halves = jnp.arange(HD // 2, dtype=jnp.float32)
    inverse = jnp.power(10000.0, -2.0 * halves / HD)
    ratio = orig_context * inverse / (2.0 * math.pi)
    ramp_part = jnp.clip((ratio - 1.0) / 31.0, 0.0, 1.0)
    frequency = inverse / yarn_factor * (1.0 - ramp_part) + inverse * ramp_part
    angles = places[:, None] * frequency[None, :]
    magnitude = 0.1 * math.log(yarn_factor) + 1.0
    return (jnp.cos(angles) * magnitude, jnp.sin(angles) * magnitude)


def rotate(values, cosine, sine):
    first = values[..., : HD // 2]
    second = values[..., HD // 2 :]
    cosine_row = cosine[:, None, :]
    sine_row = sine[:, None, :]
    return jnp.concatenate(
        [first * cosine_row - second * sine_row, second * cosine_row + first * sine_row], -1
    )


def unrotate(values, cosine, sine):
    first = values[..., : HD // 2]
    second = values[..., HD // 2 :]
    cosine_row = cosine[:, None, :]
    sine_row = sine[:, None, :]
    return jnp.concatenate(
        [first * cosine_row + second * sine_row, second * cosine_row - first * sine_row], -1
    )


def rms_norm(values, gain_row):
    return values * lax.rsqrt(jnp.mean(values * values, -1, keepdims=True) + eps_norm) * gain_row


def norm_back(values, gain_row, upstream):
    factor = lax.rsqrt(jnp.mean(values * values, -1, keepdims=True) + eps_norm)
    normed = values * factor
    gain_grad = jnp.sum(upstream * normed, 0)
    inner = upstream * gain_row
    return (factor * (inner - normed * jnp.mean(inner * normed, -1, keepdims=True)), gain_grad)


def matmul(left, right):
    return jnp.dot(left, right, preferred_element_type=jnp.float32)


def matmul_nt(left, right):
    return lax.dot_general(
        left, right, (((1,), (1,)), ((), ())), preferred_element_type=jnp.float32
    )


def matmul_tn(left, right):
    return lax.dot_general(
        left, right, (((0,), (0,)), ((), ())), preferred_element_type=jnp.float32
    )


def finish(weight, update, weight_square, entries):
    return weight - learn_rate * jnp.maximum(0.001, jnp.sqrt(weight_square / entries)) * update


low = jnp.bfloat16
full = jnp.float32


class Place:
    def __init__(self):
        self.seqs = lax.axis_size("seq")
        self.dps = lax.axis_size("dp")
        self.dp = lax.axis_index("dp")
        self.s = lax.axis_index("seq")
        self.his = self.seqs // 2
        self.y, self.c = self.dp // 2, self.dp % 2
        self.hi, self.lo = self.s // 2, self.s % 2
        self.t = self.dp * 2 + self.lo

    def send(self, value, dy=0, dc=0, dlo=0, up=0):
        pairs = []
        for d in range(self.dps):
            for s in range(self.seqs):
                to_d = d ^ (2 * dy + dc)
                to_s = ((s // 2 + up) % self.his) * 2 + ((s % 2) ^ dlo)
                pairs.append((d * self.seqs + s, to_d * self.seqs + to_s))
        return lax.ppermute(value, ("dp", "seq"), pairs)


def pick(array, index, axis):
    return lax.dynamic_index_in_dim(array, index, axis, keepdims=False)


def put(array, block, index, axis):
    return lax.dynamic_update_slice_in_dim(array, jnp.expand_dims(block, axis), index, axis)


def plane_parts(k):
    return dict(dy=(k >> 2) & 1, dc=(k >> 1) & 1, dlo=k & 1)


def plane_swap(pl, blocks):
    out = put(jnp.zeros_like(blocks), pick(blocks, pl.t, 0), pl.t, 0)
    for k in range(1, 8):
        out = put(out, pl.send(pick(blocks, pl.t ^ k, 0), **plane_parts(k)), pl.t ^ k, 0)
    return out


def plane_gather(pl, rows):
    first = [rows] + [pl.send(rows, dy=j >> 1, dlo=j & 1) for j in (1, 2, 3)]
    first = jnp.stack(first)
    return jnp.stack([first, pl.send(first, dc=1)]).reshape(8 * rows.shape[0], rows.shape[1])


def plane_scatter(pl, part):
    part = part.reshape(2, 4, part.shape[0] // 8, part.shape[1])
    both = part[0] + pl.send(part[1].astype(low), dc=1).astype(full)
    total = both[0]
    for j in (1, 2, 3):
        total = total + pl.send(both[j].astype(low), dy=j >> 1, dlo=j & 1).astype(full)
    return total


def ring_sum(pl, part, axis):
    n = pl.his
    acc = pick(part, (pl.hi + n - 1) % n, axis).astype(low)
    for j in range(1, n):
        got = pl.send(acc, up=1).astype(full)
        acc = got + pick(part, (pl.hi + 2 * n - 1 - j) % n, axis).astype(full)
        if j < n - 1:
            acc = acc.astype(low)
    return acc


def halve(pl, part, mine, axis, **way):
    got = pl.send(pick(part, 1 - mine, axis).astype(low), **way)
    return pick(part, mine, axis).astype(full) + got.astype(full)


def layer_scatter(pl, part):
    part = part.astype(low)
    columns = part.shape[-1]
    cut = columns // 256 * 128
    first, second = part[..., :cut], part[..., cut:]
    first = halve(pl, halve(pl, first, pl.y, 0, dy=1), pl.lo, 1, dlo=1)
    second = halve(pl, halve(pl, second, pl.lo, 2, dlo=1), pl.y, 0, dy=1)
    return jnp.concatenate([ring_sum(pl, first, 0), ring_sum(pl, second, 0)], -1)


def seq_sum(value):
    n = lax.axis_size("seq")
    got = lax.all_to_all(value.astype(low), "seq", split_axis=0, concat_axis=0, tiled=True)
    return jnp.sum(got.reshape(n, value.shape[0] // n, value.shape[1]).astype(full), 0)


def attend(queries, keys, values, places):
    allowed = jnp.arange(keys.shape[0], dtype=jnp.int32)[None, :] <= places[:, None]
    scores = jnp.einsum(
        "qgho,kgo->ghqk", queries, keys, preferred_element_type=full
    ) * HD ** (-0.5)
    scores = jnp.where(allowed, scores, -1e30)
    high = jnp.max(scores, -1)
    weights = jnp.exp(scores - high[..., None])
    denominator = jnp.sum(weights, -1)
    out = jnp.einsum(
        "ghqk,kgo->ghqo", weights.astype(low), values, preferred_element_type=full
    )
    out = jnp.transpose(out / denominator[..., None], (2, 0, 1, 3))
    return out, high + jnp.log(denominator)


def attend_back(queries, grad_out, log_total, delta, keys, values, places):
    allowed = jnp.arange(keys.shape[0], dtype=jnp.int32)[None, :] <= places[:, None]
    scale = HD ** (-0.5)
    scores = jnp.einsum("qgho,kgo->ghqk", queries, keys, preferred_element_type=full) * scale
    weights = jnp.where(allowed, jnp.exp(scores - log_total[..., None]), 0.0)
    weight_grad = jnp.einsum("qgho,kgo->ghqk", grad_out, values, preferred_element_type=full)
    score_grad = (weights * (weight_grad - delta[..., None])).astype(low)
    query_grad = (
        jnp.einsum("ghqk,kgo->qgho", score_grad, keys, preferred_element_type=full) * scale
    )
    key_grad = (
        jnp.einsum("ghqk,qgho->kgo", score_grad, queries, preferred_element_type=full) * scale
    )
    value_grad = jnp.einsum(
        "ghqk,qgho->kgo", weights.astype(low), grad_out, preferred_element_type=full
    )
    return query_grad, key_grad, value_grad


def on_device(
    tok_ids,
    targets,
    positions,
    answer_mask,
    emb,
    head,
    attn_w,
    mlp_w,
    gains,
    emb_row,
    emb_col,
    head_row,
    head_col,
    attn_row,
    attn_col,
    mlp_row,
    mlp_col,
    gains_moment,
):
    pl = Place()
    seqs, his = pl.seqs, pl.his
    tokens = tok_ids.shape[1] // seqs
    picks = targets.shape[1] // seqs
    group = HEADS // KVH
    kv_width = KVH * HD
    block = D // (pl.dps * seqs)
    emb_n, emb_m = emb.shape
    part = FF // 8

    attn_block = jnp.concatenate(
        [attn_w, jnp.pad(gains.T, ((0, 0), (0, 125)))], 1
    ).astype(low)
    attn_full = lax.all_gather(attn_block, ("dp", "seq"), axis=0, tiled=True)
    gain_float = attn_full[:, QKV + D : QKV + D + 3].astype(full).T
    head_rows = lax.all_gather(head.astype(low), "dp", axis=1, tiled=True)
    mlp_blocks = jnp.transpose(mlp_w.astype(low).reshape(block, 3, 8, part), (2, 0, 1, 3))
    mlp_plane = plane_swap(pl, mlp_blocks.reshape(8, block, 3 * part))
    mlp_full = jnp.zeros((pl.dps, his, 2, block, 3 * part), low)
    moving = mlp_plane.reshape(pl.dps, 2, block, 3 * part)
    mlp_full = put(mlp_full, moving, pl.hi, 1)
    for j in range(1, his):
        moving = pl.send(moving, up=1)
        mlp_full = put(mlp_full, moving, (pl.hi + his - j) % his, 1)
    mlp_full = mlp_full.reshape(D, 3 * part)

    ids = jnp.concatenate([tok_ids.reshape(seqs, tokens), targets.reshape(seqs, picks)], 1)
    ids = ids.reshape(seqs * (tokens + picks))
    ids_two = jnp.stack([ids, pl.send(ids, dy=1)])
    emb_low = emb.astype(low)
    chip_low = jnp.concatenate([emb_low, pl.send(emb_low, dc=1), jnp.zeros((8, emb_m), low)])
    local = ids_two - pl.dp * emb_n
    other = ids_two - (pl.dp ^ 1) * emb_n
    places_in = jnp.where(
        (local >= 0) & (local < emb_n),
        local,
        jnp.where((other >= 0) & (other < emb_n), other + emb_n, 2 * emb_n),
    )
    looked = jnp.take(chip_low, places_in[1], axis=0)
    looked = jnp.take(chip_low, places_in[0], axis=0) + pl.send(looked, dy=1)
    start = lax.all_to_all(looked, "seq", split_axis=0, concat_axis=1, tiled=True).astype(full)
    start_tok, start_pick = start[:tokens], start[tokens:]

    token_pos = pl.s * tokens + jnp.arange(tokens, dtype=jnp.int32)
    pick_pos = lax.dynamic_slice_in_dim(positions[0], pl.s * picks, picks)
    cosine, sine = yarn_tables(token_pos.astype(full))
    pick_cosine, pick_sine = yarn_tables(pick_pos.astype(full))
    normed = rms_norm(start, gain_float[0]).astype(low)
    normed_tok, normed_pick = normed[:tokens], normed[tokens:]
    projected = matmul(normed_tok, attn_full[:, D:QKV])
    keys = rotate(projected[:, :kv_width].reshape(tokens, KVH, HD), cosine, sine).astype(low)
    both = jnp.concatenate(
        [keys.reshape(tokens, kv_width), projected[:, kv_width:].astype(low)], 1
    )
    both = lax.all_gather(both, "seq", axis=0, tiled=True)
    key_all = both[:, :kv_width].reshape(-1, KVH, HD)
    value_all = both[:, kv_width:].reshape(-1, KVH, HD)
    queries = (
        rotate(
            matmul(normed_pick, attn_full[:, :D]).reshape(picks, HEADS, HD),
            pick_cosine,
            pick_sine,
        )
        .astype(low)
        .reshape(picks, KVH, group, HD)
    )
    attended, log_total = attend(queries, key_all, value_all, pick_pos)
    attended_low = attended.reshape(picks, D).astype(low)
    middle = start_pick + matmul_nt(attended_low, attn_full[:, QKV : QKV + D])
    normed_two = plane_gather(pl, rms_norm(middle, gain_float[1]).astype(low))
    gate_up = matmul(normed_two, mlp_full[:, : 2 * part])
    gate = gate_up[:, :part]
    upward = gate_up[:, part:]
    mixed = (jax.nn.silu(gate) * upward).astype(low)
    ending = middle + plane_scatter(pl, matmul_nt(mixed, mlp_full[:, 2 * part :]))
    final = rms_norm(ending, gain_float[2]).astype(low)
    chosen = lax.all_gather(final, "seq", axis=0, tiled=True)
    logits = matmul_nt(chosen, head_rows)
    vocab_part = head_rows.shape[0]
    target_hit = (
        targets[0][:, None]
        == pl.s * vocab_part + jnp.arange(vocab_part, dtype=jnp.int32)[None, :]
    )
    part_high = jnp.max(logits, 1)
    part_sum = jnp.sum(jnp.exp(logits - part_high[:, None]), 1)
    part_target = jnp.sum(jnp.where(target_hit, logits, 0.0), 1)
    stats = lax.all_gather(jnp.stack([part_high, part_sum, part_target]), "seq")
    all_high = jnp.max(stats[:, 0], 0)
    all_sum_exp = jnp.sum(stats[:, 1] * jnp.exp(stats[:, 0] - all_high), 0)
    target_logit = jnp.sum(stats[:, 2], 0)
    row_total = all_high + jnp.log(all_sum_exp)
    mask_float = answer_mask.astype(full)
    count = jnp.sum(mask_float)
    own_mask = lax.dynamic_slice_in_dim(mask_float, pl.dp, 1, 0)[0]
    loss_part = jnp.where(
        pl.s == 0,
        jnp.sum(own_mask * (row_total - target_logit + zloss_weight * row_total * row_total)),
        0.0,
    )
    probs = jnp.exp(logits - row_total[:, None])
    logit_grad = (
        (own_mask / count)[:, None]
        * (probs * (1.0 + 2.0 * zloss_weight * row_total)[:, None] - target_hit.astype(full))
    ).astype(low)
    head_rows_grad = matmul_tn(logit_grad, chosen)
    head_grad = lax.psum_scatter(
        head_rows_grad.astype(low), "dp", scatter_dimension=1, tiled=True
    ).astype(full)
    final_grad = seq_sum(matmul(logit_grad, head_rows))
    ending_grad, final_gain_grad = norm_back(ending, gain_float[2], final_grad)
    branch_grad = plane_gather(pl, ending_grad.astype(low))
    down_grad = matmul_tn(branch_grad, mixed)
    mixed_grad = matmul(branch_grad, mlp_full[:, 2 * part :])
    sigmoid_gate = jax.nn.sigmoid(gate)
    gate_grad = mixed_grad * upward * sigmoid_gate * (1.0 + gate * (1.0 - sigmoid_gate))
    upward_grad = mixed_grad * gate * sigmoid_gate
    gate_up_grad = jnp.concatenate([gate_grad, upward_grad], 1).astype(low)
    mlp_term = jnp.concatenate([matmul_tn(normed_two, gate_up_grad), down_grad], 1)
    mlp_term = ring_sum(
        pl, mlp_term.astype(low).reshape(pl.dps, his, 2, block, 3 * part), 1
    )
    mlp_term = plane_swap(pl, mlp_term.astype(low).reshape(8, block, 3 * part))
    mlp_grad = (
        jnp.transpose(mlp_term.reshape(8, block, 3, part), (1, 2, 0, 3))
        .reshape(block, 3 * FF)
        .astype(full)
    )
    middle_part, middle_gain_grad = norm_back(
        middle, gain_float[1], plane_scatter(pl, matmul_nt(gate_up_grad, mlp_full[:, : 2 * part]))
    )
    middle_grad = ending_grad + middle_part
    attn_branch_grad = middle_grad.astype(low)
    attended_grad = matmul(attn_branch_grad, attn_full[:, QKV : QKV + D]).astype(low)
    grad_out = attended_grad.reshape(picks, KVH, group, HD)
    delta = jnp.einsum("qgho,qgho->ghq", grad_out.astype(full), attended)
    query_grad, key_term, value_term = attend_back(
        queries, grad_out, log_total, delta, key_all, value_all, pick_pos
    )
    kv_grad = seq_sum(
        jnp.concatenate([key_term.reshape(-1, kv_width), value_term.reshape(-1, kv_width)], 1)
    )
    query_raw = (
        unrotate(query_grad.reshape(picks, HEADS, HD), pick_cosine, pick_sine)
        .reshape(picks, D)
        .astype(low)
    )
    key_raw = unrotate(kv_grad[:, :kv_width].reshape(tokens, KVH, HD), cosine, sine)
    kv_raw = jnp.concatenate(
        [key_raw.reshape(tokens, kv_width), kv_grad[:, kv_width:]], 1
    ).astype(low)
    tok_up = matmul_nt(kv_raw, attn_full[:, D:QKV])
    pick_up = matmul_nt(query_raw, attn_full[:, :D])
    start_part, start_gain_grad = norm_back(
        start, gain_float[0], jnp.concatenate([tok_up, pick_up], 0)
    )
    start_grad = jnp.concatenate(
        [start_part[:tokens], start_part[tokens:] + middle_grad], 0
    ).astype(low)

    gains_term = jnp.stack([start_gain_grad, middle_gain_grad, final_gain_grad], 1)

    def by_core(rows, core):
        rows = rows.reshape(rows.shape[0], 2, 2, seqs * block)
        return pick(rows, core, 2).reshape(rows.shape[0], D // 2)

    def attn_term(core):
        return jnp.concatenate(
            [
                matmul_tn(by_core(normed_pick, core), query_raw),
                matmul_tn(by_core(normed_tok, core), kv_raw),
                matmul_tn(by_core(attn_branch_grad, core), attended_low),
                jnp.pad(by_core(gains_term.T, core).T, ((0, 0), (0, 125))),
            ],
            1,
        )

    attn_sum = attn_term(pl.c) + pl.send(attn_term(1 - pl.c).astype(low), dc=1).astype(full)
    attn_sum = layer_scatter(pl, attn_sum.reshape(2, his, 2, block, attn_sum.shape[-1]))
    attn_grad = attn_sum[:, : QKV + D]
    gains_grad = attn_sum[:, QKV + D : QKV + D + 3].T

    back_rows = lax.all_to_all(start_grad, "seq", split_axis=1, concat_axis=0, tiled=True)
    back_two = jnp.concatenate([back_rows, pl.send(back_rows, dy=1)], 0)
    chip_grad = (
        jnp.zeros((2 * emb_n + 8, emb_m), full).at[places_in.reshape(-1)].add(back_two.astype(full))
    )
    emb_grad = chip_grad[:emb_n] + pl.send(chip_grad[emb_n : 2 * emb_n], dc=1)

    attn_square = attn_grad * attn_grad + eps_square
    mlp_square = mlp_grad * mlp_grad + eps_square
    emb_square = emb_grad * emb_grad + eps_square
    head_square = head_grad * head_grad + eps_square
    attn_row_new = decay_rate * attn_row + (1.0 - decay_rate) * jnp.mean(attn_square, 1)
    mlp_row_new = decay_rate * mlp_row + (1.0 - decay_rate) * jnp.mean(mlp_square, 1)
    emb_rows = jnp.sum(emb_square, 1)
    head_rows_sum = jnp.sum(head_square, 1)
    scalars = jnp.stack(
        [
            loss_part,
            jnp.sum(attn_row_new),
            jnp.sum(attn_w * attn_w),
            jnp.sum(mlp_row_new),
            jnp.sum(mlp_w * mlp_w),
            jnp.where(pl.s == 0, jnp.sum(emb_row), 0.0),
            jnp.sum(emb * emb),
            jnp.where(pl.dp == 0, jnp.sum(head_row), 0.0),
            jnp.sum(head * head),
            jnp.sum(gains * gains),
            jnp.sum(emb_rows),
            jnp.sum(head_rows_sum),
        ]
    )
    attn_cols_sum, mlp_cols_sum, totals = lax.psum(
        (jnp.sum(attn_square, 0), jnp.sum(mlp_square, 0), scalars), ("dp", "seq")
    )
    emb_row_sum, head_col_sum = lax.psum((emb_rows, jnp.sum(head_square, 0)), "seq")
    head_row_sum, emb_col_sum = lax.psum((head_rows_sum, jnp.sum(emb_square, 0)), "dp")
    attn_col_new = decay_rate * attn_col + (1.0 - decay_rate) * attn_cols_sum / D
    mlp_col_new = decay_rate * mlp_col + (1.0 - decay_rate) * mlp_cols_sum / D
    attn_update = attn_grad * lax.rsqrt(
        attn_row_new[:, None] * attn_col_new[None, :] / (totals[1] / D)
    )
    mlp_update = mlp_grad * lax.rsqrt(mlp_row_new[:, None] * mlp_col_new[None, :] / (totals[3] / D))
    emb_row_new = decay_rate * emb_row + (1.0 - decay_rate) * emb_row_sum / D
    emb_col_new = decay_rate * emb_col + (1.0 - decay_rate) * emb_col_sum / VOCAB
    emb_mean = (decay_rate * totals[5] + (1.0 - decay_rate) * totals[10] / D) / VOCAB
    emb_update = emb_grad * lax.rsqrt(emb_row_new[:, None] * emb_col_new[None, :] / emb_mean)
    head_row_new = decay_rate * head_row + (1.0 - decay_rate) * head_row_sum / D
    head_col_new = decay_rate * head_col + (1.0 - decay_rate) * head_col_sum / VOCAB
    head_mean = (decay_rate * totals[7] + (1.0 - decay_rate) * totals[11] / D) / VOCAB
    head_update = head_grad * lax.rsqrt(head_row_new[:, None] * head_col_new[None, :] / head_mean)
    moment_new = decay_rate * gains_moment + (1.0 - decay_rate) * (
        gains_grad * gains_grad + eps_square
    )
    gains_update = gains_grad * lax.rsqrt(moment_new)
    attn_new = finish(attn_w, attn_update, totals[2], D * (QKV + D))
    mlp_new = finish(mlp_w, mlp_update, totals[4], D * 3 * FF)
    emb_new = finish(emb, emb_update, totals[6], VOCAB * D)
    head_new = finish(head, head_update, totals[8], VOCAB * D)
    gains_new = finish(gains, gains_update, totals[9], 3 * D)
    return (
        totals[0],
        count,
        emb_grad,
        emb_new,
        emb_row_new,
        emb_col_new,
        head_grad,
        head_new,
        head_row_new,
        head_col_new,
        attn_grad,
        attn_new,
        attn_row_new,
        attn_col_new,
        mlp_grad,
        mlp_new,
        mlp_row_new,
        mlp_col_new,
        gains_grad,
        moment_new,
        gains_new,
    )


def solution(mesh):
    return jax.shard_map(
        on_device,
        mesh=mesh,
        in_specs=(
            P("dp", None),
            P("dp", None),
            P("dp", None),
            P(),
            P("dp", "seq"),
            P("seq", "dp"),
            P(("dp", "seq"), None),
            P(("dp", "seq"), None),
            P(None, ("dp", "seq")),
            P("dp"),
            P("seq"),
            P("seq"),
            P("dp"),
            P(("dp", "seq")),
            P(),
            P(("dp", "seq")),
            P(),
            P(None, ("dp", "seq")),
        ),
        out_specs=(
            P(),
            P(),
            P("dp", "seq"),
            P("dp", "seq"),
            P("dp"),
            P("seq"),
            P("seq", "dp"),
            P("seq", "dp"),
            P("seq"),
            P("dp"),
            P(("dp", "seq"), None),
            P(("dp", "seq"), None),
            P(("dp", "seq")),
            P(),
            P(("dp", "seq"), None),
            P(("dp", "seq"), None),
            P(("dp", "seq")),
            P(),
            P(None, ("dp", "seq")),
            P(None, ("dp", "seq")),
            P(None, ("dp", "seq")),
        ),
        check_vma=False,
    )
```

time: 3680 us -> 1460 us (0.40)
  waiting for transfers between devices: 2730 us -> 627 us
  matrix products: 285 us -> 151 us
  local copies, waits for them, and re-layouts: 83.5 us -> 171 us
  other arithmetic: 285 us -> 223 us
  blocking collectives: 247 us -> 195 us
  starting transfers between devices: 7.23 us -> 53 us
    unnamed x18 -> x6, waiting for transfers between devices: 1190 us -> 0.1 us
    reduce_scatter x5 -> x1, waiting for transfers between devices: 645 us -> 0.02 us  [on_device(): lax.psum_scatter(head_rows_grad.astype(low), 'dp', scatter_dimension=1, t...]
    ppermute x0 -> x52, waiting for transfers between devices: none -> 516 us  [send(): return lax.ppermute(value, ('dp', 'seq'), pairs)]
    all_gather x6 -> x4, waiting for transfers between devices: 556 us -> 49.3 us  [the longest x1 48.9 us: on_device(): chosen = lax.all_gather(final, 'seq', axis=0, tiled=True)]
    psum x3 -> x1, waiting for transfers between devices: 336 us -> 0.01 us  [on_device(): lax.psum((jnp.sum(attn_square, 0), jnp.sum(mlp_square, 0), scalars), ('dp...]
    all_gather x4 -> x1, blocking collectives: 175 us -> 31 us  [on_device(): stats = lax.all_gather(jnp.stack([part_high, part_sum, part_target]), 'seq')]
    concatenate x2 -> x6, other arithmetic: 119 us -> 26.1 us  [the longest x1 13.2 us: on_device(): jnp.concatenate([emb_low, pl.send(emb_low, dc=1), jnp.zeros((8, emb_m), l...]
    all_to_all x1, waiting for transfers between devices: 0.01 us -> 60.6 us  [on_device(): lax.all_to_all(looked, 'seq', split_axis=0, concat_axis=1, tiled=True)]
  transfers between devices with their start and end apart: 17 -> 60, of which waited for: 14 -> 41; matrix products, arithmetic and copies ran while one was open for 11% -> 28% of each run, Pallas kernels for 0% -> 0%
where the time goes in v1:
time: 1460 us; the launch traced here: 1450 us
  waiting for transfers between devices  627 us (43%)
  other arithmetic  223 us (15%)
  blocking collectives  195 us (13%)
  local copies, waits for them, and re-layouts  171 us (12%)
  matrix products  151 us (10%)
  starting transfers between devices  53 us (4%)
  between operations  25.9 us (2%)
    ppermute x52, waiting for transfers between devices, send(): return lax.ppermute(value, ('dp', 'seq'), pairs)  516 us
    all_to_all x1, waiting for transfers between devices, on_device(): lax.all_to_all(looked, 'seq', split_axis=0, concat_axis=1, tiled=True)  60.6 us
    all_gather x1, waiting for transfers between devices, on_device(): chosen = lax.all_gather(final, 'seq', axis=0, tiled=True)  48.9 us
    all_to_all x1, blocking collectives, seq_sum(): lax.all_to_all(value.astype(low), 'seq', split_axis=0, concat_axis=0, til...  44.8 us
    unnamed x257, local copies, waits for them, and re-layouts  43.4 us
    ppermute x52, starting transfers between devices, send(): return lax.ppermute(value, ('dp', 'seq'), pairs)  41.8 us
    dot_general x9, matrix products, matmul_tn(): lax.dot_general(left, right, (((0,), (0,)), ((), ())), preferred_element_...  40.1 us
    scatter-add x1, other arithmetic, on_device(): jnp.zeros((2 * emb_n + 8, emb_m), full).at[places_in.reshape(-1)]  37.3 us
  transfers between devices with their start and end apart: 60, of which 41 were waited for; matrix products, arithmetic and copies ran while one was open for 28% of the time, Pallas kernels for 0%

profile of v1, /device:TPU:0, one launch (start us, length us, event | category | flops | bytes accessed | tf_op | source)
XLA Modules:
  0.0 1446.5 jit_solution(14645240658700228437)
XLA Ops:
  30.3 13.2 maximum_maximum_fusion
  69.0 25.1 %collective-permute-done.2 = bf16[2560,256]{1,0:T(8,128)(2,1)S(1)} collective-permute-done((bf16[2560,256]{1,0:T(8,128)(2,1)}, bf16[2560,256]{1,0:T(8,128)(2,1)S(1)}, u32[]{:S(2)}, u32[]{:S(2)}) %collective-permute-start.2) | collective-permute-done | bytes 1310752 | tf_op jit(solution)/shard_map/ppermute | solution.py:112
  103.0 60.6 %all-to-all-done = bf16[8,320,256]{2,1,0:T(8,128)(2,1)S(1)} async-done(((bf16[8,320,256]{2,1,0:T(8,128)(2,1)}), bf16[8,320,256]{2,1,0:T(8,128)(2,1)S(1)}, u32[]{:S(2)}, u32[]{:S(2)}) %all-to-all-start) | async-done | bytes 1310752 | tf_op jit(solution)/shard_map/all_to_all | solution.py:276
  239.1 52.4 %collective-permute-done.14 = bf16[4,2,64,2112]{3,2,1,0:T(8,128)(2,1)} collective-permute-done((bf16[4,2,64,2112]{3,2,1,0:T(8,128)(2,1)S(1)}, bf16[4,2,64,2112]{3,2,1,0:T(8,128)(2,1)}, u32[]{:S(2)}, u32[]{:S(2)}) %collective-permute-start.14) | collective-permute-done | bytes 2162720 | tf_op jit(solution)/shard_map/ppermute | solution.py:112
  296.2 47.1 %collective-permute-done.15 = bf16[4,2,64,2112]{3,2,1,0:T(8,128)(2,1)} collective-permute-done((bf16[4,2,64,2112]{3,2,1,0:T(8,128)(2,1)}, bf16[4,2,64,2112]{3,2,1,0:T(8,128)(2,1)}, u32[]{:S(2)}, u32[]{:S(2)}) %collective-permute-start.15) | collective-permute-done | bytes 2162720 | tf_op jit(solution)/shard_map/ppermute | solution.py:112
  422.4 48.9 %all-gather.11.cloned.1.call-done = bf16[512,2048]{1,0:T(8,128)(2,1)} async-done(((bf16[64,2048]{1,0:T(8,128)(2,1)}), bf16[512,2048]{1,0:T(8,128)(2,1)}) %all-gather.11.cloned.1.call-update) | async-done | bytes 2097168 | tf_op jit(solution)/shard_map/all_gather | solution.py:312
  471.3 12.7 fusion.165
  486.6 31.0 %all-gather.1 = f32[8,3,512]{2,1,0:T(4,128)S(1)} all-gather(f32[1,3,512]{2,1,0:T(4,128)S(1)} %maximum_bitcast_fusion.1), channel_id=2, replica_groups=mesh['dp'=4,'seq'=8] {'seq'}, dimensions={0}, use_global_device_ids=true | all-gather | bytes 55296 | tf_op jit(solution)/shard_map/all_gather | solution.py:322
  518.9 15.9 %convolution_convert_fusion.4 = bf16[512,2048]{1,0:T(8,128)(2,1)S(1)} fusion(bf16[4000,2048]{1,0:T(8,128)(2,1)} %all-gather.13.cloned.1.call-done, f32[512,4000]{0,1:T(8,128)S(1)} %get-tuple-element.275, f32[512]{0:T(512)S(1)} %get-tuple-element.177, f32[512]{0:T(512)S(1)} %get-tuple-element.178, f32[512]{0:T(512)S(1)} %get-tuple-element.250, ...), kind=kOutput, calls=%fused_computation.93 | convolution fusion | flops 8403992576 | bytes 26697344 | tf_op jit(solution)/shard_map/dot_general | solution.py:71
  534.8 44.8 %all_to_all.44 = bf16[8,64,2048]{2,1,0:T(8,128)(2,1)S(1)} all-to-all(bf16[8,64,2048]{2,1,0:T(8,128)(2,1)S(1)} %bitcast.508), channel_id=1, replica_groups=mesh['dp'=4,'seq'=8] {'seq'}, dimensions={0} | all-to-all | bytes 4194304 | tf_op jit(solution)/shard_map/all_to_all | solution.py:177
  618.0 52.1 %collective-permute-done.40 = bf16[4,2,64,2112]{3,2,1,0:T(8,128)(2,1)} collective-permute-done((bf16[4,2,64,2112]{3,2,1,0:T(8,128)(2,1)}, bf16[4,2,64,2112]{3,2,1,0:T(8,128)(2,1)}, u32[]{:S(2)}, u32[]{:S(2)}) %collective-permute-start.40) | collective-permute-done | bytes 2162720 | tf_op jit(solution)/shard_map/ppermute | solution.py:112
  674.1 52.1 %collective-permute-done.41 = bf16[4,2,64,2112]{3,2,1,0:T(8,128)(2,1)} collective-permute-done((bf16[4,2,64,2112]{3,2,1,0:T(8,128)(2,1)}, bf16[4,2,64,2112]{3,2,1,0:T(8,128)(2,1)}, u32[]{:S(2)}, u32[]{:S(2)}) %collective-permute-start.41) | collective-permute-done | bytes 2162720 | tf_op jit(solution)/shard_map/ppermute | solution.py:112
  743.8 37.5 %collective-permute-done.42 = bf16[4,2,64,2112]{3,2,1,0:T(8,128)(2,1)} collective-permute-done((bf16[4,2,64,2112]{3,2,1,0:T(8,128)(2,1)}, bf16[4,2,64,2112]{3,2,1,0:T(8,128)(2,1)}, u32[]{:S(2)}, u32[]{:S(2)}) %collective-permute-start.42) | collective-permute-done | bytes 2162720 | tf_op jit(solution)/shard_map/ppermute | solution.py:112
  795.2 11.8 collective-permute-done.45
  831.4 16.0 %convolution_convert_fusion = bf16[4000,2048]{1,0:T(8,128)(2,1)} fusion(bf16[512,2048]{1,0:T(8,128)(2,1)} %all-gather.11.cloned.1.call-done, f32[512,4000]{0,1:T(8,128)} %copy-done.28, f32[512]{0:T(512)S(1)} %get-tuple-element.177, f32[512]{0:T(512)S(1)} %get-tuple-element.178, f32[512]{0:T(512)S(1)} %get-tuple-element.250, s32[512]{0:T(512)S(1)} %bitcast.552, ...), kind=kOutput, calls=%fused_computation.17 | convolution fusion | flops 8411136000 | bytes 26697344 | tf_op jit(solution)/shard_map/dot_general | solution.py:81
  871.6 12.1 fusion.68
  965.6 37.1 %all_to_all.45 = bf16[320,8,256]{2,0,1:T(8,128)(2,1)S(1)} all-to-all(bf16[320,8,256]{2,0,1:T(8,128)(2,1)S(1)} %pad_maximum_fusion.5), channel_id=1, replica_groups=mesh['dp'=4,'seq'=8] {'seq'}, dimensions={1} | all-to-all | bytes 2621440 | tf_op jit(solution)/shard_map/all_to_all | solution.py:417
  1004.3 55.8 %collective-permute-done.50 = bf16[2560,256]{1,0:T(8,128)(2,1)S(1)} collective-permute-done((bf16[2560,256]{1,0:T(8,128)(2,1)S(1)}, bf16[2560,256]{1,0:T(8,128)(2,1)S(1)}, u32[]{:S(2)}, u32[]{:S(2)}) %collective-permute-start.50) | collective-permute-done | bytes 1310752 | tf_op jit(solution)/shard_map/ppermute | solution.py:112
  1061.2 37.3 %scatter_custom_fusion = f32[16008,256]{1,0:T(8,128)} fusion(s32[5120]{0:T(1024)} %bitcast.546, f32[]{:T(128)} %constant.370.clone.1, bf16[2560,256]{1,0:T(8,128)(2,1)} %copy-done.54, bf16[]{:T(256)} %constant.435, bf16[2560,256]{1,0:T(8,128)(2,1)S(1)} %bitcast.490), kind=kCustom, calls=%fused_computation.37 | custom fusion | flops 6553600 | bytes 19014656 | tf_op jit(solution)/shard_map/scatter-add | solution.py:420
  1195.4 29.2 %collective-permute-done.35 = bf16[2,4,64,2432]{3,2,1,0:T(8,128)(2,1)S(1)} collective-permute-done((bf16[2,4,64,2432]{3,2,1,0:T(8,128)(2,1)}, bf16[2,4,64,2432]{3,2,1,0:T(8,128)(2,1)S(1)}, u32[]{:S(2)}, u32[]{:S(2)}) %collective-permute-start.35) | collective-permute-done | bytes 2490400 | tf_op jit(solution)/shard_map/ppermute | solution.py:112
  1227.1 22.1 %collective-permute-done.31 = bf16[4,64,2304]{2,1,0:T(8,128)(2,1)S(1)} collective-permute-done((bf16[4,64,2304]{2,1,0:T(8,128)(2,1)S(1)}, bf16[4,64,2304]{2,1,0:T(8,128)(2,1)S(1)}, u32[]{:S(2)}, u32[]{:S(2)}) %collective-permute-start.31) | collective-permute-done | bytes 1179680 | tf_op jit(solution)/shard_map/ppermute | solution.py:112
  1309.9 34.3 %all-reduce.4 = (f32[8000]{0:T(1024)S(1)}, f32[512]{0:T(512)S(1)}) all-reduce(f32[8000]{0:T(1024)S(1)} %copy-done.69, f32[512]{0:T(512)S(1)} %get-tuple-element.128), channel_id=1, replica_groups=mesh['dp'=4,'seq'=8] {'seq'}, use_global_device_ids=true, to_apply=%region_38.40 | all-reduce | flops 8512 | bytes 68096 | tf_op jit(solution)/shard_map/psum | solution.py:451
  1362.8 37.1 %all-reduce.3 = (f32[12]{0:T(128)S(1)}, f32[4608]{0:T(1024)S(1)}) all-reduce(f32[12]{0:T(128)S(1)} %stack.155, f32[4608]{0:T(1024)S(1)} %copy-done.76), channel_id=1, replica_groups=mesh['dp'=4,'seq'=8] {'dp','seq'}, use_global_device_ids=true, to_apply=%region_36.38 | all-reduce | flops 4620 | bytes 36960 | tf_op jit(solution)/shard_map/psum | solution.py:448
  1416.5 12.0 multiply_subtract_fusion.1
  (623 shorter events, 622.3 us)
Async XLA Ops:
  7.2 160.5 %all-gather.7.cloned.1.call-start = ((), (), s32[]{:S(2)}) async-start(), calls=%async_computation.5 | async-start | bytes 20004864 | tf_op jit(solution)/shard_map/all_gather | solution.py:249
  56.3 37.8 %collective-permute-start.2 = (bf16[2560,256]{1,0:T(8,128)(2,1)}, bf16[2560,256]{1,0:T(8,128)(2,1)S(1)}, u32[]{:S(2)}, u32[]{:S(2)}) collective-permute-start(bf16[2560,256]{1,0:T(8,128)(2,1)} %broadcast_select_fusion), channel_id=1, source_target_pairs={{0,16},{1,17},{2,18},{3,19},{4,20},{5,21},{6,22},{7,23},{8,24},{9,... | collective-permute-start | bytes 3932168 | tf_op jit(solution)/shard_map/ppermute | solution.py:112
  96.3 67.3 %all-to-all-start = ((bf16[8,320,256]{2,1,0:T(8,128)(2,1)}), bf16[8,320,256]{2,1,0:T(8,128)(2,1)S(1)}, u32[]{:S(2)}, u32[]{:S(2)}) async-start(bf16[8,320,256]{2,1,0:T(8,128)(2,1)} %bitcast.3), calls=%async_computation | async-start | bytes 2621440 | tf_op jit(solution)/shard_map/all_to_all | solution.py:276
  102.2 249.5 %all-gather.9.cloned.1.call-start = ((), (), s32[]{:S(2)}) async-start(), calls=%async_computation.6 | async-start | bytes 2359296 | tf_op jit(solution)/shard_map/all_gather | solution.py:290
  174.8 247.6 %all-gather.13.cloned.1.call-start = ((), (), s32[]{:S(2)}) async-start(), calls=%async_computation.8 | async-start | bytes 20480000 | tf_op jit(solution)/shard_map/all_gather | solution.py:251
  185.1 286.2 %all-gather.11.cloned.1.call-start = ((), (), s32[]{:S(2)}) async-start(), calls=%async_computation.7 | async-start | bytes 2359296 | tf_op jit(solution)/shard_map/all_gather | solution.py:312
  239.1 52.4 %collective-permute-start.14 = (bf16[4,2,64,2112]{3,2,1,0:T(8,128)(2,1)S(1)}, bf16[4,2,64,2112]{3,2,1,0:T(8,128)(2,1)}, u32[]{:S(2)}, u32[]{:S(2)}) collective-permute-start(bf16[4,2,64,2112]{3,2,1,0:T(8,128)(2,1)S(1)} %bitcast.480), channel_id=1, source_target_pairs={{0,2},{1,3},{2,4},{3,5},{4,6},{5,7},{6,0},{7,1},{8,10},{9,11},{10,... | collective-permute-start | bytes 6488072 | tf_op jit(solution)/shard_map/ppermute | solution.py:112
  291.5 51.7 %collective-permute-start.15 = (bf16[4,2,64,2112]{3,2,1,0:T(8,128)(2,1)}, bf16[4,2,64,2112]{3,2,1,0:T(8,128)(2,1)}, u32[]{:S(2)}, u32[]{:S(2)}) collective-permute-start(bf16[4,2,64,2112]{3,2,1,0:T(8,128)(2,1)} %collective-permute-done.14), channel_id=1, source_target_pairs={{0,2},{1,3},{2,4},{3,5},{4,6},{5,7},{6,0},{7,1},{8,10},{9,11},{10,... | collective-permute-start | bytes 6488072 | tf_op jit(solution)/shard_map/ppermute | solution.py:112
  343.2 51.0 %collective-permute-start.16 = (bf16[4,2,64,2112]{3,2,1,0:T(8,128)(2,1)}, bf16[4,2,64,2112]{3,2,1,0:T(8,128)(2,1)}, u32[]{:S(2)}, u32[]{:S(2)}) collective-permute-start(bf16[4,2,64,2112]{3,2,1,0:T(8,128)(2,1)} %collective-permute-done.15), channel_id=1, source_target_pairs={{0,2},{1,3},{2,4},{3,5},{4,6},{5,7},{6,0},{7,1},{8,10},{9,11},{10,... | collective-permute-start | bytes 6488072 | tf_op jit(solution)/shard_map/ppermute | solution.py:112
  421.7 747.0 %all-reduce.8.cloned.1.call-start = ((), (), s32[]{:S(2)}) async-start(), calls=%async_computation.10 | async-start | bytes 139264 | tf_op jit(solution)/shard_map/psum | solution.py:448
  617.3 52.9 %collective-permute-start.40 = (bf16[4,2,64,2112]{3,2,1,0:T(8,128)(2,1)}, bf16[4,2,64,2112]{3,2,1,0:T(8,128)(2,1)}, u32[]{:S(2)}, u32[]{:S(2)}) collective-permute-start(bf16[4,2,64,2112]{3,2,1,0:T(8,128)(2,1)} %fusion.80), channel_id=1, source_target_pairs={{0,2},{1,3},{2,4},{3,5},{4,6},{5,7},{6,0},{7,1},{8,10},{9,11},{10,... | collective-permute-start | bytes 6488072 | tf_op jit(solution)/shard_map/ppermute | solution.py:112
  674.1 52.1 %collective-permute-start.41 = (bf16[4,2,64,2112]{3,2,1,0:T(8,128)(2,1)}, bf16[4,2,64,2112]{3,2,1,0:T(8,128)(2,1)}, u32[]{:S(2)}, u32[]{:S(2)}) collective-permute-start(bf16[4,2,64,2112]{3,2,1,0:T(8,128)(2,1)} %fusion.45), channel_id=1, source_target_pairs={{0,2},{1,3},{2,4},{3,5},{4,6},{5,7},{6,0},{7,1},{8,10},{9,11},{10,... | collective-permute-start | bytes 6488072 | tf_op jit(solution)/shard_map/ppermute | solution.py:112
  730.1 51.2 %collective-permute-start.42 = (bf16[4,2,64,2112]{3,2,1,0:T(8,128)(2,1)}, bf16[4,2,64,2112]{3,2,1,0:T(8,128)(2,1)}, u32[]{:S(2)}, u32[]{:S(2)}) collective-permute-start(bf16[4,2,64,2112]{3,2,1,0:T(8,128)(2,1)} %fusion.44), channel_id=1, source_target_pairs={{0,2},{1,3},{2,4},{3,5},{4,6},{5,7},{6,0},{7,1},{8,10},{9,11},{10,... | collective-permute-start | bytes 6488072 | tf_op jit(solution)/shard_map/ppermute | solution.py:112
  786.8 60.7 %collective-permute-start.28 = (bf16[64,2048]{1,0:T(8,128)(2,1)}, bf16[64,2048]{1,0:T(8,128)(2,1)}, u32[]{:S(2)}, u32[]{:S(2)}) collective-permute-start(bf16[64,2048]{1,0:T(8,128)(2,1)} %get-tuple-element.224), channel_id=1, source_target_pairs={{0,17},{1,16},{2,19},{3,18},{4,21},{5,20},{6,23},{7,22},{8,25},{9,... | collective-permute-start | bytes 786440 | tf_op jit(solution)/shard_map/ppermute | solution.py:112
  787.9 59.7 %collective-permute-start.27 = (bf16[64,2048]{1,0:T(8,128)(2,1)}, bf16[64,2048]{1,0:T(8,128)(2,1)}, u32[]{:S(2)}, u32[]{:S(2)}) collective-permute-start(bf16[64,2048]{1,0:T(8,128)(2,1)} %get-tuple-element.225), channel_id=1, source_target_pairs={{0,16},{1,17},{2,18},{3,19},{4,20},{5,21},{6,22},{7,23},{8,24},{9,... | collective-permute-start | bytes 786440 | tf_op jit(solution)/shard_map/ppermute | solution.py:112
  788.5 59.0 %collective-permute-start.26 = (bf16[64,2048]{1,0:T(8,128)(2,1)}, bf16[64,2048]{1,0:T(8,128)(2,1)}, u32[]{:S(2)}, u32[]{:S(2)}) collective-permute-start(bf16[64,2048]{1,0:T(8,128)(2,1)} %get-tuple-element.223), channel_id=1, source_target_pairs={{0,1},{1,0},{2,3},{3,2},{4,5},{5,4},{6,7},{7,6},{8,9},{9,8},{10,11... | collective-permute-start | bytes 786440 | tf_op jit(solution)/shard_map/ppermute | solution.py:112
  831.2 470.3 %reduce-scatter.2.cloned.1.call-start = ((), (), s32[]{:S(2)}) async-start(), calls=%async_computation.9 | async-start | bytes 20480000 | tf_op jit(solution)/shard_map/reduce_scatter | solution.py:341
  888.7 53.9 %all-to-all-start.2 = ((bf16[8,256,512]{1,2,0:T(8,128)(2,1)}), bf16[8,256,512]{1,2,0:T(8,128)(2,1)}, u32[]{:S(2)}, u32[]{:S(2)}) async-start(bf16[8,256,512]{1,2,0:T(8,128)(2,1)} %pad_maximum_fusion.3), calls=%async_computation.2 | async-start | bytes 4194304 | tf_op jit(solution)/shard_map/all_to_all | solution.py:177
  964.2 155.8 %collective-permute-start.29 = (bf16[1024,4736]{1,0:T(8,128)(2,1)}, bf16[1024,4736]{1,0:T(8,128)(2,1)}, u32[]{:S(2)}, u32[]{:S(2)}) collective-permute-start(bf16[1024,4736]{1,0:T(8,128)(2,1)} %fusion.11), channel_id=1, source_target_pairs={{0,8},{1,9},{2,10},{3,11},{4,12},{5,13},{6,14},{7,15},{8,0},{9,1},... | collective-permute-start | bytes 29097992 | tf_op jit(solution)/shard_map/ppermute | solution.py:112
  1002.7 57.4 %collective-permute-start.50 = (bf16[2560,256]{1,0:T(8,128)(2,1)S(1)}, bf16[2560,256]{1,0:T(8,128)(2,1)S(1)}, u32[]{:S(2)}, u32[]{:S(2)}) collective-permute-start(bf16[2560,256]{1,0:T(8,128)(2,1)S(1)} %bitcast.489), channel_id=1, source_target_pairs={{0,16},{1,17},{2,18},{3,19},{4,20},{5,21},{6,22},{7,23},{8,24},{9,... | collective-permute-start | bytes 3932168 | tf_op jit(solution)/shard_map/ppermute | solution.py:112
  1106.0 64.4 %collective-permute-start.51 = (f32[8000,256]{1,0:T(8,128)}, f32[8000,256]{1,0:T(8,128)}, u32[]{:S(2)}, u32[]{:S(2)}) collective-permute-start(f32[8000,256]{1,0:T(8,128)} %slice.342), channel_id=1, source_target_pairs={{0,8},{1,9},{2,10},{3,11},{4,12},{5,13},{6,14},{7,15},{8,0},{9,1},... | collective-permute-start | bytes 24576008 | tf_op jit(solution)/shard_map/ppermute | solution.py:112
  1137.6 54.0 %collective-permute-start.30 = (bf16[4,2,64,2304]{3,2,1,0:T(8,128)(2,1)}, bf16[4,2,64,2304]{3,2,1,0:T(8,128)(2,1)}, u32[]{:S(2)}, u32[]{:S(2)}) collective-permute-start(bf16[4,2,64,2304]{3,2,1,0:T(8,128)(2,1)} %dynamic-slice_bitcast_fusion.1), channel_id=1, source_target_pairs={{0,16},{1,17},{2,18},{3,19},{4,20},{5,21},{6,22},{7,23},{8,24},{9,... | collective-permute-start | bytes 7077896 | tf_op jit(solution)/shard_map/ppermute | solution.py:112
  1167.5 57.1 %collective-permute-start.35 = (bf16[2,4,64,2432]{3,2,1,0:T(8,128)(2,1)}, bf16[2,4,64,2432]{3,2,1,0:T(8,128)(2,1)S(1)}, u32[]{:S(2)}, u32[]{:S(2)}) collective-permute-start(bf16[2,4,64,2432]{3,2,1,0:T(8,128)(2,1)} %dynamic-slice_bitcast_fusion), channel_id=1, source_target_pairs={{0,1},{1,0},{2,3},{3,2},{4,5},{5,4},{6,7},{7,6},{8,9},{9,8},{10,11... | collective-permute-start | bytes 7471112 | tf_op jit(solution)/shard_map/ppermute | solution.py:112
  1193.9 55.3 %collective-permute-start.31 = (bf16[4,64,2304]{2,1,0:T(8,128)(2,1)S(1)}, bf16[4,64,2304]{2,1,0:T(8,128)(2,1)S(1)}, u32[]{:S(2)}, u32[]{:S(2)}) collective-permute-start(bf16[4,64,2304]{2,1,0:T(8,128)(2,1)S(1)} %fusion.97), channel_id=1, source_target_pairs={{0,1},{1,0},{2,3},{3,2},{4,5},{5,4},{6,7},{7,6},{8,9},{9,8},{10,11... | collective-permute-start | bytes 3538952 | tf_op jit(solution)/shard_map/ppermute | solution.py:112
  (157 other events, 2846.8 us)
Sparse Core Ops, SparseCore 0:
  12.3 155.3 all-gather.6
  174.9 59.3 all-gather.8
  236.4 101.9 all-gather.12
  421.8 49.4 all-gather.10
  831.3 130.8 all-reduce.7
  964.7 157.2 reduce-scatter.1

commit v2 on v1

v2 whole, which is shorter than its diff:
```python
import functools
import math

import jax
import jax.numpy as jnp
from jax import lax
from jax.experimental import pallas
from jax.experimental.pallas import tpu as pltpu
from jax.sharding import PartitionSpec as P

D = 2048
HEADS = 32
KVH = 4
HD = 64
FF = 5632
VOCAB = 32000
QKV = 2560


eps_norm = 1e-05
eps_square = 1e-30
decay_rate = 0.5
learn_rate = 1.0
zloss_weight = 0.0001
orig_context = 2048.0
yarn_factor = 4.0
highest = lax.Precision.HIGHEST


def yarn_tables(places):
    halves = jnp.arange(HD // 2, dtype=jnp.float32)
    inverse = jnp.power(10000.0, -2.0 * halves / HD)
    ratio = orig_context * inverse / (2.0 * math.pi)
    ramp_part = jnp.clip((ratio - 1.0) / 31.0, 0.0, 1.0)
    frequency = inverse / yarn_factor * (1.0 - ramp_part) + inverse * ramp_part
    angles = places[:, None] * frequency[None, :]
    magnitude = 0.1 * math.log(yarn_factor) + 1.0
    return (jnp.cos(angles) * magnitude, jnp.sin(angles) * magnitude)


def rotate(values, cosine, sine):
    first = values[..., : HD // 2]
    second = values[..., HD // 2 :]
    cosine_row = cosine[:, None, :]
    sine_row = sine[:, None, :]
    return jnp.concatenate(
        [first * cosine_row - second * sine_row, second * cosine_row + first * sine_row], -1
    )


def unrotate(values, cosine, sine):
    first = values[..., : HD // 2]
    second = values[..., HD // 2 :]
    cosine_row = cosine[:, None, :]
    sine_row = sine[:, None, :]
    return jnp.concatenate(
        [first * cosine_row + second * sine_row, second * cosine_row - first * sine_row], -1
    )


def rms_norm(values, gain_row):
    return values * lax.rsqrt(jnp.mean(values * values, -1, keepdims=True) + eps_norm) * gain_row


def norm_back(values, gain_row, upstream):
    factor = lax.rsqrt(jnp.mean(values * values, -1, keepdims=True) + eps_norm)
    normed = values * factor
    gain_grad = jnp.sum(upstream * normed, 0)
    inner = upstream * gain_row
    return (factor * (inner - normed * jnp.mean(inner * normed, -1, keepdims=True)), gain_grad)


def matmul(left, right):
    return jnp.dot(left, right, preferred_element_type=jnp.float32)


def matmul_nt(left, right):
    return lax.dot_general(
        left, right, (((1,), (1,)), ((), ())), preferred_element_type=jnp.float32
    )


def matmul_tn(left, right):
    return lax.dot_general(
        left, right, (((0,), (0,)), ((), ())), preferred_element_type=jnp.float32
    )


def finish(weight, update, weight_square, entries):
    return weight - learn_rate * jnp.maximum(0.001, jnp.sqrt(weight_square / entries)) * update


low = jnp.bfloat16
full = jnp.float32


class Place:
    def __init__(self):
        self.seqs = lax.axis_size("seq")
        self.dps = lax.axis_size("dp")
        self.dp = lax.axis_index("dp")
        self.s = lax.axis_index("seq")
        self.his = self.seqs // 2
        self.y, self.c = self.dp // 2, self.dp % 2
        self.hi, self.lo = self.s // 2, self.s % 2

    def send(self, value, dy=0, dc=0, dlo=0, up=0):
        pairs = []
        for d in range(self.dps):
            for s in range(self.seqs):
                to_d = d ^ (2 * dy + dc)
                to_s = ((s // 2 + up) % self.his) * 2 + ((s % 2) ^ dlo)
                pairs.append((d * self.seqs + s, to_d * self.seqs + to_s))
        return lax.ppermute(value, ("dp", "seq"), pairs)

    def ways(self, names):
        steps = []
        for name in names:
            if name == "hi":
                bit = 1
                while bit < self.his:
                    steps.append(lambda value, bit=bit: self.swap_hi(value, bit))
                    bit *= 2
            else:
                steps.append(lambda value, name=name: self.send(value, **{name: 1}))
        return steps

    def swap_hi(self, value, bit):
        pairs = []
        for d in range(self.dps):
            for s in range(self.seqs):
                pairs.append((d * self.seqs + s, d * self.seqs + (s ^ (2 * bit))))
        return lax.ppermute(value, ("dp", "seq"), pairs)


def after(value, *events):
    return lax.optimization_barrier((value, *events))[0] if events else value


def pick(array, index, axis):
    return lax.dynamic_index_in_dim(array, index, axis, keepdims=False)


def put(array, block, index, axis):
    return lax.dynamic_update_slice_in_dim(array, jnp.expand_dims(block, axis), index, axis)


def line_parts(pl, blocks):
    n = pl.his
    got = []
    for dc in range(2):
        for k in range(n):
            block = pick(blocks, (pl.c ^ dc) * n + (pl.hi + k) % n, 0)
            got.append(pl.send(block, dc=dc, up=k) if dc or k else block)
    return got


def line_place(pl, got):
    n = pl.his
    out = jnp.zeros((2 * n, *got[0].shape), got[0].dtype)
    for at, block in enumerate(got):
        origin = (pl.c ^ (at // n)) * n + (pl.hi + n - at % n) % n
        out = put(out, block, origin, 0)
    return out


def line_gather(pl, rows, work=()):
    first = jnp.stack([rows] + [after(pl.send(rows, up=k), *work) for k in range(1, pl.his)])
    both = jnp.stack([first, pl.send(first, dc=1)])
    return both.reshape(2 * pl.his * rows.shape[0], rows.shape[1])


def hi_sum_start(pl, part):
    parts = [pick(part, pl.hi, 0)]
    for k in range(1, pl.his):
        block = pick(part, (pl.hi + k) % pl.his, 0).astype(low)
        parts.append(pl.send(block, up=k))
    return parts


def hi_sum_end(parts, *work):
    parts = after(parts, *work)
    return sum((part.astype(full) for part in parts[1:]), parts[0].astype(full))


def cross_start(pl, term):
    a, b = term[:, 0], term[:, 1]
    got_a = pl.send(pick(a, 1 - pl.y, 0), dy=1)
    got_b = pl.send(pick(b, 1 - pl.lo, 2), dlo=1)
    return a, b, got_a, got_b


def cross_next(pl, state, *work):
    a, b, got_a, got_b = state
    got_a, got_b = after((got_a, got_b), *work)
    a = pick(a, pl.y, 0).astype(full) + got_a.astype(full)
    b = pick(b, pl.lo, 2).astype(full) + got_b.astype(full)
    send_a = pick(a, 1 - pl.lo, 1).astype(low)
    send_b = pick(b, 1 - pl.y, 0).astype(low)
    return pick(a, pl.lo, 1), pick(b, pl.y, 0), pl.send(send_a, dlo=1), pl.send(send_b, dy=1)


def cross_end(pl, state, *work):
    a, b, got_a, got_b = state
    got_a, got_b = after((got_a, got_b), *work)
    a = (a + got_a.astype(full)).astype(low)
    b = (b + got_b.astype(full)).astype(low)
    return jnp.stack([a, b]).reshape(2 * pl.his, *a.shape[1:])


def split_kernel(line, part, in_ref, out_ref):
    for j in range(3):
        for t in range(line):
            at = (j * line + t) * part
            out_ref[t, :, j * part : (j + 1) * part] = in_ref[:, at : at + part].astype(low)


def split_columns(weight, line):
    rows, columns = weight.shape
    part = columns // (3 * line)
    return pallas.pallas_call(
        lambda *refs: split_kernel(line, part, *refs),
        out_shape=jax.ShapeDtypeStruct((line, rows, 3 * part), low),
        in_specs=[pallas.BlockSpec(memory_space=pltpu.VMEM)],
        out_specs=pallas.BlockSpec(memory_space=pltpu.VMEM),
        compiler_params=pltpu.CompilerParams(vmem_limit_bytes=40 * 2**20),
        name="split_columns",
    )(weight)


def join_kernel(line, part, in_ref, out_ref, rows_ref, columns_ref):
    total = jnp.zeros(rows_ref.shape, full)
    for j in range(3):
        for t in range(line):
            at = (j * line + t) * part
            block = in_ref[t, :, j * part : (j + 1) * part].astype(full)
            out_ref[:, at : at + part] = block
            square = block * block + eps_square
            columns_ref[:, at : at + part] = jnp.sum(square, 0, keepdims=True)
            total = total + jnp.sum(square, 1, keepdims=True)
    rows_ref[...] = total


def join_columns(blocks):
    line, rows, wide = blocks.shape
    part = wide // 3
    grad, row_sum, column_sum = pallas.pallas_call(
        lambda *refs: join_kernel(line, part, *refs),
        out_shape=(
            jax.ShapeDtypeStruct((rows, line * wide), full),
            jax.ShapeDtypeStruct((rows, 1), full),
            jax.ShapeDtypeStruct((1, line * wide), full),
        ),
        in_specs=[pallas.BlockSpec(memory_space=pltpu.VMEM)],
        out_specs=(pallas.BlockSpec(memory_space=pltpu.VMEM),) * 3,
        compiler_params=pltpu.CompilerParams(vmem_limit_bytes=40 * 2**20),
        name="join_columns",
    )(blocks)
    return grad, row_sum[:, 0], column_sum[0]


def halve(pl, part, mine, axis, **way):
    got = pl.send(pick(part, 1 - mine, axis).astype(low), **way)
    return pick(part, mine, axis).astype(full) + got.astype(full)


def hi_sum(pl, part, *work):
    total = pick(part, pl.hi, 0).astype(full)
    for k in range(1, pl.his):
        block = pick(part, (pl.hi + k) % pl.his, 0).astype(low)
        total = total + after(pl.send(block, up=k), *work).astype(full)
    return total


MESH = pallas.DeviceIdType.MESH
ROWS = 16
SMALL = pallas.CostEstimate(flops=1024, bytes_accessed=1024, transcendentals=0)


class Core:
    def __init__(self, his):
        dp, s = lax.axis_index("dp"), lax.axis_index("seq")
        self.his = his
        self.hi, self.lo, self.c = s // 2, s % 2, dp % 2
        self.side = {"c": self.c, "lo": self.lo}
        self.ids = {
            "c": (dp + 1 - 2 * self.c, s),
            "lo": (dp, s + 1 - 2 * self.lo),
            "up": (dp, lax.rem(self.hi + 1, his) * 2 + self.lo),
            "down": (dp, lax.rem(self.hi + his - 1, his) * 2 + self.lo),
        }

    def meet(self, *names):
        barrier = pltpu.get_barrier_semaphore()
        for name in names:
            pallas.semaphore_signal(
                barrier, inc=1, device_id=self.ids[name], device_id_type=MESH
            )
        pallas.semaphore_wait(barrier, len(names))

    def copy(self, source, target, sems, at, name):
        return pltpu.make_async_remote_copy(
            src_ref=source,
            dst_ref=target,
            send_sem=sems[0].at[at],
            recv_sem=sems[1].at[at],
            device_id=self.ids[name],
            device_id_type=MESH,
        )


def by_rows(n, step):
    def one(i, carry):
        step(pallas.ds(pallas.multiple_of(i * ROWS, ROWS), ROWS))
        return carry

    lax.fori_loop(0, n // ROWS, one, 0)


def kernel_scatter(core, name, part, total, held, side_sems, up_sems):
    his, side = core.his, core.side[name]
    side_out, side_in, up_out, up_in = held
    n = part.shape[2]
    over = []
    for j in range(his):
        h = lax.rem(core.hi + 2 * his - 1 - j, his)

        def cast(at, j=j, h=h):
            side_out[j, at, :] = part[h, 1 - side, at, :].astype(low)

        by_rows(n, cast)
        over.append(core.copy(side_out.at[j], side_in.at[j], side_sems, j, name))
        over[j].start()
    climb = []
    for j in range(his):
        h = lax.rem(core.hi + 2 * his - 1 - j, his)
        over[j].wait_recv()
        if j:
            climb[j - 1].wait_recv()

        def add(at, j=j, h=h):
            acc = part[h, side, at, :].astype(full) + side_in[j, at, :].astype(full)
            if j:
                acc = acc + up_in[j - 1, at, :].astype(full)
            if j < his - 1:
                up_out[j, at, :] = acc.astype(low)
            else:
                total[at, :] = acc

        by_rows(n, add)
        if j < his - 1:
            climb.append(core.copy(up_out.at[j], up_in.at[j], up_sems, j, "up"))
            climb[j].start()
    return over + climb


def kernel_gather(core, name, own, out, local_sem, side_sems, up_sems):
    his, side = core.his, core.side[name]
    here = pltpu.make_async_copy(own, out.at[core.hi, side], local_sem)
    here.start()
    over, climb = [], []
    for j in range(his):
        h = lax.rem(core.hi + his - j, his)
        block = out.at[h, side]
        source = own if j == 0 else block
        if j:
            climb[j - 1].wait_recv()
        if j < his - 1:
            climb.append(core.copy(source, block, up_sems, j, "up"))
            climb[j].start()
        over.append(core.copy(source, block, side_sems, j, name))
        over[j].start()
    for copy in over:
        copy.wait_recv()
    here.wait()
    return over + climb


def sent(copies):
    for copy in copies:
        copy.wait_send()


def norm_rows(values, gain):
    return values * lax.rsqrt(jnp.mean(values * values, -1, keepdims=True) + eps_norm) * gain


def norm_rows_back(values, gain, upstream):
    factor = lax.rsqrt(jnp.mean(values * values, -1, keepdims=True) + eps_norm)
    normed = values * factor
    inner = upstream * gain
    back = factor * (inner - normed * jnp.mean(inner * normed, -1, keepdims=True))
    return back, jnp.sum(upstream * normed, 0, keepdims=True)


def norm_gather_body(his, values, gain, out, own, *sems):
    core = Core(his)
    by_rows(
        values.shape[0],
        lambda at: own.__setitem__(
            (at, slice(None)), norm_rows(values[at, :], gain[...]).astype(low)
        ),
    )
    core.meet("c", "up", "down")
    sent(kernel_gather(core, "c", own, out, sems[0], sems[1:3], sems[3:5]))


def turn_keys(source, cosine, sine, target):
    width = KVH * HD
    for at in range(0, width, 2 * HD):
        pair = turned(source[:, at : at + 2 * HD], cosine, sine)
        target[:, at : at + 2 * HD] = pair.astype(low)
    target[:, width:] = source[:, width:].astype(low)


def keys_body(his, projected, cosine, sine, out, own, *sems):
    core = Core(his)
    turn_keys(projected, cosine[...], sine[...], own)
    core.meet("lo", "up", "down")
    sent(kernel_gather(core, "lo", own, out, sems[0], sems[1:3], sems[3:5]))


def keys_back_body(his, part, cosine, sine, out, total, *rest):
    held, sems = rest[:4], rest[4:]
    core = Core(his)
    core.meet("lo", "up", "down")
    copies = kernel_scatter(core, "lo", part, total, held, sems[0:2], sems[2:4])
    turn_keys(total, cosine[...], -sine[...], out)
    sent(copies)


def ending_body(his, part, middle, gain, ending, chosen, own, *rest):
    held, sems = rest[:4], rest[4:]
    core = Core(his)
    core.meet("c", "lo", "up", "down")
    copies = kernel_scatter(core, "c", part, ending, held, sems[0:2], sems[2:4])

    def finish_rows(at):
        values = ending[at, :] + middle[at, :]
        ending[at, :] = values
        own[at, :] = norm_rows(values, gain[...]).astype(low)

    by_rows(middle.shape[0], finish_rows)
    copies += kernel_gather(core, "lo", own, chosen, sems[4], sems[5:7], sems[7:9])
    sent(copies)


def ending_back_body(his, part, ending, gain, grad, gain_grad, branch, own, *rest):
    held, sems = rest[:4], rest[4:]
    core = Core(his)
    core.meet("c", "lo", "up", "down")
    copies = kernel_scatter(core, "lo", part, grad, held, sems[0:2], sems[2:4])
    gain_grad[...] = jnp.zeros(gain_grad.shape, full)

    def back_rows(at):
        back, gained = norm_rows_back(ending[at, :], gain[...], grad[at, :])
        grad[at, :] = back
        own[at, :] = back.astype(low)
        gain_grad[...] += gained

    by_rows(ending.shape[0], back_rows)
    copies += kernel_gather(core, "c", own, branch, sems[4], sems[5:7], sems[7:9])
    sent(copies)


def middle_back_body(his, part, middle, gain, ending_grad, grad, grad_low, gain_grad, *rest):
    held, sems = rest[:4], rest[4:]
    core = Core(his)
    core.meet("c", "up", "down")
    copies = kernel_scatter(core, "c", part, grad, held, sems[0:2], sems[2:4])
    gain_grad[...] = jnp.zeros(gain_grad.shape, full)

    def back_rows(at):
        back, gained = norm_rows_back(middle[at, :], gain[...], grad[at, :])
        back = back + ending_grad[at, :]
        grad[at, :] = back
        grad_low[at, :] = back.astype(low)
        gain_grad[...] += gained

    by_rows(middle.shape[0], back_rows)
    sent(copies)


def move(body, collective_id, outs, args, his, scatter=None, own=None, own_type=low, gathers=False):
    dma = pltpu.SemaphoreType.DMA
    scratch = []
    if own:
        scratch.append(pltpu.VMEM(own, own_type))
    if scatter:
        scratch += [pltpu.VMEM((count, *scatter), low) for count in (his, his, his - 1, his - 1)]
        scratch += [dma((his,)), dma((his,)), dma((his - 1,)), dma((his - 1,))]
    if gathers:
        scratch += [dma, dma((his,)), dma((his,)), dma((his - 1,)), dma((his - 1,))]
    return pallas.pallas_call(
        body,
        out_shape=tuple(jax.ShapeDtypeStruct(shape, dtype) for shape, dtype, _ in outs),
        in_specs=[pallas.BlockSpec(memory_space=pltpu.VMEM)] * len(args),
        out_specs=tuple(pallas.BlockSpec(memory_space=memory) for _, _, memory in outs),
        scratch_shapes=scratch,
        cost_estimate=SMALL,
        compiler_params=pltpu.CompilerParams(
            collective_id=collective_id,
            has_side_effects=True,
            vmem_limit_bytes=48 * 2**20,
        ),
    )(*args)


HALF = HD // 2
STACK = 4


def turn_tables(cosine, sine):
    return jnp.concatenate([cosine] * 4, 1), jnp.concatenate([-sine, sine] * 2, 1)


def turned(values, cosine, sine):
    lane = lax.broadcasted_iota(jnp.int32, values.shape, 1) % HD
    other = jnp.where(
        lane < HALF, pltpu.roll(values, 2 * HD - HALF, 1), pltpu.roll(values, HALF, 1)
    )
    return values * cosine + other * sine


def heads_loop(loops, step):
    def one(t, carry):
        step(t)
        return carry

    lax.fori_loop(0, loops, one, 0)


def split_kv(kv, k_held, v_held):
    width = KVH * HD
    for g in range(KVH):
        k_held[g] = kv[:, g * HD : (g + 1) * HD]
        v_held[g] = kv[:, width + g * HD : width + (g + 1) * HD]


def allowed_keys(places, keys):
    places = jnp.concatenate([places] * STACK, 0)
    return lax.broadcasted_iota(jnp.int32, (places.shape[0], keys), 1) <= places


def dot_nt(left, right):
    return lax.dot_general(
        left, right, (((1,), (1,)), ((), ())), preferred_element_type=jnp.float32
    )


def attend_body(raw, cosine, sine, places, kv, turned_out, out_low, held_out, logs, k_held, v_held):
    picks, keys = raw.shape[0], kv.shape[0]
    split_kv(kv, k_held, v_held)
    for j in range(D // (2 * HD)):
        pair = turned(raw[:, 2 * HD * j : 2 * HD * (j + 1)], cosine[...], sine[...]).astype(low)
        for i in range(2):
            t, at = divmod(2 * j + i, STACK)
            turned_out[t, at * picks : (at + 1) * picks, :] = pair[:, i * HD : (i + 1) * HD]
    allowed = allowed_keys(places[...], keys)

    def step(t):
        g = t // (HEADS // KVH // STACK)
        scores = dot_nt(turned_out[t], k_held[g]) * HD ** (-0.5)
        scores = jnp.where(allowed, scores, -1e30)
        high = jnp.max(scores, 1, keepdims=True)
        weights = jnp.exp(scores - high)
        total = jnp.sum(weights, 1, keepdims=True)
        result = jnp.dot(weights.astype(low), v_held[g], preferred_element_type=full)
        held_out[t] = result / total
        logs[t] = jnp.broadcast_to(high + jnp.log(total), (STACK * picks, 2 * HD))

    heads_loop(HEADS // STACK, step)
    for j in range(D // (2 * HD)):
        pair = []
        for i in range(2):
            t, at = divmod(2 * j + i, STACK)
            pair.append(held_out[t, at * picks : (at + 1) * picks, :])
        pair = jnp.concatenate(pair, 1)
        out_low[:, 2 * HD * j : 2 * HD * (j + 1)] = pair.astype(low)


def attend_rows(raw, tables, places, kv):
    picks, keys = raw.shape[0], kv.shape[0]
    stacks, rows = HEADS // STACK, STACK * picks
    return pallas.pallas_call(
        attend_body,
        out_shape=(
            jax.ShapeDtypeStruct((stacks, rows, HD), low),
            jax.ShapeDtypeStruct((picks, D), low),
            jax.ShapeDtypeStruct((stacks, rows, HD), full),
            jax.ShapeDtypeStruct((stacks, rows, 2 * HD), full),
        ),
        in_specs=[pallas.BlockSpec(memory_space=pltpu.VMEM)] * 5,
        out_specs=(pallas.BlockSpec(memory_space=pltpu.VMEM),) * 4,
        scratch_shapes=[pltpu.VMEM((KVH, keys, HD), low)] * 2,
        compiler_params=pltpu.CompilerParams(vmem_limit_bytes=56 * 2**20),
        cost_estimate=SMALL,
        name="attend",
    )(raw, *tables, places[:, None], kv)


def attend_back_body(
    grad, cosine, sine, places, kv, queries, held_out, logs, raw, kv_grad, k_held, v_held,
    grad_held, query_held, *sums
):
    picks, keys = grad.shape[0], kv.shape[0]
    scale = HD ** (-0.5)
    split_kv(kv, k_held, v_held)
    for j in range(D // (2 * HD)):
        pair = grad[:, 2 * HD * j : 2 * HD * (j + 1)]
        for i in range(2):
            t, at = divmod(2 * j + i, STACK)
            grad_held[t, at * picks : (at + 1) * picks, :] = pair[:, i * HD : (i + 1) * HD]
    allowed = allowed_keys(places[...], keys)
    total = sums[0] if sums else kv_grad
    total[...] = jnp.zeros(total.shape, full)

    def step(t):
        g = t // (HEADS // KVH // STACK)
        query, up = queries[t], grad_held[t]
        delta = jnp.sum(up.astype(full) * held_out[t], 1, keepdims=True)
        scores = dot_nt(query, k_held[g]) * scale
        weights = jnp.where(allowed, jnp.exp(scores - logs[t][:, :1]), 0.0)
        weight_grad = dot_nt(up, v_held[g])
        score_grad = (weights * (weight_grad - delta)).astype(low)
        query_held[t] = jnp.dot(score_grad, k_held[g], preferred_element_type=full) * scale
        total[g] += matmul_tn(query, score_grad) * scale
        total[KVH + g] += matmul_tn(up, weights.astype(low))

    heads_loop(HEADS // STACK, step)
    for j in range(D // (2 * HD)):
        pair = []
        for i in range(2):
            t, at = divmod(2 * j + i, STACK)
            pair.append(query_held[t, at * picks : (at + 1) * picks, :])
        pair = jnp.concatenate(pair, 1)
        raw[:, 2 * HD * j : 2 * HD * (j + 1)] = turned(pair, cosine[...], -sine[...]).astype(low)
    if sums:
        for g in range(0, 2 * KVH, 2):
            both = jnp.concatenate([total[g], total[g + 1]], 0)
            kv_grad[:, g * HD : (g + 2) * HD] = both.T


def attend_rows_back(grad, tables, places, kv, queries, held_out, logs):
    picks, keys = grad.shape[0], kv.shape[0]
    stacks, rows = HEADS // STACK, STACK * picks
    outside = keys > 4096
    by_head = (2 * KVH, HD, keys)
    raw, kv_grad = pallas.pallas_call(
        attend_back_body,
        out_shape=(
            jax.ShapeDtypeStruct((picks, D), low),
            jax.ShapeDtypeStruct(by_head if outside else (keys, 2 * KVH * HD), full),
        ),
        in_specs=[pallas.BlockSpec(memory_space=pltpu.VMEM)] * 8,
        out_specs=(pallas.BlockSpec(memory_space=pltpu.VMEM),) * 2,
        scratch_shapes=[
            pltpu.VMEM((KVH, keys, HD), low),
            pltpu.VMEM((KVH, keys, HD), low),
            pltpu.VMEM((stacks, rows, HD), low),
            pltpu.VMEM((stacks, rows, HD), full),
        ]
        + ([] if outside else [pltpu.VMEM(by_head, full)]),
        compiler_params=pltpu.CompilerParams(vmem_limit_bytes=58 * 2**20),
        cost_estimate=SMALL,
        name="attend_back",
    )(grad, *tables, places[:, None], kv, queries, held_out, logs)
    return raw, kv_grad.reshape(2 * KVH * HD, keys).T if outside else kv_grad


def sum_body(his, rows, packed, out, bufs, got, send_sems, recv_sems):
    core = Core(his)
    dp, s = lax.axis_index("dp"), lax.axis_index("seq")
    ways = [("lo", 0)]
    bit = 1
    while bit < his:
        up = lax.rem(core.hi // bit, 2)
        core.ids[f"hi{bit}"] = (dp, s + 2 * bit * (1 - 2 * up))
        ways.append((f"hi{bit}", 0))
        bit *= 2
    y = dp // 2
    core.ids["y"] = (dp + 2 * (1 - 2 * y), s)
    ways += [("c", 1), ("y", 1)]
    core.meet(*(name for name, _ in ways))
    bufs[0] = packed[...]
    copies = []
    for j, (name, over_dp) in enumerate(ways):
        first = rows[0] if over_dp else 0
        last = rows[0] + rows[1] + (rows[2] if over_dp else 0)
        copy = core.copy(
            bufs.at[j, first:last], got.at[j, first:last], (send_sems, recv_sems), j, name
        )
        copy.start()
        copies.append(copy)
        copy.wait_recv()
        bufs[j + 1] = bufs[j]
        bufs[j + 1, first:last] = bufs[j, first:last] + got[j, first:last]
    out[...] = bufs[len(ways)]
    sent(copies)


def padded(parts):
    return [
        jnp.pad(part, (0, -part.shape[0] % 1024)).reshape(-1, 128) for part in parts
    ]


def sum_statistics(his, over_seq, over_all, over_dp):
    groups = [padded(parts) for parts in (over_seq, over_all, over_dp)]
    rows = tuple(sum(part.shape[0] for part in group) for group in groups)
    steps = 3 + his.bit_length() - 1
    total = sum(rows)
    dma = pltpu.SemaphoreType.DMA
    out = pallas.pallas_call(
        functools.partial(sum_body, his, rows),
        out_shape=jax.ShapeDtypeStruct((total, 128), full),
        in_specs=[pallas.BlockSpec(memory_space=pltpu.VMEM)],
        out_specs=pallas.BlockSpec(memory_space=pltpu.VMEM),
        scratch_shapes=[
            pltpu.VMEM((steps + 1, total, 128), full),
            pltpu.VMEM((steps, total, 128), full),
            dma((steps,)),
            dma((steps,)),
        ],
        compiler_params=pltpu.CompilerParams(
            collective_id=6, has_side_effects=True, vmem_limit_bytes=32 * 2**20
        ),
        name="sum_statistics",
    )(jnp.concatenate([part for group in groups for part in group], 0))
    results, at = [], 0
    for parts, group in zip((over_seq, over_all, over_dp), groups):
        for part, block in zip(parts, group):
            results.append(out[at : at + block.shape[0]].reshape(-1)[: part.shape[0]])
            at += block.shape[0]
    return results


def on_device(
    tok_ids,
    targets,
    positions,
    answer_mask,
    emb,
    head,
    attn_w,
    mlp_w,
    gains,
    emb_row,
    emb_col,
    head_row,
    head_col,
    attn_row,
    attn_col,
    mlp_row,
    mlp_col,
    gains_moment,
):
    pl = Place()
    seqs, his = pl.seqs, pl.his
    tokens = tok_ids.shape[1] // seqs
    picks = targets.shape[1] // seqs
    group = HEADS // KVH
    kv_width = KVH * HD
    block = D // (pl.dps * seqs)
    emb_n, emb_m = emb.shape
    line = 2 * his
    part = FF // line
    wide = 3 * part

    def swap_rows(rows, **way):
        return pl.send(rows.astype(low), **way)

    mlp_got = line_parts(pl, split_columns(mlp_w, line))
    ids = jnp.concatenate([tok_ids.reshape(seqs, tokens), targets.reshape(seqs, picks)], 1)
    ids = ids.reshape(seqs * (tokens + picks))
    ids_all = jnp.stack(
        [
            jnp.stack([ids, pl.send(ids, dc=1)]),
            jnp.stack([pl.send(ids, dy=1), pl.send(ids, dy=1, dc=1)]),
        ]
    )
    local = ids_all - pl.dp * emb_n
    local = jnp.where((local >= 0) & (local < emb_n), local, emb_n)

    def look(dy, dc, *work):
        at = after(local[dy, dc], *work)
        rows = jnp.take(emb, jnp.minimum(at, emb_n - 1), axis=0, mode="clip")
        return jnp.where((at < emb_n)[:, None], rows, 0.0).astype(low)

    far_other = look(1, 1)
    far_got = pl.send(far_other, dc=1)
    far_own = look(1, 0, far_other)
    near_other = look(0, 1, far_own)
    near_got = pl.send(near_other, dc=1)
    far_sum = far_own + after(far_got, near_other)
    across = pl.send(far_sum, dy=1)

    first_block = jnp.concatenate(
        [attn_w[:, :QKV], jnp.pad(gains.T, ((0, 0), (0, 125)))], 1
    ).astype(low)
    qkv_full = lax.all_gather(first_block, ("dp", "seq"), axis=0, tiled=True)
    gain_float = qkv_full[:, QKV : QKV + 3].astype(full).T
    out_full = lax.all_gather(
        attn_w[:, QKV:].astype(low), ("dp", "seq"), axis=0, tiled=True
    )
    near_own = look(0, 0, far_sum)
    near_sum = near_own + after(near_got, near_own)
    head_low = after(head, near_sum).astype(low)
    emb_square_sum = jnp.sum(after(emb, head_low) ** 2)
    looked = near_sum + after(across, emb_square_sum)
    mlp_line = line_place(pl, after(mlp_got, looked)).reshape(2, his, block, wide)
    mlp_x, mlp_y = pl.send(mlp_line, dlo=1), pl.send(mlp_line, dy=1)
    start = lax.all_to_all(looked, "seq", split_axis=0, concat_axis=1, tiled=True).astype(full)

    token_pos = pl.s * tokens + jnp.arange(tokens, dtype=jnp.int32)
    pick_pos = lax.dynamic_slice_in_dim(positions[0], pl.s * picks, picks)
    token_tables = turn_tables(*yarn_tables(token_pos.astype(full)))
    pick_tables = turn_tables(*yarn_tables(pick_pos.astype(full)))
    start, token_tables, pick_tables, mlp_line = lax.optimization_barrier(
        (start, token_tables, pick_tables, mlp_line)
    )
    head_rows = lax.all_gather(after(head_low, start), "dp", axis=1, tiled=True)
    normed = rms_norm(start, gain_float[0]).astype(low)
    normed_tok, normed_pick = normed[:tokens], normed[tokens:]
    start_pick = start[tokens:]
    projected = matmul(normed_tok, qkv_full[:, D:QKV])
    (kv_all,) = move(
        functools.partial(keys_body, his),
        0,
        [((his, 2, tokens, 2 * kv_width), low, pallas.ANY)],
        [projected, *token_tables],
        his,
        own=(tokens, 2 * kv_width),
        gathers=True,
    )
    kv_all = kv_all.reshape(seqs * tokens, 2 * kv_width)
    raw = matmul(normed_pick, qkv_full[:, :D])
    mlp_x, mlp_y = after((mlp_x, mlp_y), kv_all)
    mlp_far = (pl.send(mlp_x[0], dy=1), pl.send(mlp_y[1], dlo=1))
    pick_line = line_gather(pl, after(normed_pick, kv_all))
    queries, attended_low, attended, log_total = attend_rows(
        after(raw, mlp_x, mlp_y), pick_tables, pick_pos, kv_all
    )

    def shares(rows):
        rows = jnp.transpose(rows.reshape(picks, line, D // line), (1, 0, 2))
        return jnp.concatenate(line_parts(pl, rows), 0)

    attended_share = shares(attended_low)
    middle = start_pick + matmul_nt(attended_low, out_full)
    mlp_full = jnp.zeros((2, 2, his, 2, block, wide), low)
    for held, at_y, at_lo in (
        (after(mlp_line, middle), pl.y, pl.lo),
        (mlp_x, pl.y, 1 - pl.lo),
        (mlp_y, 1 - pl.y, pl.lo),
    ):
        mlp_full = lax.dynamic_update_slice(
            mlp_full, held[None, :, :, None], (at_y, 0, 0, at_lo, 0, 0)
        )
    (normed_two,) = move(
        functools.partial(norm_gather_body, his),
        1,
        [((his, 2, picks, D), low, pallas.ANY)],
        [middle, gain_float[1:2]],
        his,
        own=(picks, D),
        gathers=True,
    )
    normed_two = normed_two.reshape(line * picks, D)

    mlp_far = after(mlp_far, normed_two)
    for at_c in range(2):
        mlp_full = lax.dynamic_update_slice(
            mlp_full, mlp_far[at_c][None, None, :, None], (1 - pl.y, at_c, 0, 1 - pl.lo, 0, 0)
        )
    mlp_full = mlp_full.reshape(D, wide)

    gate_up = matmul(normed_two, mlp_full[:, : 2 * part])
    gate = gate_up[:, :part]
    upward = gate_up[:, part:]
    mixed = (jax.nn.silu(gate) * upward).astype(low)
    down = matmul_nt(mixed, mlp_full[:, 2 * part :])
    ending, chosen = move(
        functools.partial(ending_body, his),
        2,
        [((picks, D), full, pltpu.VMEM), ((his, 2, picks, D), low, pallas.ANY)],
        [down.reshape(his, 2, picks, D), middle, gain_float[2:3]],
        his,
        scatter=(picks, D),
        own=(picks, D),
        gathers=True,
    )
    chosen = chosen.reshape(seqs * picks, D)
    logits = matmul_nt(chosen, head_rows)
    vocab_part = head_rows.shape[0]
    target_hit = (
        targets[0][:, None]
        == pl.s * vocab_part + jnp.arange(vocab_part, dtype=jnp.int32)[None, :]
    )
    part_high = jnp.max(logits, 1)
    part_sum = jnp.sum(jnp.exp(logits - part_high[:, None]), 1)
    part_target = jnp.sum(jnp.where(target_hit, logits, 0.0), 1)
    stats = jnp.stack([part_high, part_sum, part_target])
    for step in pl.ways(("dlo", "hi")):
        other = step(stats)
        larger = jnp.maximum(stats[0], other[0])
        summed = stats[1] * jnp.exp(stats[0] - larger) + other[1] * jnp.exp(other[0] - larger)
        stats = jnp.stack([larger, summed, stats[2] + other[2]])
    all_high, all_sum_exp, target_logit = stats
    row_total = all_high + jnp.log(all_sum_exp)
    mask_float = answer_mask.astype(full)
    count = jnp.sum(mask_float)
    own_mask = lax.dynamic_slice_in_dim(mask_float, pl.dp, 1, 0)[0]
    loss_part = jnp.where(
        pl.s == 0,
        jnp.sum(own_mask * (row_total - target_logit + zloss_weight * row_total * row_total)),
        0.0,
    )
    probs = jnp.exp(logits - row_total[:, None])
    logit_grad = (
        (own_mask / count)[:, None]
        * (probs * (1.0 + 2.0 * zloss_weight * row_total)[:, None] - target_hit.astype(full))
    ).astype(low)
    chosen_part = matmul(logit_grad, head_rows)
    ending_grad, final_gain_grad, branch_grad = move(
        functools.partial(ending_back_body, his),
        3,
        [
            ((picks, D), full, pltpu.VMEM),
            ((1, D), full, pltpu.VMEM),
            ((his, 2, picks, D), low, pallas.ANY),
        ],
        [chosen_part.reshape(his, 2, picks, D), ending, gain_float[2:3]],
        his,
        scatter=(picks, D),
        own=(picks, D),
        gathers=True,
    )
    branch_grad = branch_grad.reshape(line * picks, D)
    mixed_grad = matmul(branch_grad, mlp_full[:, 2 * part :])
    sigmoid_gate = jax.nn.sigmoid(gate)
    gate_grad = mixed_grad * upward * sigmoid_gate * (1.0 + gate * (1.0 - sigmoid_gate))
    upward_grad = mixed_grad * gate * sigmoid_gate
    gate_up_grad = jnp.concatenate([gate_grad, upward_grad], 1).astype(low)
    middle_up = matmul_nt(gate_up_grad, mlp_full[:, : 2 * part])
    down_grad = matmul_tn(after(branch_grad, middle_up), mixed)
    mlp_term = jnp.concatenate([matmul_tn(normed_two, gate_up_grad), down_grad], 1)
    mlp_term = mlp_term.astype(low).reshape(2, 2, his, 2, block, wide)
    mlp_state = cross_start(pl, mlp_term)
    head_rows_grad = matmul_tn(after(logit_grad, mlp_term), chosen).astype(low)
    head_grad = lax.psum_scatter(head_rows_grad, "dp", scatter_dimension=1, tiled=True)
    middle_up = after(middle_up, mlp_term, head_rows_grad)
    middle_grad, attn_branch_grad, middle_gain_grad = move(
        functools.partial(middle_back_body, his),
        4,
        [
            ((picks, D), full, pltpu.VMEM),
            ((picks, D), low, pltpu.VMEM),
            ((1, D), full, pltpu.VMEM),
        ],
        [middle_up.reshape(his, 2, picks, D), middle, gain_float[1:2], ending_grad],
        his,
        scatter=(picks, D),
    )
    branch_line = line_gather(pl, attn_branch_grad)
    attended_grad = matmul(attn_branch_grad, out_full).astype(low)
    query_raw, kv_part = attend_rows_back(
        attended_grad, pick_tables, pick_pos, kv_all, queries, attended, log_total
    )
    query_share = shares(query_raw)
    (kv_raw,) = move(
        functools.partial(keys_back_body, his),
        5,
        [((tokens, 2 * kv_width), low, pltpu.VMEM)],
        [kv_part.reshape(his, 2, tokens, 2 * kv_width), *token_tables],
        his,
        scatter=(tokens, 2 * kv_width),
        own=(tokens, 2 * kv_width),
        own_type=full,
    )
    pick_up = matmul_nt(query_raw, qkv_full[:, :D])
    tok_up = matmul_nt(kv_raw, qkv_full[:, D:QKV])
    start_part, start_gain_grad = norm_back(
        start, gain_float[0], jnp.concatenate([tok_up, pick_up], 0)
    )
    start_grad = jnp.concatenate(
        [start_part[:tokens], start_part[tokens:] + middle_grad], 0
    ).astype(low)

    back_rows = lax.all_to_all(start_grad, "seq", split_axis=1, concat_axis=0, tiled=True)
    branch_line, pick_line, query_share = after((branch_line, pick_line, query_share), start_grad)
    query_term = jnp.concatenate(
        [matmul_tn(pick_line, query_share), matmul_tn(branch_line, attended_share)], 1
    )
    query_term = query_term.astype(low).reshape(2, 2, his, 2, block, query_term.shape[-1])
    query_state = cross_start(pl, query_term)
    gains_term = jnp.stack([start_gain_grad, middle_gain_grad[0], final_gain_grad[0]], 1)

    def by_core(rows, core):
        rows = rows.reshape(rows.shape[0], 2, 2, seqs * block)
        return pick(rows, core, 2).reshape(rows.shape[0], D // 2)

    def grid(rows):
        return rows.astype(low).reshape(2, his, 2, block, rows.shape[-1])

    def token_term(core):
        return jnp.concatenate(
            [
                matmul_tn(by_core(after(normed_tok, start_grad), core), kv_raw),
                jnp.pad(by_core(gains_term.T, core).T, ((0, 0), (0, 125))),
            ],
            1,
        )

    token_got = pl.send(token_term(1 - pl.c).astype(low), dc=1)
    token_keep = token_term(pl.c)
    other_squares = [jnp.sum(after(w, token_keep) ** 2) for w in (attn_w, mlp_w, head)]
    mlp_state = cross_next(pl, mlp_state, other_squares)
    back_rows = after(back_rows, mlp_state[:2], query_term)
    back_got = pl.send(back_rows, dy=1)
    token_sum = grid(token_keep + after(token_got, back_rows).astype(full))
    token_got = pl.send(pick(token_sum, 1 - pl.y, 0), dy=1)

    other = ids_all[:, 0] - (pl.dp ^ 1) * emb_n
    places_in = jnp.where(
        local[:, 0] < emb_n,
        local[:, 0],
        jnp.where((other >= 0) & (other < emb_n), other + emb_n, 2 * emb_n),
    )
    chip_grad = (
        jnp.zeros((2 * emb_n + 8, emb_m), full)
        .at[places_in[0]]
        .add(after(back_rows, token_sum).astype(full))
    )
    mlp_term = cross_end(pl, mlp_state, chip_grad)
    mlp_got = line_parts(pl, mlp_term)
    query_state = cross_next(pl, query_state, chip_grad)
    token_sum = pick(token_sum, pl.y, 0).astype(full) + after(token_got, chip_grad).astype(full)
    token_got = pl.send(pick(token_sum, 1 - pl.lo, 1).astype(low), dlo=1)
    back_got = after(back_got, mlp_term, query_state[:2], token_sum)
    chip_grad = chip_grad.at[places_in[1]].add(back_got.astype(full))
    emb_part = chip_grad[emb_n : 2 * emb_n].astype(low)
    emb_got = pl.send(emb_part, dc=1)
    query_term = cross_end(pl, query_state, emb_part)
    query_got = line_parts(pl, query_term)
    token_sum = pick(token_sum, pl.lo, 1) + after(token_got, emb_part).astype(full)
    token_parts = hi_sum_start(pl, token_sum)
    head_grad = after(head_grad, emb_part).astype(full)
    head_square = head_grad * head_grad + eps_square
    head_rows_sum = jnp.sum(head_square, 1)
    head_cols_sum = jnp.sum(head_square, 0)
    emb_grad = chip_grad[:emb_n] + after(emb_got, head_rows_sum).astype(full)
    emb_square = emb_grad * emb_grad + eps_square
    emb_rows = jnp.sum(emb_square, 1)
    mlp_grad, mlp_rows, mlp_cols = join_columns(line_place(pl, after(mlp_got, emb_rows)))
    mlp_row_new = decay_rate * mlp_row + (1.0 - decay_rate) * mlp_rows / (3 * FF)
    token_sum = hi_sum_end(token_parts, mlp_cols)
    query_all = line_place(pl, after(query_got, mlp_cols)).reshape(line, block, 2, D // line)
    query_all = jnp.transpose(query_all, (1, 2, 0, 3)).reshape(block, 2 * D).astype(full)
    attn_grad = jnp.concatenate(
        [query_all[:, :D], token_sum[:, : 2 * kv_width], query_all[:, D:]], 1
    )
    gains_grad = token_sum[:, 2 * kv_width : 2 * kv_width + 3].T
    attn_square = attn_grad * attn_grad + eps_square
    attn_row_new = decay_rate * attn_row + (1.0 - decay_rate) * jnp.mean(attn_square, 1)
    attn_weight_square, mlp_weight_square, head_weight_square = other_squares
    scalars = [
        loss_part,
        jnp.sum(attn_row_new),
        *other_squares,
        jnp.where(pl.s == 0, jnp.sum(emb_row), 0.0),
        emb_square_sum,
        jnp.where(pl.dp == 0, jnp.sum(head_row), 0.0),
        jnp.sum(gains * gains),
        jnp.sum(emb_rows),
        jnp.sum(mlp_row_new),
        jnp.sum(head_rows_sum),
    ]
    slot = jnp.arange(128, dtype=jnp.int32)
    scalars = sum(jnp.where(slot == i, value, 0.0) for i, value in enumerate(scalars))
    (
        emb_row_sum,
        head_col_sum,
        attn_cols_sum,
        mlp_cols_sum,
        totals,
        head_row_sum,
        emb_col_sum,
    ) = sum_statistics(
        his,
        (emb_rows, head_cols_sum),
        (jnp.sum(attn_square, 0), mlp_cols, scalars),
        (head_rows_sum, jnp.sum(emb_square, 0)),
    )
    mlp_row_total, head_row_total = totals[10], totals[11]

    attn_col_new = decay_rate * attn_col + (1.0 - decay_rate) * attn_cols_sum / D
    mlp_col_new = decay_rate * mlp_col + (1.0 - decay_rate) * mlp_cols_sum / D
    attn_update = attn_grad * lax.rsqrt(
        attn_row_new[:, None] * attn_col_new[None, :] / (totals[1] / D)
    )
    mlp_update = mlp_grad * lax.rsqrt(
        mlp_row_new[:, None] * mlp_col_new[None, :] / (mlp_row_total / D)
    )
    emb_row_new = decay_rate * emb_row + (1.0 - decay_rate) * emb_row_sum / D
    emb_col_new = decay_rate * emb_col + (1.0 - decay_rate) * emb_col_sum / VOCAB
    emb_mean = (decay_rate * totals[5] + (1.0 - decay_rate) * totals[9] / D) / VOCAB
    emb_update = emb_grad * lax.rsqrt(emb_row_new[:, None] * emb_col_new[None, :] / emb_mean)
    head_row_new = decay_rate * head_row + (1.0 - decay_rate) * head_row_sum / D
    head_col_new = decay_rate * head_col + (1.0 - decay_rate) * head_col_sum / VOCAB
    head_mean = (decay_rate * totals[7] + (1.0 - decay_rate) * head_row_total / D) / VOCAB
    head_update = head_grad * lax.rsqrt(head_row_new[:, None] * head_col_new[None, :] / head_mean)
    moment_new = decay_rate * gains_moment + (1.0 - decay_rate) * (
        gains_grad * gains_grad + eps_square
    )
    gains_update = gains_grad * lax.rsqrt(moment_new)
    attn_new = finish(attn_w, attn_update, totals[2], D * (QKV + D))
    mlp_new = finish(mlp_w, mlp_update, totals[3], D * 3 * FF)
    emb_new = finish(emb, emb_update, totals[6], VOCAB * D)
    head_new = finish(head, head_update, totals[4], VOCAB * D)
    gains_new = finish(gains, gains_update, totals[8], 3 * D)
    return (
        totals[0],
        count,
        emb_grad,
        emb_new,
        emb_row_new,
        emb_col_new,
        head_grad,
        head_new,
        head_row_new,
        head_col_new,
        attn_grad,
        attn_new,
        attn_row_new,
        attn_col_new,
        mlp_grad,
        mlp_new,
        mlp_row_new,
        mlp_col_new,
        gains_grad,
        moment_new,
        gains_new,
    )


def solution(mesh):
    return jax.shard_map(
        on_device,
        mesh=mesh,
        in_specs=(
            P("dp", None),
            P("dp", None),
            P("dp", None),
            P(),
            P("dp", "seq"),
            P("seq", "dp"),
            P(("dp", "seq"), None),
            P(("dp", "seq"), None),
            P(None, ("dp", "seq")),
            P("dp"),
            P("seq"),
            P("seq"),
            P("dp"),
            P(("dp", "seq")),
            P(),
            P(("dp", "seq")),
            P(),
            P(None, ("dp", "seq")),
        ),
        out_specs=(
            P(),
            P(),
            P("dp", "seq"),
            P("dp", "seq"),
            P("dp"),
            P("seq"),
            P("seq", "dp"),
            P("seq", "dp"),
            P("seq"),
            P("dp"),
            P(("dp", "seq"), None),
            P(("dp", "seq"), None),
            P(("dp", "seq")),
            P(),
            P(("dp", "seq"), None),
            P(("dp", "seq"), None),
            P(("dp", "seq")),
            P(),
            P(None, ("dp", "seq")),
            P(None, ("dp", "seq")),
            P(None, ("dp", "seq")),
        ),
        check_vma=False,
    )
```

time: 1460 us -> 1090 us (0.75)
  waiting for transfers between devices: 627 us -> 167 us
  Pallas kernels: 0 us -> 338 us
  blocking collectives: 195 us -> 0 us
  starting transfers between devices: 53 us -> 105 us
  matrix products: 151 us -> 103 us
  other arithmetic: 223 us -> 197 us
  local copies, waits for them, and re-layouts: 171 us -> 145 us
    ppermute x52 -> x70, waiting for transfers between devices: 516 us -> 154 us  [send(): return lax.ppermute(value, ('dp', 'seq'), pairs)]
    pallas_call x0 -> x11, Pallas kernels: none -> 338 us  [the longest x6 276 us: move(): pallas.pallas_call(body, out_shape=tuple((jax.ShapeDtypeStruct(shape, dty...]
    all_to_all x2 -> x0, blocking collectives: 81.9 us -> none  [the longest x1 44.8 us: seq_sum(): lax.all_to_all(value.astype(low), 'seq', split_axis=0, concat_axis=0, til...]
    psum x3 -> x0, blocking collectives: 81.7 us -> none  [the longest x1 37.1 us: on_device(): lax.psum((jnp.sum(attn_square, 0), jnp.sum(mlp_square, 0), scalars), ('dp...]
    ppermute x52 -> x70, starting transfers between devices: 41.8 us -> 93.4 us  [send(): return lax.ppermute(value, ('dp', 'seq'), pairs)]
    all_to_all x1, waiting for transfers between devices: 60.6 us -> 11 us  [on_device(): lax.all_to_all(looked, 'seq', split_axis=0, concat_axis=1, tiled=True)]
    all_gather x4 -> x3, waiting for transfers between devices: 49.3 us -> 0.02 us  [the longest x1 0.02 us: on_device(): qkv_full = lax.all_gather(first_block, ('dp', 'seq'), axis=0, tiled=True)]
    dot_general x6 -> x0, matrix products: 39 us -> none  [the longest x1 12.1 us: attend_back(): jnp.einsum('ghqk,qgho->kgo', weights.astype(low), grad_out, preferred_ele...]
  transfers between devices with their start and end apart: 60 -> 78, of which waited for: 41 -> 27; matrix products, arithmetic and copies ran while one was open for 28% -> 29% of each run, Pallas kernels for 0% -> 24%
where the time goes in v2:
time: 1090 us; the launch traced here: 1080 us
  Pallas kernels  338 us (31%)
  other arithmetic  197 us (18%)
  waiting for transfers between devices  167 us (15%)
  local copies, waits for them, and re-layouts  145 us (13%)
  starting transfers between devices  105 us (10%)
  matrix products  103 us (9%)
  between operations  25.4 us (2%)
    pallas_call x6, Pallas kernels, move(): pallas.pallas_call(body, out_shape=tuple((jax.ShapeDtypeStruct(shape, dty...  276 us
    ppermute x70, waiting for transfers between devices, send(): return lax.ppermute(value, ('dp', 'seq'), pairs)  154 us
    ppermute x70, starting transfers between devices, send(): return lax.ppermute(value, ('dp', 'seq'), pairs)  93.4 us
    dot_general x6, matrix products, matmul(): return jnp.dot(left, right, preferred_element_type=jnp.float32)  39 us
    gather x4, local copies, waits for them, and re-layouts, look(): rows = jnp.take(emb, jnp.minimum(at, emb_n - 1), axis=0, mode='clip')  36.3 us
    dot_general x6, matrix products, matmul_nt(): lax.dot_general(left, right, (((1,), (1,)), ((), ())), preferred_element_...  36.1 us
    dot_general x7, matrix products, matmul_tn(): lax.dot_general(left, right, (((0,), (0,)), ((), ())), preferred_element_...  27.9 us
    scatter-add x1, other arithmetic, on_device(): chip_grad = chip_grad.at[places_in[1]].add(back_got.astype(full))  26 us
  transfers between devices with their start and end apart: 78, of which 27 were waited for; matrix products, arithmetic and copies ran while one was open for 29% of the time, Pallas kernels for 24%

profile of v2, /device:TPU:0, one launch (start us, length us, event | category | flops | bytes accessed | tf_op | source)
XLA Modules:
  0.0 1080.8 jit_solution(18195452973948773181)
XLA Ops:
  30.3 9.1 gather_fusion
  50.7 9.1 gather_fusion.2
  67.3 9.1 gather_fusion.3
  87.6 23.7 %collective-permute-done.5 = bf16[2560,256]{1,0:T(8,128)(2,1)} collective-permute-done((bf16[2560,256]{1,0:T(8,128)(2,1)}, bf16[2560,256]{1,0:T(8,128)(2,1)}, u32[]{:S(2)}, u32[]{:S(2)}) %collective-permute-start.5) | collective-permute-done | bytes 1310752 | tf_op jit(solution)/shard_map/ppermute | solution.py:114
  124.0 16.5 %collective-permute-done.12 = bf16[64,2112]{1,0:T(8,128)(2,1)} collective-permute-done((bf16[64,2112]{1,0:T(8,128)(2,1)}, bf16[64,2112]{1,0:T(8,128)(2,1)}, u32[]{:S(2)}, u32[]{:S(2)}) %collective-permute-start.12) | collective-permute-done | bytes 270368 | tf_op jit(solution)/shard_map/ppermute | solution.py:114
  154.6 11.0 %all-to-all-done = bf16[8,320,256]{2,1,0:T(8,128)(2,1)S(1)} async-done(((bf16[8,320,256]{2,1,0:T(8,128)(2,1)}), bf16[8,320,256]{2,1,0:T(8,128)(2,1)S(1)}, u32[]{:S(2)}, u32[]{:S(2)}) %all-to-all-start) | async-done | bytes 1310752 | tf_op jit(solution)/shard_map/all_to_all | solution.py:813
  177.2 85.5 %shard_map.337 = bf16[4,2,256,512]{3,2,1,0:T(8,128)(2,1)S(1)} custom-call(f32[256,512]{1,0:T(8,128)S(1)} %fusion.32.projected, f32[256,128]{1,0:T(8,128)S(1)} %pad_maximum_fusion.15.cosine, f32[256,128]{1,0:T(8,128)S(1)} %pad_maximum_fusion.16.sine), custom_call_target="tpu_custom_call" | custom-call | flops 1024 | bytes 1024 | tf_op jit(solution)/shard_map/pallas_call | solution.py:494
  271.0 15.7 %attend.1 = (bf16[8,256,64]{2,1,0:T(8,128)(2,1)}, bf16[64,2048]{1,0:T(8,128)(2,1)}, f32[8,256,64]{2,1,0:T(8,128)}, f32[8,256,128]{2,1,0:T(8,128)}) custom-call(f32[64,2048]{1,0:T(8,128)} %fusion.8.raw, f32[64,128]{1,0:T(8,128)} %pad_maximum_fusion.17.cosine, f32[64,128]{1,0:T(8,128)} %pad_maximum_fusion.18.sine, s32[64,1]{1,0:T(8,128)} %copy.228.places, ...), custom_call_target="tpu_custom_call" | custom-call | flops 1024 | bytes 1024 | tf_op jit(solution)/shard_map/attend/pallas_call | solution.py:585
  303.6 22.1 %shard_map.338 = bf16[4,2,64,2048]{3,2,1,0:T(8,128)(2,1)S(1)} custom-call(f32[64,2048]{1,0:T(8,128)S(1)} %convolution_add_fusion.values.middle, f32[1,2048]{1,0:T(1,128)S(1)} %get-tuple-element.376.gain), custom_call_target="tpu_custom_call" | custom-call | flops 1024 | bytes 1024 | tf_op jit(solution)/shard_map/pallas_call | solution.py:494
  327.6 17.0 %collective-permute-done.15 = bf16[4,64,2112]{2,1,0:T(8,128)(2,1)S(1)} collective-permute-done((bf16[4,64,2112]{2,1,0:T(8,128)(2,1)S(1)}, bf16[4,64,2112]{2,1,0:T(8,128)(2,1)S(1)}, u32[]{:S(2)}, u32[]{:S(2)}) %collective-permute-start.15) | collective-permute-done | bytes 1081376 | tf_op jit(solution)/shard_map/ppermute | solution.py:114
  354.0 55.8 %shard_map.339 = (f32[64,2048]{1,0:T(8,128)S(1)}, bf16[4,2,64,2048]{3,2,1,0:T(8,128)(2,1)S(1)}) custom-call(f32[4,2,64,2048]{3,2,1,0:T(8,128)} %bitcast.467, f32[64,2048]{1,0:T(8,128)S(1)} %convolution_add_fusion.values.middle, f32[1,2048]{1,0:T(1,128)S(1)} %get-tuple-element.375.gain), custom_call_target="tpu_custom_call" | custom-call | flops 1024 | bytes 1024 | tf_op jit(solution)/shard_map/pallas_call | solution.py:494
  411.2 12.5 %fusion.105 = (f32[512]{0:T(512)S(1)}, f32[512,4000]{0,1:T(8,128)S(1)}) fusion(bf16[512,2048]{1,0:T(8,128)(2,1)} %bitcast.437, bf16[4000,2048]{1,0:T(8,128)(2,1)} %all-gather.8.cloned.1.call-done), kind=kOutput, calls=%fused_computation.420 | convolution fusion | flops 8390655488 | bytes 26675200 | tf_op jit(solution)/shard_map/dot_general | solution.py:78
  451.9 16.2 %fusion.106 = f32[512,2048]{1,0:T(8,128)} fusion(bf16[512,4000]{0,1:T(8,128)(2,1)S(1)} %fusion.5, bf16[4000,2048]{1,0:T(8,128)(2,1)} %all-gather.8.cloned.1.call-done), kind=kOutput, calls=%fused_computation.421 | convolution fusion | flops 8388608000 | bytes 24674304 | tf_op jit(solution)/shard_map/dot_general | solution.py:74
  468.1 56.4 %shard_map.340 = (f32[64,2048]{1,0:T(8,128)S(1)}, f32[1,2048]{1,0:T(1,128)S(1)}, bf16[4,2,64,2048]{3,2,1,0:T(8,128)(2,1)S(1)}) custom-call(f32[4,2,64,2048]{3,2,1,0:T(8,128)} %bitcast.466, f32[64,2048]{1,0:T(8,128)S(1)} %get-tuple-element.145.ending, f32[1,2048]{1,0:T(1,128)S(1)} %get-tuple-element.375.gain), custom_call_target="tpu_custom_call" | custom-call | flops 1024 | bytes 1024 | tf_op jit(solution)/shard_map/pallas_call | solution.py:494
  549.6 11.6 %convolution_convert_fusion = bf16[4000,2048]{1,0:T(8,128)(2,1)} fusion(bf16[512,4000]{0,1:T(8,128)(2,1)S(1)} %copy-done.24, bf16[512,2048]{1,0:T(8,128)(2,1)S(1)} %bitcast.438), kind=kOutput, calls=%fused_computation.6 | convolution fusion | flops 8396800000 | bytes 22577152 | tf_op jit(solution)/shard_map/dot_general | solution.py:84
  571.0 18.4 %collective-permute-done.27 = bf16[64,2048]{1,0:T(8,128)(2,1)S(1)} collective-permute-done((bf16[64,2048]{1,0:T(8,128)(2,1)S(1)}, bf16[64,2048]{1,0:T(8,128)(2,1)S(1)}, u32[]{:S(2)}, u32[]{:S(2)}) %collective-permute-start.27) | collective-permute-done | bytes 262176 | tf_op jit(solution)/shard_map/ppermute | solution.py:114
  604.5 27.4 %shard_map.341 = (f32[64,2048]{1,0:T(8,128)S(1)}, bf16[64,2048]{1,0:T(8,128)(2,1)S(1)}, f32[1,2048]{1,0:T(1,128)S(1)}) custom-call(f32[4,2,64,2048]{3,2,1,0:T(8,128)S(1)} %bitcast.432, f32[64,2048]{1,0:T(8,128)S(1)} %convolution_add_fusion.values.middle, f32[1,2048]{1,0:T(1,128)S(1)} %get-tuple-element.376.gain, f32[64,2048]{1,0:T(8,128)S(1)} %get-tuple-element.150.ending_grad), custom_call_target="tpu_custom_call" | custom-call | flops 1024 | bytes 1024 | tf_op jit(solution)/shard_map/pallas_call | solution.py:494
  637.7 20.4 %attend_back.1 = (bf16[64,2048]{1,0:T(8,128)(2,1)}, f32[2048,512]{1,0:T(8,128)}) custom-call(bf16[64,2048]{1,0:T(8,128)(2,1)} %convolution_convert_fusion.5.grad, f32[64,128]{1,0:T(8,128)} %pad_maximum_fusion.17.cosine, f32[64,128]{1,0:T(8,128)} %pad_maximum_fusion.18.sine, s32[64,1]{1,0:T(8,128)} %copy.228.places, bf16[2048,512]{1,0:T(8,128)(2,1)} %bitcast.429, ...), custom_call_target="tpu_custom_call" | custom-call | flops 1024 | bytes 1024 | tf_op jit(solution)/shard_map/attend_back/pallas_call | solution.py:649
  660.5 29.2 %shard_map.342 = bf16[256,512]{1,0:T(8,128)(2,1)S(1)} custom-call(f32[4,2,256,512]{3,2,1,0:T(8,128)S(1)} %bitcast.433, f32[256,128]{1,0:T(8,128)S(1)} %pad_maximum_fusion.15.cosine, f32[256,128]{1,0:T(8,128)S(1)} %pad_maximum_fusion.16.sine), custom_call_target="tpu_custom_call" | custom-call | flops 1024 | bytes 1024 | tf_op jit(solution)/shard_map/pallas_call | solution.py:494
  813.7 21.3 %scatter_custom_fusion = f32[16008,256]{1,0:T(8,128)} fusion(s32[2560]{0:T(1024)} %get-tuple-element.287, f32[]{:T(128)} %constant.518.clone.1, bf16[2560,256]{1,0:T(8,128)(2,1)S(1)} %bitcast.461), kind=kCustom, calls=%fused_computation.14 | custom fusion | flops 1310720 | bytes 17703424 | tf_op jit(solution)/shard_map/scatter-add | solution.py:1033
  841.5 30.4 %collective-permute-done.50 = bf16[4,2,64,640]{3,2,1,0:T(8,128)(2,1)S(1)} collective-permute-done((bf16[4,2,64,640]{3,2,1,0:T(8,128)(2,1)}, bf16[4,2,64,640]{3,2,1,0:T(8,128)(2,1)S(1)}, u32[]{:S(2)}, u32[]{:S(2)}) %collective-permute-start.50) | collective-permute-done | bytes 655392 | tf_op jit(solution)/shard_map/ppermute | solution.py:114
  879.1 26.0 %scatter_custom_fusion.1 = f32[16008,256]{1,0:T(8,128)} fusion(f32[16008,256]{1,0:T(8,128)} %scatter_custom_fusion, s32[2560]{0:T(1024)} %get-tuple-element.286, bf16[2560,256]{1,0:T(8,128)(2,1)} %collective-permute-done.45), kind=kCustom, calls=%fused_computation.65 | custom fusion | flops 1310720 | bytes 17702912 | tf_op jit(solution)/shard_map/scatter-add | solution.py:1041
  1017.1 21.6 %sum_statistics.1 = f32[296,128]{1,0:T(8,128)S(1)} custom-call(f32[296,128]{1,0:T(8,128)S(1)} %constant_dynamic-update-slice_fusion.18.packed), custom_call_target="tpu_custom_call" | custom-call | tf_op jit(solution)/shard_map/sum_statistics/pallas_call | solution.py:714
  1051.8 12.1 %multiply_subtract_fusion.1 = f32[8000,256]{1,0:T(8,128)} fusion(f32[8000,256]{1,0:T(8,128)} %param.22, f32[8000,256]{1,0:T(8,128)} %get-tuple-element.298, f32[]{:T(128)} %bitcast.184, f32[256]{0:T(256)S(1)} %bitcast_add_fusion.4, f32[8000]{0:T(1024)S(1)} %fusion.61, f32[]{:T(128)} %bitcast.181), kind=kLoop, calls=%fused_computation.23 | loop fusion | flops 10240000 | bytes 24609032 | tf_op jit(solution)/shard_map/sub | solution.py:90
  (597 shorter events, 477.4 us)
Async XLA Ops:
  7.2 163.3 %all-gather.4.cloned.1.call-start = ((), (), s32[]{:S(2)}) async-start(), calls=%async_computation.3 | async-start | bytes 11354112 | tf_op jit(solution)/shard_map/all_gather | solution.py:801
  10.9 275.8 %all-gather.6.cloned.1.call-start = ((), (), s32[]{:S(2)}) async-start(), calls=%async_computation.4 | async-start | bytes 8650752 | tf_op jit(solution)/shard_map/all_gather | solution.py:803
  20.8 66.5 %collective-permute-start.6 = (bf16[64,2112]{1,0:T(8,128)(2,1)}, bf16[64,2112]{1,0:T(8,128)(2,1)}, u32[]{:S(2)}, u32[]{:S(2)}) collective-permute-start(bf16[64,2112]{1,0:T(8,128)(2,1)} %get-tuple-element.322), channel_id=1, source_target_pairs={{0,2},{1,3},{2,4},{3,5},{4,6},{5,7},{6,0},{7,1},{8,10},{9,11},{10,... | collective-permute-start | bytes 811016 | tf_op jit(solution)/shard_map/ppermute | solution.py:114
  22.6 65.0 %collective-permute-start.7 = (bf16[64,2112]{1,0:T(8,128)(2,1)}, bf16[64,2112]{1,0:T(8,128)(2,1)}, u32[]{:S(2)}, u32[]{:S(2)}) collective-permute-start(bf16[64,2112]{1,0:T(8,128)(2,1)} %get-tuple-element.321), channel_id=1, source_target_pairs={{0,4},{1,5},{2,6},{3,7},{4,0},{5,1},{6,2},{7,3},{8,12},{9,13},{10,... | collective-permute-start | bytes 811016 | tf_op jit(solution)/shard_map/ppermute | solution.py:114
  28.5 95.4 %collective-permute-start.8 = (bf16[64,2112]{1,0:T(8,128)(2,1)}, bf16[64,2112]{1,0:T(8,128)(2,1)}, u32[]{:S(2)}, u32[]{:S(2)}) collective-permute-start(bf16[64,2112]{1,0:T(8,128)(2,1)} %get-tuple-element.320), channel_id=1, source_target_pairs={{0,6},{1,7},{2,0},{3,1},{4,2},{5,3},{6,4},{7,5},{8,14},{9,15},{10,... | collective-permute-start | bytes 811016 | tf_op jit(solution)/shard_map/ppermute | solution.py:114
  65.8 45.4 %collective-permute-start.5 = (bf16[2560,256]{1,0:T(8,128)(2,1)}, bf16[2560,256]{1,0:T(8,128)(2,1)}, u32[]{:S(2)}, u32[]{:S(2)}) collective-permute-start(bf16[2560,256]{1,0:T(8,128)(2,1)} %fusion.135), channel_id=1, source_target_pairs={{0,16},{1,17},{2,18},{3,19},{4,20},{5,21},{6,22},{7,23},{8,24},{9,... | collective-permute-start | bytes 3932168 | tf_op jit(solution)/shard_map/ppermute | solution.py:114
  77.5 46.4 %collective-permute-start.9 = (bf16[64,2112]{1,0:T(8,128)(2,1)}, bf16[64,2112]{1,0:T(8,128)(2,1)}, u32[]{:S(2)}, u32[]{:S(2)}) collective-permute-start(bf16[64,2112]{1,0:T(8,128)(2,1)} %get-tuple-element.319), channel_id=1, source_target_pairs={{0,8},{1,9},{2,10},{3,11},{4,12},{5,13},{6,14},{7,15},{8,0},{9,1},... | collective-permute-start | bytes 811016 | tf_op jit(solution)/shard_map/ppermute | solution.py:114
  120.1 45.5 %all-to-all-start = ((bf16[8,320,256]{2,1,0:T(8,128)(2,1)}), bf16[8,320,256]{2,1,0:T(8,128)(2,1)S(1)}, u32[]{:S(2)}, u32[]{:S(2)}) async-start(bf16[8,320,256]{2,1,0:T(8,128)(2,1)} %bitcast.3), calls=%async_computation | async-start | bytes 2621440 | tf_op jit(solution)/shard_map/all_to_all | solution.py:813
  123.7 287.5 %all-gather.8.cloned.1.call-start = ((), (), s32[]{:S(2)}) async-start(), calls=%async_computation.5 | async-start | bytes 20480000 | tf_op jit(solution)/shard_map/all_gather | solution.py:822
  166.3 771.3 %reduce-scatter.2.cloned.1.call-start = ((), (), s32[]{:S(2)}) async-start(), calls=%async_computation.6 | async-start | bytes 20480000 | tf_op jit(solution)/shard_map/reduce_scatter | solution.py:951
  167.2 96.8 %collective-permute-start.13 = (bf16[2,4,64,2112]{3,2,1,0:T(8,128)(2,1)}, bf16[2,4,64,2112]{3,2,1,0:T(8,128)(2,1)}, u32[]{:S(2)}, u32[]{:S(2)}) collective-permute-start(bf16[2,4,64,2112]{3,2,1,0:T(8,128)(2,1)} %bitcast.22), channel_id=1, source_target_pairs={{0,1},{1,0},{2,3},{3,2},{4,5},{5,4},{6,7},{7,6},{8,9},{9,8},{10,11... | collective-permute-start | bytes 6488072 | tf_op jit(solution)/shard_map/ppermute | solution.py:114
  168.8 95.3 %collective-permute-start.14 = (bf16[2,4,64,2112]{3,2,1,0:T(8,128)(2,1)}, bf16[2,4,64,2112]{3,2,1,0:T(8,128)(2,1)}, u32[]{:S(2)}, u32[]{:S(2)}) collective-permute-start(bf16[2,4,64,2112]{3,2,1,0:T(8,128)(2,1)} %bitcast.22), channel_id=1, source_target_pairs={{0,16},{1,17},{2,18},{3,19},{4,20},{5,21},{6,22},{7,23},{8,24},{9,... | collective-permute-start | bytes 6488072 | tf_op jit(solution)/shard_map/ppermute | solution.py:114
  294.1 50.5 %collective-permute-start.15 = (bf16[4,64,2112]{2,1,0:T(8,128)(2,1)S(1)}, bf16[4,64,2112]{2,1,0:T(8,128)(2,1)S(1)}, u32[]{:S(2)}, u32[]{:S(2)}) collective-permute-start(bf16[4,64,2112]{2,1,0:T(8,128)(2,1)S(1)} %slice_bitcast_fusion.1), channel_id=1, source_target_pairs={{0,16},{1,17},{2,18},{3,19},{4,20},{5,21},{6,22},{7,23},{8,24},{9,... | collective-permute-start | bytes 3244040 | tf_op jit(solution)/shard_map/ppermute | solution.py:114
  296.9 47.7 %collective-permute-start.16 = (bf16[4,64,2112]{2,1,0:T(8,128)(2,1)S(1)}, bf16[4,64,2112]{2,1,0:T(8,128)(2,1)}, u32[]{:S(2)}, u32[]{:S(2)}) collective-permute-start(bf16[4,64,2112]{2,1,0:T(8,128)(2,1)S(1)} %slice_bitcast_fusion), channel_id=1, source_target_pairs={{0,1},{1,0},{2,3},{3,2},{4,5},{5,4},{6,7},{7,6},{8,9},{9,8},{10,11... | collective-permute-start | bytes 3244040 | tf_op jit(solution)/shard_map/ppermute | solution.py:114
  712.2 38.4 %collective-permute-start.24 = (bf16[64,2048]{1,0:T(8,128)(2,1)S(1)}, bf16[64,2048]{1,0:T(8,128)(2,1)S(1)}, u32[]{:S(2)}, u32[]{:S(2)}) collective-permute-start(bf16[64,2048]{1,0:T(8,128)(2,1)S(1)} %get-tuple-element.151), channel_id=1, source_target_pairs={{0,6},{1,7},{2,0},{3,1},{4,2},{5,3},{6,4},{7,5},{8,14},{9,15},{10,... | collective-permute-start | bytes 786440 | tf_op jit(solution)/shard_map/ppermute | solution.py:114
  716.9 88.8 %all-to-all-start.1 = ((bf16[320,8,256]{2,0,1:T(8,128)(2,1)}), bf16[320,8,256]{2,0,1:T(8,128)(2,1)S(1)}, u32[]{:S(2)}, u32[]{:S(2)}) async-start(bf16[320,8,256]{2,0,1:T(8,128)(2,1)} %pad_maximum_fusion.7), calls=%async_computation.1 | async-start | bytes 2621440 | tf_op jit(solution)/shard_map/all_to_all | solution.py:990
  729.1 64.0 %collective-permute-start.20 = (bf16[4,2,64,2112]{3,2,0,1:T(8,128)(2,1)}, bf16[4,2,64,2112]{3,2,0,1:T(8,128)(2,1)}, u32[]{:S(2)}, u32[]{:S(2)}) collective-permute-start(bf16[4,2,64,2112]{3,2,0,1:T(8,128)(2,1)} %bitcast.406), channel_id=1, source_target_pairs={{0,16},{1,17},{2,18},{3,19},{4,20},{5,21},{6,22},{7,23},{8,24},{9,... | collective-permute-start | bytes 6488072 | tf_op jit(solution)/shard_map/ppermute | solution.py:114
  732.4 60.8 %collective-permute-start.21 = (bf16[2,4,64,2112]{3,2,1,0:T(8,128)(2,1)}, bf16[2,4,64,2112]{3,2,1,0:T(8,128)(2,1)}, u32[]{:S(2)}, u32[]{:S(2)}) collective-permute-start(bf16[2,4,64,2112]{3,2,1,0:T(8,128)(2,1)} %dynamic-slice_bitcast_fusion.2), channel_id=1, source_target_pairs={{0,1},{1,0},{2,3},{3,2},{4,5},{5,4},{6,7},{7,6},{8,9},{9,8},{10,11... | collective-permute-start | bytes 6488072 | tf_op jit(solution)/shard_map/ppermute | solution.py:114
  750.6 55.2 %collective-permute-start.44 = (bf16[1024,640]{0,1:T(8,128)(2,1)}, bf16[1024,640]{0,1:T(8,128)(2,1)}, u32[]{:S(2)}, u32[]{:S(2)}) collective-permute-start(bf16[1024,640]{0,1:T(8,128)(2,1)} %fusion.35), channel_id=1, source_target_pairs={{0,8},{1,9},{2,10},{3,11},{4,12},{5,13},{6,14},{7,15},{8,0},{9,1},... | collective-permute-start | bytes 3932168 | tf_op jit(solution)/shard_map/ppermute | solution.py:114
  791.4 43.6 %collective-permute-start.48 = (bf16[4,2,64,512]{3,2,0,1:T(8,128)(2,1)}, bf16[4,2,64,512]{3,2,0,1:T(8,128)(2,1)}, u32[]{:S(2)}, u32[]{:S(2)}) collective-permute-start(bf16[4,2,64,512]{3,2,0,1:T(8,128)(2,1)} %bitcast.408), channel_id=1, source_target_pairs={{0,16},{1,17},{2,18},{3,19},{4,20},{5,21},{6,22},{7,23},{8,24},{9,... | collective-permute-start | bytes 1572872 | tf_op jit(solution)/shard_map/ppermute | solution.py:114
  792.3 42.7 %collective-permute-start.49 = (bf16[2,4,64,512]{3,2,1,0:T(8,128)(2,1)}, bf16[2,4,64,512]{3,2,1,0:T(8,128)(2,1)}, u32[]{:S(2)}, u32[]{:S(2)}) collective-permute-start(bf16[2,4,64,512]{3,2,1,0:T(8,128)(2,1)} %dynamic-slice_bitcast_fusion.6), channel_id=1, source_target_pairs={{0,1},{1,0},{2,3},{3,2},{4,5},{5,4},{6,7},{7,6},{8,9},{9,8},{10,11... | collective-permute-start | bytes 1572872 | tf_op jit(solution)/shard_map/ppermute | solution.py:114
  802.6 70.6 %collective-permute-start.46 = (bf16[4,64,2112]{2,1,0:T(8,128)(2,1)}, bf16[4,64,2112]{2,1,0:T(8,128)(2,1)}, u32[]{:S(2)}, u32[]{:S(2)}) collective-permute-start(bf16[4,64,2112]{2,1,0:T(8,128)(2,1)} %fusion.36), channel_id=1, source_target_pairs={{0,1},{1,0},{2,3},{3,2},{4,5},{5,4},{6,7},{7,6},{8,9},{9,8},{10,11... | collective-permute-start | bytes 3244040 | tf_op jit(solution)/shard_map/ppermute | solution.py:114
  803.7 69.5 %collective-permute-start.47 = (bf16[4,64,2112]{2,1,0:T(8,128)(2,1)}, bf16[4,64,2112]{2,1,0:T(8,128)(2,1)}, u32[]{:S(2)}, u32[]{:S(2)}) collective-permute-start(bf16[4,64,2112]{2,1,0:T(8,128)(2,1)} %fusion.37), channel_id=1, source_target_pairs={{0,16},{1,17},{2,18},{3,19},{4,20},{5,21},{6,22},{7,23},{8,24},{9,... | collective-permute-start | bytes 3244040 | tf_op jit(solution)/shard_map/ppermute | solution.py:114
  805.7 73.4 %collective-permute-start.45 = (bf16[2560,256]{1,0:T(8,128)(2,1)S(1)}, bf16[2560,256]{1,0:T(8,128)(2,1)}, u32[]{:S(2)}, u32[]{:S(2)}) collective-permute-start(bf16[2560,256]{1,0:T(8,128)(2,1)S(1)} %bitcast.460), channel_id=1, source_target_pairs={{0,16},{1,17},{2,18},{3,19},{4,20},{5,21},{6,22},{7,23},{8,24},{9,... | collective-permute-start | bytes 3932168 | tf_op jit(solution)/shard_map/ppermute | solution.py:114
  (138 other events, 2120.8 us)
Sparse Core Ops, SparseCore 0:
  11.6 131.1 all-gather.3
  145.8 113.0 all-gather.5
  261.0 126.0 all-gather.7
  561.4 125.3 reduce-scatter.1

commit v3 on v2

--- a/solution.py
+++ b/solution.py
@@ -145,42 +145,50 @@
     return lax.dynamic_update_slice_in_dim(array, jnp.expand_dims(block, axis), index, axis)
 
 
-def line_parts(pl, blocks):
-    n = pl.his
+def line_pairs(pl, blocks):
+    grid = blocks.reshape(2, pl.his, *blocks.shape[1:])
+    return pick(grid, pl.c, 0), pl.send(pick(grid, 1 - pl.c, 0), dc=1)
+
+
+def line_sends(pl, here, came):
+    pairs = jnp.stack([here, came], 1)
     got = []
-    for dc in range(2):
-        for k in range(n):
-            block = pick(blocks, (pl.c ^ dc) * n + (pl.hi + k) % n, 0)
-            got.append(pl.send(block, dc=dc, up=k) if dc or k else block)
+    for k in range(pl.his):
+        pair = pick(pairs, (pl.hi + k) % pl.his, 0)
+        got.append(pl.send(pair, up=k) if k else pair)
     return got
 
 
+def place_body(*refs):
+    pairs, out, sems = refs[:-2], refs[-2], refs[-1]
+    n = len(pairs)
+    dp, s = lax.axis_index("dp"), lax.axis_index("seq")
+    c, hi = dp % 2, s // 2
+    copies = []
+    for k, pair in enumerate(pairs):
+        for j, side in enumerate((c, 1 - c)):
+            copies.append(
+                pltpu.make_async_copy(
+                    pair.at[j], out.at[side * n + lax.rem(hi + n - k, n)], sems.at[2 * k + j]
+                )
+            )
+            copies[-1].start()
+    for copy in copies:
+        copy.wait()
+
+
 def line_place(pl, got):
-    n = pl.his
-    out = jnp.zeros((2 * n, *got[0].shape), got[0].dtype)
-    for at, block in enumerate(got):
-        origin = (pl.c ^ (at // n)) * n + (pl.hi + n - at % n) % n
-        out = put(out, block, origin, 0)
-    return out
-
-
-def line_gather(pl, rows, work=()):
-    first = jnp.stack([rows] + [after(pl.send(rows, up=k), *work) for k in range(1, pl.his)])
-    both = jnp.stack([first, pl.send(first, dc=1)])
-    return both.reshape(2 * pl.his * rows.shape[0], rows.shape[1])
-
-
-def hi_sum_start(pl, part):
-    parts = [pick(part, pl.hi, 0)]
-    for k in range(1, pl.his):
-        block = pick(part, (pl.hi + k) % pl.his, 0).astype(low)
-        parts.append(pl.send(block, up=k))
-    return parts
-
-
-def hi_sum_end(parts, *work):
-    parts = after(parts, *work)
-    return sum((part.astype(full) for part in parts[1:]), parts[0].astype(full))
+    count = len(got)
+    shape = (2 * count, *got[0].shape[1:])
+    return pallas.pallas_call(
+        place_body,
+        out_shape=jax.ShapeDtypeStruct(shape, got[0].dtype),
+        in_specs=[pallas.BlockSpec(memory_space=pallas.ANY)] * count,
+        out_specs=pallas.BlockSpec(memory_space=pltpu.VMEM),
+        scratch_shapes=[pltpu.SemaphoreType.DMA((2 * count,))],
+        cost_estimate=SMALL,
+        name="line_place",
+    )(*got)
 
 
 def cross_start(pl, term):
@@ -197,7 +205,12 @@
     b = pick(b, pl.lo, 2).astype(full) + got_b.astype(full)
     send_a = pick(a, 1 - pl.lo, 1).astype(low)
     send_b = pick(b, 1 - pl.y, 0).astype(low)
-    return pick(a, pl.lo, 1), pick(b, pl.y, 0), pl.send(send_a, dlo=1), pl.send(send_b, dy=1)
+    keep = pick(a, pl.lo, 1), pick(b, pl.y, 0)
+    return keep, (send_a, send_b)
+
+
+def cross_send(pl, keep, sends):
+    return *keep, pl.send(sends[0], dlo=1), pl.send(sends[1], dy=1)
 
 
 def cross_end(pl, state, *work):
@@ -283,6 +296,9 @@
         self.his = his
         self.hi, self.lo, self.c = s // 2, s % 2, dp % 2
         self.side = {"c": self.c, "lo": self.lo}
+        self.across = [
+            (dp, lax.rem(self.hi + k, his) * 2 + self.lo) for k in range(his)
+        ]
         self.ids = {
             "c": (dp + 1 - 2 * self.c, s),
             "lo": (dp, s + 1 - 2 * self.lo),
@@ -291,12 +307,13 @@
         }
 
     def meet(self, *names):
+        others = [self.ids[name] for name in names if name != "line"]
+        if "line" in names:
+            others += self.across[1:]
         barrier = pltpu.get_barrier_semaphore()
-        for name in names:
-            pallas.semaphore_signal(
-                barrier, inc=1, device_id=self.ids[name], device_id_type=MESH
-            )
-        pallas.semaphore_wait(barrier, len(names))
+        for other in others:
+            pallas.semaphore_signal(barrier, inc=1, device_id=other, device_id_type=MESH)
+        pallas.semaphore_wait(barrier, len(others))
 
     def copy(self, source, target, sems, at, name):
         return pltpu.make_async_remote_copy(
@@ -304,7 +321,7 @@
             dst_ref=target,
             send_sem=sems[0].at[at],
             recv_sem=sems[1].at[at],
-            device_id=self.ids[name],
+            device_id=self.ids[name] if isinstance(name, str) else self.across[name],
             device_id_type=MESH,
         )
 
@@ -317,7 +334,7 @@
     lax.fori_loop(0, n // ROWS, one, 0)
 
 
-def kernel_scatter(core, name, part, total, held, side_sems, up_sems):
+def kernel_scatter(core, name, part, total, held, side_sems, up_sems, beside=iter(())):
     his, side = core.his, core.side[name]
     side_out, side_in, up_out, up_in = held
     n = part.shape[2]
@@ -351,17 +368,22 @@
         if j < his - 1:
             climb.append(core.copy(up_out.at[j], up_in.at[j], up_sems, j, "up"))
             climb[j].start()
+        next(beside, None)
     return over + climb
 
 
-def kernel_gather(core, name, own, out, local_sem, side_sems, up_sems):
+def gather_steps(core, name, own, out, copies, sems, side_first=False):
     his, side = core.his, core.side[name]
-    here = pltpu.make_async_copy(own, out.at[core.hi, side], local_sem)
+    local_sem, side_sems, up_sems = sems[0], sems[1:3], sems[3:5]
+
+    def slot(h):
+        return out.at[side, h] if side_first else out.at[h, side]
+
+    here = pltpu.make_async_copy(own, slot(core.hi), local_sem)
     here.start()
     over, climb = [], []
     for j in range(his):
-        h = lax.rem(core.hi + his - j, his)
-        block = out.at[h, side]
+        block = slot(lax.rem(core.hi + his - j, his))
         source = own if j == 0 else block
         if j:
             climb[j - 1].wait_recv()
@@ -370,10 +392,79 @@
             climb[j].start()
         over.append(core.copy(source, block, side_sems, j, name))
         over[j].start()
+        yield
     for copy in over:
         copy.wait_recv()
     here.wait()
-    return over + climb
+    copies += over + climb
+
+
+def kernel_gather(*args, **kwargs):
+    for _ in gather_steps(*args, **kwargs):
+        pass
+
+
+def direct_start(core, own, out, sems):
+    here = pltpu.make_async_copy(own, out.at[core.c, core.hi], sems[0])
+    place = out.at[core.c, core.hi]
+    climb = [core.copy(own, place, sems[3:5], k - 1, k) for k in range(1, core.his)]
+    over = [core.copy(own, place, sems[1:3], 0, "c")]
+    for copy in [here, *climb, *over]:
+        copy.start()
+    return here, climb, over
+
+
+def direct_end(core, started, out, sems):
+    here, climb, over = started
+    order = sorted(range(1, core.his), key=lambda k: min(k, core.his - k))
+    for k in order:
+        climb[k - 1].wait_recv()
+        block = out.at[core.c, lax.rem(core.hi + core.his - k, core.his)]
+        over.append(core.copy(block, block, sems[1:3], k, "c"))
+        over[-1].start()
+    for copy in over:
+        copy.wait_recv()
+    here.wait()
+    sent(climb + over)
+
+
+def direct_scratch(his):
+    dma = pltpu.SemaphoreType.DMA
+    return [dma, dma((his,)), dma((his,)), dma((his - 1,)), dma((his - 1,))]
+
+
+def kernel_swap_start(core, blocks, came, side_sems):
+    his = core.his
+    over = core.copy(
+        blocks.at[pallas.ds((1 - core.c) * his, his)], came, side_sems, 0, "c"
+    )
+    over.start()
+    return over
+
+
+def kernel_swap_end(core, over, blocks, came, out, local_sems, up_sems):
+    his, c, hi = core.his, core.c, core.hi
+    mine, theirs = c * his + hi, (1 - c) * his + hi
+    here = [pltpu.make_async_copy(blocks.at[mine], out.at[mine], local_sems.at[0])]
+    climb = []
+    for k in range(1, his):
+        to = lax.rem(hi + k, his)
+        climb.append(core.copy(blocks.at[c * his + to], out.at[mine], up_sems, 2 * k - 2, k))
+    over.wait_recv()
+    here.append(pltpu.make_async_copy(came.at[hi], out.at[theirs], local_sems.at[1]))
+    for k in range(1, his):
+        to = lax.rem(hi + k, his)
+        climb.append(core.copy(came.at[to], out.at[theirs], up_sems, 2 * k - 1, k))
+    for copy in here + climb:
+        copy.start()
+    return here, [over] + climb
+
+
+def swap_done(here, copies):
+    for copy in here:
+        copy.wait()
+    for copy in copies[1:]:
+        copy.wait_recv()
 
 
 def sent(copies):
@@ -393,7 +484,7 @@
     return back, jnp.sum(upstream * normed, 0, keepdims=True)
 
 
-def norm_gather_body(his, values, gain, out, own, *sems):
+def norm_gather_body(his, values, gain, blocks, out, swapped, came, own, *sems):
     core = Core(his)
     by_rows(
         values.shape[0],
@@ -401,8 +492,13 @@
             (at, slice(None)), norm_rows(values[at, :], gain[...]).astype(low)
         ),
     )
-    core.meet("c", "up", "down")
-    sent(kernel_gather(core, "c", own, out, sems[0], sems[1:3], sems[3:5]))
+    core.meet("c", "line")
+    over = kernel_swap_start(core, blocks, came, sems[1:3])
+    copies = []
+    kernel_gather(core, "c", own, out, copies, sems[5:10])
+    here, more = kernel_swap_end(core, over, blocks, came, swapped, sems[0], sems[3:5])
+    swap_done(here, more)
+    sent(copies + more)
 
 
 def turn_keys(source, cosine, sine, target):
@@ -417,16 +513,88 @@
     core = Core(his)
     turn_keys(projected, cosine[...], sine[...], own)
     core.meet("lo", "up", "down")
-    sent(kernel_gather(core, "lo", own, out, sems[0], sems[1:3], sems[3:5]))
-
-
-def keys_back_body(his, part, cosine, sine, out, total, *rest):
-    held, sems = rest[:4], rest[4:]
+    copies = []
+    kernel_gather(core, "lo", own, out, copies, sems)
+    sent(copies)
+
+
+def keys_back_body(
+    his, part, cosine, sine, blocks, out, swapped, came, total, *rest
+):
+    swap_sems, held, sems = rest[:5], rest[5:9], rest[9:13]
     core = Core(his)
-    core.meet("lo", "up", "down")
-    copies = kernel_scatter(core, "lo", part, total, held, sems[0:2], sems[2:4])
+    core.meet("c", "lo", "line")
+    over = kernel_swap_start(core, blocks, came, swap_sems[1:3])
+    copies = []
+    copies += kernel_scatter(core, "lo", part, total, held, sems[0:2], sems[2:4])
+    here, more = kernel_swap_end(core, over, blocks, came, swapped, swap_sems[0], swap_sems[3:5])
     turn_keys(total, cosine[...], -sine[...], out)
-    sent(copies)
+    swap_done(here, more)
+    sent(copies + more)
+
+
+def layer_body(his, blocks, tokens, grad, gains, rows, columns, swapped, came, out_low, in_low, *sems):
+    core = Core(his)
+    wide = blocks.shape[2] // 2
+    side, keys = 2 * his, 2 * KVH * HD
+    core.meet("c", "line")
+    over = kernel_swap_start(core, blocks, came, sems[1:3])
+    climb = []
+    for k in range(1, his):
+        to = lax.rem(core.hi + k, his)
+        out_low[k - 1] = tokens[to].astype(low)
+        climb.append(core.copy(out_low.at[k - 1], in_low.at[k - 1], sems[5:7], k - 1, k))
+        climb[-1].start()
+    here, more = kernel_swap_end(core, over, blocks, came, swapped, sems[0], sems[3:5])
+    total = tokens[core.hi]
+    for k, copy in enumerate(climb):
+        copy.wait_recv()
+        total = total + in_low[k].astype(full)
+    gains[...] = total[:, keys:]
+    row_sum = jnp.zeros(rows.shape, full)
+    pieces = [(D, total[:, :keys])]
+    swap_done(here, more)
+    for t in range(side):
+        pieces.append((t * wide, swapped[t, :, :wide].astype(full)))
+        pieces.append((QKV + t * wide, swapped[t, :, wide:].astype(full)))
+    for at, piece in pieces:
+        till = at + piece.shape[1]
+        grad[:, at:till] = piece
+        square = piece * piece + eps_square
+        columns[:, at:till] = jnp.sum(square, 0, keepdims=True)
+        row_sum = row_sum + jnp.sum(square, 1, keepdims=True)
+    rows[...] = row_sum
+    sent(climb + more)
+
+
+def layer_gradient(his, blocks, tokens):
+    line, rows, columns = blocks.shape
+    extra = tokens.shape[2] - 2 * KVH * HD
+    dma = pltpu.SemaphoreType.DMA
+    return pallas.pallas_call(
+        functools.partial(layer_body, his),
+        out_shape=(
+            jax.ShapeDtypeStruct((rows, QKV + D), full),
+            jax.ShapeDtypeStruct((rows, extra), full),
+            jax.ShapeDtypeStruct((rows, 1), full),
+            jax.ShapeDtypeStruct((1, QKV + D), full),
+        ),
+        in_specs=[pallas.BlockSpec(memory_space=pltpu.VMEM)] * 2,
+        out_specs=(pallas.BlockSpec(memory_space=pltpu.VMEM),) * 4,
+        scratch_shapes=[
+            pltpu.VMEM(blocks.shape, low),
+            pltpu.VMEM((his, rows, columns), low),
+            pltpu.VMEM((his - 1, *tokens.shape[1:]), low),
+            pltpu.VMEM((his - 1, *tokens.shape[1:]), low),
+            dma((2,)),
+            *[dma((count,)) for count in (1, 1, 2 * his - 2, 2 * his - 2, his - 1, his - 1)],
+        ],
+        cost_estimate=SMALL,
+        compiler_params=pltpu.CompilerParams(
+            collective_id=7, has_side_effects=True, vmem_limit_bytes=32 * 2**20
+        ),
+        name="layer_gradient",
+    )(blocks, tokens)
 
 
 def ending_body(his, part, middle, gain, ending, chosen, own, *rest):
@@ -441,7 +609,7 @@
         own[at, :] = norm_rows(values, gain[...]).astype(low)
 
     by_rows(middle.shape[0], finish_rows)
-    copies += kernel_gather(core, "lo", own, chosen, sems[4], sems[5:7], sems[7:9])
+    kernel_gather(core, "lo", own, chosen, copies, sems[4:9])
     sent(copies)
 
 
@@ -459,7 +627,7 @@
         gain_grad[...] += gained
 
     by_rows(ending.shape[0], back_rows)
-    copies += kernel_gather(core, "c", own, branch, sems[4], sems[5:7], sems[7:9])
+    kernel_gather(core, "c", own, branch, copies, sems[4:9])
     sent(copies)
 
 
@@ -481,15 +649,20 @@
     sent(copies)
 
 
-def move(body, collective_id, outs, args, his, scatter=None, own=None, own_type=low, gathers=False):
+def move(body, collective_id, outs, args, his, scatter=None, own=None, own_type=low, gathers=0, swap=None):
     dma = pltpu.SemaphoreType.DMA
     scratch = []
+    if swap:
+        scratch.append(pltpu.VMEM(swap, low))
     if own:
         scratch.append(pltpu.VMEM(own, own_type))
+    if swap:
+        scratch += [dma((2,))]
+        scratch += [dma((count,)) for count in (1, 1, 2 * his - 2, 2 * his - 2)]
     if scatter:
         scratch += [pltpu.VMEM((count, *scatter), low) for count in (his, his, his - 1, his - 1)]
         scratch += [dma((his,)), dma((his,)), dma((his - 1,)), dma((his - 1,))]
-    if gathers:
+    for _ in range(gathers):
         scratch += [dma, dma((his,)), dma((his,)), dma((his - 1,)), dma((his - 1,))]
     return pallas.pallas_call(
         body,
@@ -548,8 +721,13 @@
     )
 
 
-def attend_body(raw, cosine, sine, places, kv, turned_out, out_low, held_out, logs, k_held, v_held):
+def attend_body(
+    his, raw, cosine, sine, places, kv, own, turned_out, out_low, held_out, logs, line_out, k_held, v_held, *sems
+):
     picks, keys = raw.shape[0], kv.shape[0]
+    core = Core(his)
+    core.meet("c", "line")
+    started = direct_start(core, own, line_out, sems)
     split_kv(kv, k_held, v_held)
     for j in range(D // (2 * HD)):
         pair = turned(raw[:, 2 * HD * j : 2 * HD * (j + 1)], cosine[...], sine[...]).astype(low)
@@ -577,33 +755,42 @@
             pair.append(held_out[t, at * picks : (at + 1) * picks, :])
         pair = jnp.concatenate(pair, 1)
         out_low[:, 2 * HD * j : 2 * HD * (j + 1)] = pair.astype(low)
-
-
-def attend_rows(raw, tables, places, kv):
+    direct_end(core, started, line_out, sems)
+
+
+def attend_rows(his, raw, tables, places, kv, own):
     picks, keys = raw.shape[0], kv.shape[0]
     stacks, rows = HEADS // STACK, STACK * picks
     return pallas.pallas_call(
-        attend_body,
+        functools.partial(attend_body, his),
         out_shape=(
             jax.ShapeDtypeStruct((stacks, rows, HD), low),
             jax.ShapeDtypeStruct((picks, D), low),
             jax.ShapeDtypeStruct((stacks, rows, HD), full),
             jax.ShapeDtypeStruct((stacks, rows, 2 * HD), full),
+            jax.ShapeDtypeStruct((2, his, *own.shape), low),
         ),
-        in_specs=[pallas.BlockSpec(memory_space=pltpu.VMEM)] * 5,
-        out_specs=(pallas.BlockSpec(memory_space=pltpu.VMEM),) * 4,
-        scratch_shapes=[pltpu.VMEM((KVH, keys, HD), low)] * 2,
-        compiler_params=pltpu.CompilerParams(vmem_limit_bytes=56 * 2**20),
+        in_specs=[pallas.BlockSpec(memory_space=pltpu.VMEM)] * 6,
+        out_specs=(pallas.BlockSpec(memory_space=pltpu.VMEM),) * 4
+        + (pallas.BlockSpec(memory_space=pallas.ANY),),
+        scratch_shapes=[pltpu.VMEM((KVH, keys, HD), low)] * 2 + direct_scratch(his),
+        compiler_params=pltpu.CompilerParams(
+            collective_id=9, has_side_effects=True, vmem_limit_bytes=56 * 2**20
+        ),
         cost_estimate=SMALL,
         name="attend",
-    )(raw, *tables, places[:, None], kv)
+    )(raw, *tables, places[:, None], kv, own)
 
 
 def attend_back_body(
-    grad, cosine, sine, places, kv, queries, held_out, logs, raw, kv_grad, k_held, v_held,
-    grad_held, query_held, *sums
+    his, grad, cosine, sine, places, kv, queries, held_out, logs, own, raw, kv_grad, line_out, k_held, v_held,
+    grad_held, query_held, *rest
 ):
     picks, keys = grad.shape[0], kv.shape[0]
+    sems, sums = rest[:5], rest[5:]
+    core = Core(his)
+    core.meet("c", "line")
+    started = direct_start(core, own, line_out, sems)
     scale = HD ** (-0.5)
     split_kv(kv, k_held, v_held)
     for j in range(D // (2 * HD)):
@@ -639,33 +826,186 @@
         for g in range(0, 2 * KVH, 2):
             both = jnp.concatenate([total[g], total[g + 1]], 0)
             kv_grad[:, g * HD : (g + 2) * HD] = both.T
-
-
-def attend_rows_back(grad, tables, places, kv, queries, held_out, logs):
+    direct_end(core, started, line_out, sems)
+
+
+def attend_rows_back(his, grad, tables, places, kv, queries, held_out, logs, own):
     picks, keys = grad.shape[0], kv.shape[0]
     stacks, rows = HEADS // STACK, STACK * picks
     outside = keys > 4096
     by_head = (2 * KVH, HD, keys)
-    raw, kv_grad = pallas.pallas_call(
-        attend_back_body,
+    raw, kv_grad, line_out = pallas.pallas_call(
+        functools.partial(attend_back_body, his),
         out_shape=(
             jax.ShapeDtypeStruct((picks, D), low),
             jax.ShapeDtypeStruct(by_head if outside else (keys, 2 * KVH * HD), full),
+            jax.ShapeDtypeStruct((2, his, *own.shape), low),
         ),
-        in_specs=[pallas.BlockSpec(memory_space=pltpu.VMEM)] * 8,
-        out_specs=(pallas.BlockSpec(memory_space=pltpu.VMEM),) * 2,
+        in_specs=[pallas.BlockSpec(memory_space=pltpu.VMEM)] * 9,
+        out_specs=(pallas.BlockSpec(memory_space=pltpu.VMEM),) * 2
+        + (pallas.BlockSpec(memory_space=pallas.ANY),),
         scratch_shapes=[
             pltpu.VMEM((KVH, keys, HD), low),
             pltpu.VMEM((KVH, keys, HD), low),
             pltpu.VMEM((stacks, rows, HD), low),
             pltpu.VMEM((stacks, rows, HD), full),
+            *direct_scratch(his),
         ]
         + ([] if outside else [pltpu.VMEM(by_head, full)]),
-        compiler_params=pltpu.CompilerParams(vmem_limit_bytes=58 * 2**20),
+        compiler_params=pltpu.CompilerParams(
+            collective_id=10, has_side_effects=True, vmem_limit_bytes=58 * 2**20
+        ),
         cost_estimate=SMALL,
         name="attend_back",
-    )(grad, *tables, places[:, None], kv, queries, held_out, logs)
-    return raw, kv_grad.reshape(2 * KVH * HD, keys).T if outside else kv_grad
+    )(grad, *tables, places[:, None], kv, queries, held_out, logs, own)
+    kv_grad = kv_grad.reshape(2 * KVH * HD, keys).T if outside else kv_grad
+    return raw, kv_grad, line_out
+
+
+def weights_body(
+    his, blocks, whole, came, local_sems, core_sems, core_sems_in, up_sems, up_sems_in, x_sems, x_sems_in, y_sems,
+    y_sems_in
+):
+    core = Core(his)
+    dp, s = lax.axis_index("dp"), lax.axis_index("seq")
+    y, c, hi, lo = dp // 2, core.c, core.hi, core.lo
+    core.ids["y"] = (dp + 2 - 4 * y, s)
+    core.meet("c", "y", "lo", "line")
+    swap = core.copy(blocks.at[pallas.ds((1 - c) * his, his)], came, (core_sems, core_sems_in), 0, "c")
+    swap.start()
+    here, climb, over_x, over_y = [], {}, {}, {}
+
+    def cross(source, slot, at):
+        over_x[at] = core.copy(source, slot, (x_sems, x_sems_in), at, "lo")
+        over_y[at] = core.copy(source, slot, (y_sems, y_sems_in), at, "y")
+        over_x[at].start()
+        over_y[at].start()
+
+    def leave(source, j, side):
+        slot = whole.at[y, side, hi, lo]
+        here.append(pltpu.make_async_copy(source(hi), slot, local_sems.at[j]))
+        here[-1].start()
+        for k in range(1, his):
+            climb[2 * k + j] = core.copy(
+                source(lax.rem(hi + k, his)), slot, (up_sems, up_sems_in), 2 * k + j - 2, k
+            )
+            climb[2 * k + j].start()
+        cross(source(hi), slot, j)
+
+    leave(lambda h: blocks.at[c * his + h], 0, c)
+    swap.wait_recv()
+    leave(lambda h: came.at[h], 1, 1 - c)
+    for k in sorted(range(1, his), key=lambda k: min(k, his - k)):
+        h = lax.rem(hi + his - k, his)
+        for j, side in enumerate((c, 1 - c)):
+            climb[2 * k + j].wait_recv()
+            slot = whole.at[y, side, h, lo]
+            cross(slot, slot, 2 * k + j)
+    for copy in [*over_x.values(), *over_y.values()]:
+        copy.wait_recv()
+    for copy in here:
+        copy.wait()
+    sent([swap, *climb.values(), *over_x.values(), *over_y.values()])
+
+
+def gather_weights(his, blocks):
+    line, block, wide = blocks.shape
+    dma = pltpu.SemaphoreType.DMA
+    counts = (1, 2 * his - 2, 2 * his, 2 * his)
+    return pallas.pallas_call(
+        functools.partial(weights_body, his),
+        out_shape=jax.ShapeDtypeStruct((2, 2, his, 2, block, wide), low),
+        in_specs=[pallas.BlockSpec(memory_space=pltpu.VMEM)],
+        out_specs=pallas.BlockSpec(memory_space=pallas.ANY),
+        scratch_shapes=[
+            pltpu.VMEM((his, block, wide), low),
+            dma((2,)),
+            *[dma((count,)) for count in counts for _ in range(2)],
+        ],
+        cost_estimate=SMALL,
+        compiler_params=pltpu.CompilerParams(
+            collective_id=8, has_side_effects=True, vmem_limit_bytes=32 * 2**20
+        ),
+        name="gather_weights",
+    )(blocks)
+
+
+def rows_body(
+    his, far, near, whole, start, far_a, far_b, got, looked, local_sem, y_sems, y_sems_in, seq_sems, seq_sems_in,
+    a_sems, a_sems_in, b_sems, b_sems_in
+):
+    core = Core(his)
+    dp, s = lax.axis_index("dp"), lax.axis_index("seq")
+    y, seqs = dp // 2, 2 * his
+    core.ids["y"] = (dp + 2 - 4 * y, s)
+    for i in range(1, seqs):
+        core.ids[f"seq{i}"] = (dp, lax.rem(s + i, seqs))
+    core.meet("y", "lo", *(f"seq{i}" for i in range(1, seqs)))
+    over, spread, carried = [], [], []
+    for i in range(seqs):
+        to = lax.rem(s + i, seqs)
+        over.append(core.copy(far.at[to], got.at[to], (y_sems, y_sems_in), i, "y"))
+        over[i].start()
+    for h in range(his):
+        carried.append(
+            core.copy(whole.at[y, 0, h, 1 - core.lo], far_a.at[h], (a_sems, a_sems_in), h, "y")
+        )
+        carried.append(
+            core.copy(whole.at[1 - y, 1, h, core.lo], far_b.at[h], (b_sems, b_sems_in), h, "lo")
+        )
+    for copy in carried:
+        copy.start()
+    here = None
+    for i in [*range(1, seqs), 0]:
+        to = lax.rem(s + i, seqs)
+        over[i].wait_recv()
+
+        def add(at, to=to):
+            looked[to, at, :] = near[to, at, :] + got[to, at, :]
+
+        by_rows(near.shape[1], add)
+        if i:
+            spread.append(
+                core.copy(looked.at[to], start.at[s], (seq_sems, seq_sems_in), i - 1, f"seq{i}")
+            )
+            spread[-1].start()
+        else:
+            here = pltpu.make_async_copy(looked.at[s], start.at[s], local_sem)
+            here.start()
+    for copy in spread + carried:
+        copy.wait_recv()
+    here.wait()
+    sent(over + spread + carried)
+
+
+def gather_rows(his, far, near, whole):
+    seqs = 2 * his
+    rows, columns = far.shape[0] // seqs, far.shape[1]
+    far, near = (part.reshape(seqs, rows, columns) for part in (far, near))
+    dma = pltpu.SemaphoreType.DMA
+    start, far_a, far_b = pallas.pallas_call(
+        functools.partial(rows_body, his),
+        out_shape=(
+            jax.ShapeDtypeStruct((seqs, rows, columns), low),
+            *[jax.ShapeDtypeStruct((his, *whole.shape[4:]), low)] * 2,
+        ),
+        in_specs=[pallas.BlockSpec(memory_space=pltpu.VMEM)] * 2
+        + [pallas.BlockSpec(memory_space=pallas.ANY)],
+        out_specs=(pallas.BlockSpec(memory_space=pallas.ANY),) * 3,
+        scratch_shapes=[
+            pltpu.VMEM((seqs, rows, columns), low),
+            pltpu.VMEM((seqs, rows, columns), low),
+            dma,
+            *[dma((count,)) for count in (seqs, seqs, seqs - 1, seqs - 1, his, his, his, his)],
+        ],
+        cost_estimate=SMALL,
+        compiler_params=pltpu.CompilerParams(
+            collective_id=11, has_side_effects=True, vmem_limit_bytes=32 * 2**20
+        ),
+        name="gather_rows",
+    )(far, near, whole)
+    start = jnp.transpose(start, (1, 0, 2)).reshape(rows, seqs * columns).astype(full)
+    return start, far_a, far_b
 
 
 def sum_body(his, rows, packed, out, bufs, got, send_sems, recv_sems):
@@ -770,60 +1110,50 @@
     def swap_rows(rows, **way):
         return pl.send(rows.astype(low), **way)
 
-    mlp_got = line_parts(pl, split_columns(mlp_w, line))
+    mlp_whole = gather_weights(his, split_columns(mlp_w, line))
     ids = jnp.concatenate([tok_ids.reshape(seqs, tokens), targets.reshape(seqs, picks)], 1)
     ids = ids.reshape(seqs * (tokens + picks))
-    ids_all = jnp.stack(
-        [
-            jnp.stack([ids, pl.send(ids, dc=1)]),
-            jnp.stack([pl.send(ids, dy=1), pl.send(ids, dy=1, dc=1)]),
-        ]
-    )
-    local = ids_all - pl.dp * emb_n
-    local = jnp.where((local >= 0) & (local < emb_n), local, emb_n)
-
-    def look(dy, dc, *work):
-        at = after(local[dy, dc], *work)
-        rows = jnp.take(emb, jnp.minimum(at, emb_n - 1), axis=0, mode="clip")
-        return jnp.where((at < emb_n)[:, None], rows, 0.0).astype(low)
-
-    far_other = look(1, 1)
+    def look(wanted, *work):
+        at = after(wanted, *work) - pl.dp * emb_n
+        rows = jnp.take(emb, jnp.clip(at, 0, emb_n - 1), axis=0, mode="clip")
+        return jnp.where(((at >= 0) & (at < emb_n))[:, None], rows, 0.0).astype(low)
+
+    ids_y = pl.send(ids, dy=1)
+    ids_c, ids_yc = pl.send(ids, dc=1), pl.send(ids, dy=1, dc=1)
+    near_own = look(ids, mlp_whole)
+    ids_c, ids_y, ids_yc = after((ids_c, ids_y, ids_yc), near_own)
+    far_other = look(ids_yc)
     far_got = pl.send(far_other, dc=1)
-    far_own = look(1, 0, far_other)
-    near_other = look(0, 1, far_own)
+    near_other = look(ids_c, far_other)
     near_got = pl.send(near_other, dc=1)
-    far_sum = far_own + after(far_got, near_other)
-    across = pl.send(far_sum, dy=1)
-
-    first_block = jnp.concatenate(
-        [attn_w[:, :QKV], jnp.pad(gains.T, ((0, 0), (0, 125)))], 1
+    far_own = look(ids_y, near_other)
+    far_sum = far_own + after(far_got, far_own)
+    near_sum = near_own + after(near_got, far_own)
+
+    kv_block = jnp.concatenate(
+        [attn_w[:, D:QKV], jnp.pad(gains.T, ((0, 0), (0, 125)))], 1
     ).astype(low)
-    qkv_full = lax.all_gather(first_block, ("dp", "seq"), axis=0, tiled=True)
-    gain_float = qkv_full[:, QKV : QKV + 3].astype(full).T
-    out_full = lax.all_gather(
-        attn_w[:, QKV:].astype(low), ("dp", "seq"), axis=0, tiled=True
-    )
-    near_own = look(0, 0, far_sum)
-    near_sum = near_own + after(near_got, near_own)
-    head_low = after(head, near_sum).astype(low)
-    emb_square_sum = jnp.sum(after(emb, head_low) ** 2)
-    looked = near_sum + after(across, emb_square_sum)
-    mlp_line = line_place(pl, after(mlp_got, looked)).reshape(2, his, block, wide)
-    mlp_x, mlp_y = pl.send(mlp_line, dlo=1), pl.send(mlp_line, dy=1)
-    start = lax.all_to_all(looked, "seq", split_axis=0, concat_axis=1, tiled=True).astype(full)
+    kv_full = lax.all_gather(kv_block, ("dp", "seq"), axis=0, tiled=True)
+    gain_float = kv_full[:, 2 * kv_width : 2 * kv_width + 3].astype(full).T
+    kv_full = kv_full[:, : 2 * kv_width]
+    rest_low = after(attn_w, mlp_whole).astype(low)
+    rest_full = lax.all_gather(
+        jnp.concatenate([rest_low[:, :D], rest_low[:, QKV:]], 1), ("dp", "seq"), axis=0, tiled=True
+    )
+    query_full, out_full = rest_full[:, :D], rest_full[:, D:]
+    start, far_a, far_b = gather_rows(his, far_sum, near_sum, mlp_whole)
+    head_low = after(head, start).astype(low)
+    emb_square_sum = jnp.sum(after(emb, start) ** 2)
 
     token_pos = pl.s * tokens + jnp.arange(tokens, dtype=jnp.int32)
     pick_pos = lax.dynamic_slice_in_dim(positions[0], pl.s * picks, picks)
     token_tables = turn_tables(*yarn_tables(token_pos.astype(full)))
     pick_tables = turn_tables(*yarn_tables(pick_pos.astype(full)))
-    start, token_tables, pick_tables, mlp_line = lax.optimization_barrier(
-        (start, token_tables, pick_tables, mlp_line)
-    )
     head_rows = lax.all_gather(after(head_low, start), "dp", axis=1, tiled=True)
     normed = rms_norm(start, gain_float[0]).astype(low)
     normed_tok, normed_pick = normed[:tokens], normed[tokens:]
     start_pick = start[tokens:]
-    projected = matmul(normed_tok, qkv_full[:, D:QKV])
+    projected = matmul(normed_tok, kv_full)
     (kv_all,) = move(
         functools.partial(keys_body, his),
         0,
@@ -831,50 +1161,37 @@
         [projected, *token_tables],
         his,
         own=(tokens, 2 * kv_width),
-        gathers=True,
+        gathers=1,
     )
     kv_all = kv_all.reshape(seqs * tokens, 2 * kv_width)
-    raw = matmul(normed_pick, qkv_full[:, :D])
-    mlp_x, mlp_y = after((mlp_x, mlp_y), kv_all)
-    mlp_far = (pl.send(mlp_x[0], dy=1), pl.send(mlp_y[1], dlo=1))
-    pick_line = line_gather(pl, after(normed_pick, kv_all))
-    queries, attended_low, attended, log_total = attend_rows(
-        after(raw, mlp_x, mlp_y), pick_tables, pick_pos, kv_all
-    )
+    raw = matmul(normed_pick, query_full)
+    queries, attended_low, attended, log_total, pick_line = attend_rows(
+        his, raw, pick_tables, pick_pos, kv_all, normed_pick
+    )
+    for c, block_far in enumerate((far_a, far_b)):
+        mlp_whole = lax.dynamic_update_slice(
+            mlp_whole, block_far[None, None, :, None], (1 - pl.y, c, 0, 1 - pl.lo, 0, 0)
+        )
+    mlp_full = mlp_whole.reshape(D, wide)
 
     def shares(rows):
-        rows = jnp.transpose(rows.reshape(picks, line, D // line), (1, 0, 2))
-        return jnp.concatenate(line_parts(pl, rows), 0)
-
-    attended_share = shares(attended_low)
+        return jnp.transpose(rows.reshape(picks, line, D // line), (1, 0, 2))
+
     middle = start_pick + matmul_nt(attended_low, out_full)
-    mlp_full = jnp.zeros((2, 2, his, 2, block, wide), low)
-    for held, at_y, at_lo in (
-        (after(mlp_line, middle), pl.y, pl.lo),
-        (mlp_x, pl.y, 1 - pl.lo),
-        (mlp_y, 1 - pl.y, pl.lo),
-    ):
-        mlp_full = lax.dynamic_update_slice(
-            mlp_full, held[None, :, :, None], (at_y, 0, 0, at_lo, 0, 0)
-        )
-    (normed_two,) = move(
+    normed_two, attended_share = move(
         functools.partial(norm_gather_body, his),
         1,
-        [((his, 2, picks, D), low, pallas.ANY)],
-        [middle, gain_float[1:2]],
+        [
+            ((his, 2, picks, D), low, pallas.ANY),
+            ((line, picks, D // line), low, pltpu.VMEM),
+        ],
+        [middle, gain_float[1:2], shares(attended_low)],
         his,
         own=(picks, D),
-        gathers=True,
+        gathers=1,
+        swap=(his, picks, D // line),
     )
     normed_two = normed_two.reshape(line * picks, D)
-
-    mlp_far = after(mlp_far, normed_two)
-    for at_c in range(2):
-        mlp_full = lax.dynamic_update_slice(
-            mlp_full, mlp_far[at_c][None, None, :, None], (1 - pl.y, at_c, 0, 1 - pl.lo, 0, 0)
-        )
-    mlp_full = mlp_full.reshape(D, wide)
-
     gate_up = matmul(normed_two, mlp_full[:, : 2 * part])
     gate = gate_up[:, :part]
     upward = gate_up[:, part:]
@@ -888,7 +1205,7 @@
         his,
         scatter=(picks, D),
         own=(picks, D),
-        gathers=True,
+        gathers=1,
     )
     chosen = chosen.reshape(seqs * picks, D)
     logits = matmul_nt(chosen, head_rows)
@@ -934,7 +1251,7 @@
         his,
         scatter=(picks, D),
         own=(picks, D),
-        gathers=True,
+        gathers=1,
     )
     branch_grad = branch_grad.reshape(line * picks, D)
     mixed_grad = matmul(branch_grad, mlp_full[:, 2 * part :])
@@ -962,24 +1279,41 @@
         his,
         scatter=(picks, D),
     )
-    branch_line = line_gather(pl, attn_branch_grad)
     attended_grad = matmul(attn_branch_grad, out_full).astype(low)
-    query_raw, kv_part = attend_rows_back(
-        attended_grad, pick_tables, pick_pos, kv_all, queries, attended, log_total
-    )
-    query_share = shares(query_raw)
-    (kv_raw,) = move(
+    query_raw, kv_part, branch_line = attend_rows_back(
+        his,
+        attended_grad,
+        pick_tables,
+        pick_pos,
+        kv_all,
+        queries,
+        attended,
+        log_total,
+        attn_branch_grad,
+    )
+    mlp_keep, mlp_sends = cross_next(pl, mlp_state, kv_part)
+    kv_part = after(kv_part, mlp_keep, mlp_sends)
+    kv_raw, query_share = move(
         functools.partial(keys_back_body, his),
         5,
-        [((tokens, 2 * kv_width), low, pltpu.VMEM)],
-        [kv_part.reshape(his, 2, tokens, 2 * kv_width), *token_tables],
+        [
+            ((tokens, 2 * kv_width), low, pltpu.VMEM),
+            ((line, picks, D // line), low, pltpu.VMEM),
+        ],
+        [
+            kv_part.reshape(his, 2, tokens, 2 * kv_width),
+            *token_tables,
+            shares(query_raw),
+        ],
         his,
+        swap=(his, picks, D // line),
         scatter=(tokens, 2 * kv_width),
         own=(tokens, 2 * kv_width),
         own_type=full,
     )
-    pick_up = matmul_nt(query_raw, qkv_full[:, :D])
-    tok_up = matmul_nt(kv_raw, qkv_full[:, D:QKV])
+    mlp_state = cross_send(pl, mlp_keep, after(mlp_sends, kv_raw))
+    pick_up = matmul_nt(query_raw, query_full)
+    tok_up = matmul_nt(kv_raw, kv_full)
     start_part, start_gain_grad = norm_back(
         start, gain_float[0], jnp.concatenate([tok_up, pick_up], 0)
     )
@@ -988,9 +1322,16 @@
     ).astype(low)
 
     back_rows = lax.all_to_all(start_grad, "seq", split_axis=1, concat_axis=0, tiled=True)
-    branch_line, pick_line, query_share = after((branch_line, pick_line, query_share), start_grad)
+    branch_line, pick_line = after((branch_line, pick_line), start_grad)
+    branch_line, pick_line = (
+        part.reshape(line * picks, D) for part in (branch_line, pick_line)
+    )
     query_term = jnp.concatenate(
-        [matmul_tn(pick_line, query_share), matmul_tn(branch_line, attended_share)], 1
+        [
+            matmul_tn(pick_line, query_share.reshape(line * picks, D // line)),
+            matmul_tn(branch_line, attended_share.reshape(line * picks, D // line)),
+        ],
+        1,
     )
     query_term = query_term.astype(low).reshape(2, 2, his, 2, block, query_term.shape[-1])
     query_state = cross_start(pl, query_term)
@@ -1015,69 +1356,67 @@
     token_got = pl.send(token_term(1 - pl.c).astype(low), dc=1)
     token_keep = token_term(pl.c)
     other_squares = [jnp.sum(after(w, token_keep) ** 2) for w in (attn_w, mlp_w, head)]
-    mlp_state = cross_next(pl, mlp_state, other_squares)
-    back_rows = after(back_rows, mlp_state[:2], query_term)
-    back_got = pl.send(back_rows, dy=1)
-    token_sum = grid(token_keep + after(token_got, back_rows).astype(full))
-    token_got = pl.send(pick(token_sum, 1 - pl.y, 0), dy=1)
-
-    other = ids_all[:, 0] - (pl.dp ^ 1) * emb_n
-    places_in = jnp.where(
-        local[:, 0] < emb_n,
-        local[:, 0],
-        jnp.where((other >= 0) & (other < emb_n), other + emb_n, 2 * emb_n),
-    )
-    chip_grad = (
-        jnp.zeros((2 * emb_n + 8, emb_m), full)
-        .at[places_in[0]]
-        .add(after(back_rows, token_sum).astype(full))
-    )
-    mlp_term = cross_end(pl, mlp_state, chip_grad)
-    mlp_got = line_parts(pl, mlp_term)
-    query_state = cross_next(pl, query_state, chip_grad)
-    token_sum = pick(token_sum, pl.y, 0).astype(full) + after(token_got, chip_grad).astype(full)
-    token_got = pl.send(pick(token_sum, 1 - pl.lo, 1).astype(low), dlo=1)
-    back_got = after(back_got, mlp_term, query_state[:2], token_sum)
-    chip_grad = chip_grad.at[places_in[1]].add(back_got.astype(full))
-    emb_part = chip_grad[emb_n : 2 * emb_n].astype(low)
-    emb_got = pl.send(emb_part, dc=1)
-    query_term = cross_end(pl, query_state, emb_part)
-    query_got = line_parts(pl, query_term)
-    token_sum = pick(token_sum, pl.lo, 1) + after(token_got, emb_part).astype(full)
-    token_parts = hi_sum_start(pl, token_sum)
-    head_grad = after(head_grad, emb_part).astype(full)
-    head_square = head_grad * head_grad + eps_square
-    head_rows_sum = jnp.sum(head_square, 1)
-    head_cols_sum = jnp.sum(head_square, 0)
-    emb_grad = chip_grad[:emb_n] + after(emb_got, head_rows_sum).astype(full)
-    emb_square = emb_grad * emb_grad + eps_square
-    emb_rows = jnp.sum(emb_square, 1)
-    mlp_grad, mlp_rows, mlp_cols = join_columns(line_place(pl, after(mlp_got, emb_rows)))
-    mlp_row_new = decay_rate * mlp_row + (1.0 - decay_rate) * mlp_rows / (3 * FF)
-    token_sum = hi_sum_end(token_parts, mlp_cols)
-    query_all = line_place(pl, after(query_got, mlp_cols)).reshape(line, block, 2, D // line)
-    query_all = jnp.transpose(query_all, (1, 2, 0, 3)).reshape(block, 2 * D).astype(full)
-    attn_grad = jnp.concatenate(
-        [query_all[:, :D], token_sum[:, : 2 * kv_width], query_all[:, D:]], 1
-    )
-    gains_grad = token_sum[:, 2 * kv_width : 2 * kv_width + 3].T
-    attn_square = attn_grad * attn_grad + eps_square
-    attn_row_new = decay_rate * attn_row + (1.0 - decay_rate) * jnp.mean(attn_square, 1)
-    attn_weight_square, mlp_weight_square, head_weight_square = other_squares
-    scalars = [
+    early = [
         loss_part,
-        jnp.sum(attn_row_new),
+        jnp.sum(attn_row),
         *other_squares,
         jnp.where(pl.s == 0, jnp.sum(emb_row), 0.0),
         emb_square_sum,
         jnp.where(pl.dp == 0, jnp.sum(head_row), 0.0),
         jnp.sum(gains * gains),
-        jnp.sum(emb_rows),
-        jnp.sum(mlp_row_new),
-        jnp.sum(head_rows_sum),
+        jnp.sum(mlp_row),
     ]
     slot = jnp.arange(128, dtype=jnp.int32)
-    scalars = sum(jnp.where(slot == i, value, 0.0) for i, value in enumerate(scalars))
+    early = sum(jnp.where(slot == i, value, 0.0) for i, value in enumerate(early))
+    mlp_term = cross_end(pl, mlp_state, early)
+    mlp_here, mlp_came = line_pairs(pl, mlp_term)
+    back_rows, early = lax.optimization_barrier((back_rows, early, mlp_term, query_term))[:2]
+    back_got = pl.send(back_rows, dy=1)
+    token_sum = grid(token_keep + after(token_got, back_rows).astype(full))
+    token_got = pl.send(pick(token_sum, 1 - pl.y, 0), dy=1)
+
+    def on_chip(wanted):
+        local, other = wanted - pl.dp * emb_n, wanted - (pl.dp ^ 1) * emb_n
+        return jnp.where(
+            (local >= 0) & (local < emb_n),
+            local,
+            jnp.where((other >= 0) & (other < emb_n), other + emb_n, 2 * emb_n),
+        )
+
+    places_in = on_chip(ids), on_chip(ids_y)
+    chip_grad = (
+        jnp.zeros((2 * emb_n + 8, emb_m), full)
+        .at[places_in[0]]
+        .add(after(back_rows, token_sum, mlp_came).astype(full))
+    )
+    mlp_got = line_sends(pl, mlp_here, after(mlp_came, token_sum))
+    near, far = mlp_got[1:2] + mlp_got[-1:], mlp_got[2:-1]
+    query_state = cross_send(pl, *cross_next(pl, query_state, chip_grad))
+    head_grad = after(head_grad, query_state[:2], near[0]).astype(full)
+    head_square = head_grad * head_grad + eps_square
+    head_rows_sum = jnp.sum(head_square, 1)
+    head_cols_sum = jnp.sum(head_square, 0)
+    back_got = after(back_got, near[1:], head_rows_sum, head_cols_sum)
+    chip_grad = chip_grad.at[places_in[1]].add(back_got.astype(full))
+    token_sum = pick(token_sum, pl.y, 0).astype(full) + after(token_got, chip_grad).astype(full)
+    token_got = pl.send(pick(token_sum, 1 - pl.lo, 1).astype(low), dlo=1)
+    emb_part = after(chip_grad, far, token_sum)[emb_n : 2 * emb_n].astype(low)
+    emb_got = pl.send(emb_part, dc=1)
+    query_term = cross_end(pl, query_state, emb_part)
+    token_sum = pick(token_sum, pl.lo, 1) + after(token_got, emb_part).astype(full)
+    mlp_grad, mlp_rows, mlp_cols = join_columns(line_place(pl, after(mlp_got, query_term)))
+    mlp_row_new = decay_rate * mlp_row + (1.0 - decay_rate) * mlp_rows / (3 * FF)
+    emb_grad = chip_grad[:emb_n] + after(emb_got, query_term, token_sum).astype(full)
+    emb_square = emb_grad * emb_grad + eps_square
+    emb_rows, emb_cols = jnp.sum(emb_square, 1), jnp.sum(emb_square, 0)
+    attn_grad, gains_grad, attn_rows, attn_cols = layer_gradient(
+        his, after(query_term, emb_rows), token_sum
+    )
+    gains_grad = gains_grad[:, :3].T
+    attn_row_new = decay_rate * attn_row + (1.0 - decay_rate) * attn_rows[:, 0] / (QKV + D)
+    scalars = early
+    for at, value in ((10, emb_cols), (11, head_cols_sum)):
+        scalars = scalars + jnp.where(slot == at, jnp.sum(value), 0.0)
     (
         emb_row_sum,
         head_col_sum,
@@ -1089,22 +1428,24 @@
     ) = sum_statistics(
         his,
         (emb_rows, head_cols_sum),
-        (jnp.sum(attn_square, 0), mlp_cols, scalars),
-        (head_rows_sum, jnp.sum(emb_square, 0)),
-    )
-    mlp_row_total, head_row_total = totals[10], totals[11]
+        (attn_cols[0], mlp_cols, scalars),
+        (head_rows_sum, emb_cols),
+    )
+    attn_row_total = decay_rate * totals[1] + (1.0 - decay_rate) * jnp.sum(attn_cols_sum) / (QKV + D)
+    mlp_row_total = decay_rate * totals[9] + (1.0 - decay_rate) * jnp.sum(mlp_cols_sum) / (3 * FF)
+    emb_row_total, head_row_total = totals[10], totals[11]
 
     attn_col_new = decay_rate * attn_col + (1.0 - decay_rate) * attn_cols_sum / D
     mlp_col_new = decay_rate * mlp_col + (1.0 - decay_rate) * mlp_cols_sum / D
     attn_update = attn_grad * lax.rsqrt(
-        attn_row_new[:, None] * attn_col_new[None, :] / (totals[1] / D)
+        attn_row_new[:, None] * attn_col_new[None, :] / (attn_row_total / D)
     )
     mlp_update = mlp_grad * lax.rsqrt(
         mlp_row_new[:, None] * mlp_col_new[None, :] / (mlp_row_total / D)
     )
     emb_row_new = decay_rate * emb_row + (1.0 - decay_rate) * emb_row_sum / D
     emb_col_new = decay_rate * emb_col + (1.0 - decay_rate) * emb_col_sum / VOCAB
-    emb_mean = (decay_rate * totals[5] + (1.0 - decay_rate) * totals[9] / D) / VOCAB
+    emb_mean = (decay_rate * totals[5] + (1.0 - decay_rate) * emb_row_total / D) / VOCAB
     emb_update = emb_grad * lax.rsqrt(emb_row_new[:, None] * emb_col_new[None, :] / emb_mean)
     head_row_new = decay_rate * head_row + (1.0 - decay_rate) * head_row_sum / D
     head_col_new = decay_rate * head_col + (1.0 - decay_rate) * head_col_sum / VOCAB

time: 1090 us -> 1040 us (0.954)
  Pallas kernels: 338 us -> 530 us
  waiting for transfers between devices: 167 us -> 32.2 us
  starting transfers between devices: 105 us -> 32 us
  local copies, waits for them, and re-layouts: 145 us -> 128 us
  other arithmetic: 197 us -> 185 us
    pallas_call x2 -> x6, Pallas kernels: 36.1 us -> 259 us  [the longest x1 104 us: gather_rows(): pallas.pallas_call(functools.partial(rows_body, his), out_shape=(jax.Shap...]
    ppermute x70 -> x23, waiting for transfers between devices: 154 us -> 29.1 us  [send(): return lax.ppermute(value, ('dp', 'seq'), pairs)]
    ppermute x70 -> x23, starting transfers between devices: 93.4 us -> 25.6 us  [send(): return lax.ppermute(value, ('dp', 'seq'), pairs)]
    pallas_call x6, Pallas kernels: 276 us -> 245 us  [move(): pallas.pallas_call(body, out_shape=tuple((jax.ShapeDtypeStruct(shape, dty...]
    dynamic_update_slice x29 -> x2, local copies, waits for them, and re-layouts: 24.9 us -> 3.53 us  [on_device(): lax.dynamic_update_slice(mlp_whole, block_far[None, None, :, None], (1 -...]
    all_to_all x1 -> x0, waiting for transfers between devices: 11 us -> none  [on_device(): lax.all_to_all(looked, 'seq', split_axis=0, concat_axis=1, tiled=True)]
    unnamed x214 -> x196, local copies, waits for them, and re-layouts: 25.7 us -> 34.4 us
    reduce_sum x5 -> x7, other arithmetic: 24.4 us -> 26.7 us  [the longest x1 8.35 us: on_device(): scalars = scalars + jnp.where(slot == at, jnp.sum(value), 0.0)]
  transfers between devices with their start and end apart: 78 -> 30, of which waited for: 27 -> 6; matrix products, arithmetic and copies ran while one was open for 29% -> 26% of each run, Pallas kernels for 24% -> 41%
where the time goes in v3:
time: 1040 us; the launch traced here: 1030 us
  Pallas kernels  530 us (51%)
  other arithmetic  185 us (18%)
  local copies, waits for them, and re-layouts  128 us (12%)
  matrix products  98.8 us (10%)
  waiting for transfers between devices  32.2 us (3%)
  starting transfers between devices  32 us (3%)
  between operations  26.7 us (3%)
    pallas_call x6, Pallas kernels, move(): pallas.pallas_call(body, out_shape=tuple((jax.ShapeDtypeStruct(shape, dty...  245 us
    pallas_call x1, Pallas kernels, gather_rows(): pallas.pallas_call(functools.partial(rows_body, his), out_shape=(jax.Shap...  104 us
    pallas_call x1, Pallas kernels, gather_weights(): pallas.pallas_call(functools.partial(weights_body, his), out_shape=jax.Sh...  71.4 us
    gather x4, local copies, waits for them, and re-layouts, look(): rows = jnp.take(emb, jnp.clip(at, 0, emb_n - 1), axis=0, mode='clip')  36.5 us
    dot_general x6, matrix products, matmul_nt(): lax.dot_general(left, right, (((1,), (1,)), ((), ())), preferred_element_...  36.3 us
    dot_general x6, matrix products, matmul(): return jnp.dot(left, right, preferred_element_type=jnp.float32)  35 us
    unnamed x196, local copies, waits for them, and re-layouts  34.4 us
    ppermute x23, waiting for transfers between devices, send(): return lax.ppermute(value, ('dp', 'seq'), pairs)  29.1 us
  transfers between devices with their start and end apart: 30, of which 6 were waited for; matrix products, arithmetic and copies ran while one was open for 26% of the time, Pallas kernels for 41%

profile of v3, /device:TPU:0, one launch (start us, length us, event | category | flops | bytes accessed | tf_op | source)
XLA Modules:
  0.0 1032.7 jit_solution(4361530171442548607)
XLA Ops:
  13.0 71.4 %gather_weights.1.whole = bf16[2,2,4,2,64,2112]{5,4,3,2,1,0:T(8,128)(2,1)S(1)} custom-call(bf16[8,64,2112]{2,1,0:T(8,128)(2,1)S(1)} %split_columns.1.blocks), custom_call_target="tpu_custom_call" | custom-call | flops 1024 | bytes 1024 | tf_op jit(solution)/shard_map/gather_weights/pallas_call | solution.py:915
  92.9 9.1 gather_fusion
  102.0 9.1 gather_fusion.1
  113.6 9.3 gather_fusion.2
  125.3 9.1 gather_fusion.3
  143.0 104.1 %gather_rows.1 = (bf16[8,320,256]{2,1,0:T(8,128)(2,1)S(1)}, bf16[4,64,2112]{2,1,0:T(8,128)(2,1)S(1)}, bf16[4,64,2112]{2,1,0:T(8,128)(2,1)S(1)}) custom-call(bf16[8,320,256]{2,1,0:T(8,128)(2,1)S(1)} %bitcast.296, bf16[8,320,256]{2,1,0:T(8,128)(2,1)S(1)} %bitcast.297, bf16[2,2,4,2,64,2112]{5,4,3,2,1,0:T(8,128)(2,1)S(1)} %copy-done.2), custom_call_target="tpu_custom_call" | custom-call | flops 1024 | bytes 1024 | tf_op jit(solution)/shard_map/gather_rows/pallas_call | solution.py:986
  267.9 28.1 %shard_map.337 = bf16[4,2,256,512]{3,2,1,0:T(8,128)(2,1)S(1)} custom-call(f32[256,512]{1,0:T(8,128)S(1)} %fusion.50.projected, f32[256,128]{1,0:T(8,128)S(1)} %get-tuple-element.370.cosine, f32[256,128]{1,0:T(8,128)S(1)} %get-tuple-element.371.sine), custom_call_target="tpu_custom_call" | custom-call | flops 1024 | bytes 1024 | tf_op jit(solution)/shard_map/pallas_call | solution.py:667
  304.0 24.6 %attend.1 = (bf16[8,256,64]{2,1,0:T(8,128)(2,1)}, bf16[64,2048]{1,0:T(8,128)(2,1)}, f32[8,256,64]{2,1,0:T(8,128)}, f32[8,256,128]{2,1,0:T(8,128)}, bf16[2,4,64,2048]{3,2,1,0:T(8,128)(2,1)}) custom-call(f32[64,2048]{1,0:T(8,128)} %fusion.12.raw, f32[64,128]{1,0:T(8,128)} %get-tuple-element.368.cosine, f32[64,128]{1,0:T(8,128)} %get-tuple-element.369.sine, ...), custom_call_target="tpu_custom_call" | custom-call | flops 1024 | bytes 1024 | tf_op jit(solution)/shard_map/attend/pallas_call | solution.py:764
  335.9 37.5 %shard_map.338 = (bf16[4,2,64,2048]{3,2,1,0:T(8,128)(2,1)S(1)}, bf16[8,64,256]{2,1,0:T(8,128)(2,1)S(1)}) custom-call(f32[64,2048]{1,0:T(8,128)S(1)} %fusion.42.values.middle, f32[1,2048]{1,0:T(1,128)S(1)} %get-tuple-element.338.gain, bf16[8,64,256]{2,1,0:T(8,128)(2,1)S(1)} %bitcast.304), custom_call_target="tpu_custom_call" | custom-call | flops 1024 | bytes 1024 | tf_op jit(solution)/shard_map/pallas_call | solution.py:667
  381.2 55.0 %shard_map.339 = (f32[64,2048]{1,0:T(8,128)S(1)}, bf16[4,2,64,2048]{3,2,1,0:T(8,128)(2,1)S(1)}) custom-call(f32[4,2,64,2048]{3,2,1,0:T(8,128)} %bitcast.333, f32[64,2048]{1,0:T(8,128)S(1)} %fusion.42.values.middle, f32[1,2048]{1,0:T(1,128)S(1)} %get-tuple-element.337.gain), custom_call_target="tpu_custom_call" | custom-call | flops 1024 | bytes 1024 | tf_op jit(solution)/shard_map/pallas_call | solution.py:667
  437.5 12.6 %fusion.118 = (f32[512]{0:T(512)S(1)}, f32[512,4000]{0,1:T(8,128)S(1)}) fusion(bf16[512,2048]{1,0:T(8,128)(2,1)} %bitcast.309, bf16[4000,2048]{1,0:T(8,128)(2,1)} %all-gather.8.cloned.1.call-done), kind=kOutput, calls=%fused_computation.329 | convolution fusion | flops 8390655488 | bytes 26675200 | tf_op jit(solution)/shard_map/dot_general | solution.py:78
  472.3 15.2 %fusion.119 = f32[512,2048]{1,0:T(8,128)} fusion(bf16[512,4000]{0,1:T(8,128)(2,1)S(1)} %fusion.5, bf16[4000,2048]{1,0:T(8,128)(2,1)} %all-gather.8.cloned.1.call-done), kind=kOutput, calls=%fused_computation.330 | convolution fusion | flops 8388608000 | bytes 24674304 | tf_op jit(solution)/shard_map/dot_general | solution.py:74
  487.5 58.1 %shard_map.340 = (f32[64,2048]{1,0:T(8,128)S(1)}, f32[1,2048]{1,0:T(1,128)S(1)}, bf16[4,2,64,2048]{3,2,1,0:T(8,128)(2,1)S(1)}) custom-call(f32[4,2,64,2048]{3,2,1,0:T(8,128)} %bitcast.332, f32[64,2048]{1,0:T(8,128)S(1)} %get-tuple-element.116.ending, f32[1,2048]{1,0:T(1,128)S(1)} %get-tuple-element.337.gain), custom_call_target="tpu_custom_call" | custom-call | flops 1024 | bytes 1024 | tf_op jit(solution)/shard_map/pallas_call | solution.py:667
  570.9 11.5 %convolution_convert_fusion = bf16[4000,2048]{1,0:T(8,128)(2,1)} fusion(bf16[512,4000]{0,1:T(8,128)(2,1)S(1)} %copy-done.31, bf16[512,2048]{1,0:T(8,128)(2,1)S(1)} %bitcast.310), kind=kOutput, calls=%fused_computation.6 | convolution fusion | flops 8396800000 | bytes 22577152 | tf_op jit(solution)/shard_map/dot_general | solution.py:84
  611.4 27.1 %shard_map.341 = (f32[64,2048]{1,0:T(8,128)S(1)}, bf16[64,2048]{1,0:T(8,128)(2,1)S(1)}, f32[1,2048]{1,0:T(1,128)S(1)}) custom-call(f32[4,2,64,2048]{3,2,1,0:T(8,128)S(1)} %bitcast.298, f32[64,2048]{1,0:T(8,128)S(1)} %fusion.42.values.middle, f32[1,2048]{1,0:T(1,128)S(1)} %get-tuple-element.338.gain, f32[64,2048]{1,0:T(8,128)S(1)} %get-tuple-element.121.ending_grad), custom_call_target="tpu_custom_call" | custom-call | flops 1024 | bytes 1024 | tf_op jit(solution)/shard_map/pallas_call | solution.py:667
  644.4 26.8 %attend_back.1 = (bf16[64,2048]{1,0:T(8,128)(2,1)}, f32[2048,512]{1,0:T(8,128)}, bf16[2,4,64,2048]{3,2,1,0:T(8,128)(2,1)}) custom-call(bf16[64,2048]{1,0:T(8,128)(2,1)} %fusion.45.grad, f32[64,128]{1,0:T(8,128)} %get-tuple-element.368.cosine, f32[64,128]{1,0:T(8,128)} %get-tuple-element.369.sine, s32[64,1]{1,0:T(8,128)} %copy.168.places, ...), custom_call_target="tpu_custom_call" | custom-call | flops 1024 | bytes 1024 | tf_op jit(solution)/shard_map/attend_back/pallas_call | solution.py:837
  689.2 39.0 %shard_map.342 = (bf16[256,512]{1,0:T(8,128)(2,1)S(1)}, bf16[8,64,256]{2,1,0:T(8,128)(2,1)S(1)}) custom-call(f32[4,2,256,512]{3,2,1,0:T(8,128)S(1)} %bitcast.299, f32[256,128]{1,0:T(8,128)S(1)} %get-tuple-element.370.cosine, f32[256,128]{1,0:T(8,128)S(1)} %get-tuple-element.371.sine, bf16[8,64,256]{2,1,0:T(8,128)(2,1)S(1)} %bitcast.303), custom_call_target="tpu_custom_call" | custom-call | flops 1024 | bytes 1024 | tf_op jit(solution)/shard_map/pallas_call | solution.py:667
  787.6 11.3 %collective-permute-done.11 = bf16[4,64,2112]{2,1,0:T(8,128)(2,1)} collective-permute-done((bf16[4,64,2112]{2,1,0:T(8,128)(2,1)}, bf16[4,64,2112]{2,1,0:T(8,128)(2,1)}, u32[]{:S(2)}, u32[]{:S(2)}) %collective-permute-start.11) | collective-permute-done | bytes 1081376 | tf_op jit(solution)/shard_map/ppermute | solution.py:114
  824.1 20.1 %scatter_custom_fusion = f32[16008,256]{1,0:T(8,128)} fusion(s32[2560]{0:T(1024)} %fusion.87, f32[]{:T(128)} %constant.295.clone.1, bf16[2560,256]{1,0:T(8,128)(2,1)} %bitcast.50), kind=kCustom, calls=%fused_computation.14 | custom fusion | flops 1310720 | bytes 17703424 | tf_op jit(solution)/shard_map/scatter-add | solution.py:1390
  851.9 10.1 collective-permute-done.18.refs_1_
  870.4 26.3 %scatter_custom_fusion.1 = f32[16008,256]{1,0:T(8,128)} fusion(f32[16008,256]{1,0:T(8,128)} %scatter_custom_fusion, s32[2560]{0:T(1024)S(1)} %compare_select_fusion.2, bf16[2560,256]{1,0:T(8,128)(2,1)} %collective-permute-done.14), kind=kCustom, calls=%fused_computation.89 | custom fusion | flops 1310720 | bytes 17702912 | tf_op jit(solution)/shard_map/scatter-add | solution.py:1400
  937.5 28.8 %layer_gradient.1 = (f32[64,4608]{1,0:T(8,128)S(1)}, f32[64,128]{1,0:T(8,128)S(1)}, f32[64,1]{1,0:T(8,128)S(1)}, f32[1,4608]{1,0:T(1,128)S(1)}) custom-call(bf16[8,64,512]{2,1,0:T(8,128)(2,1)S(1)} %bitcast.302, f32[4,64,640]{2,1,0:T(8,128)S(1)} %bitcast_add_fusion.tokens), custom_call_target="tpu_custom_call" | custom-call | flops 1024 | bytes 1024 | tf_op jit(solution)/shard_map/layer_gradient/pallas_call | solution.py:574
  967.7 21.7 %sum_statistics.1 = f32[296,128]{1,0:T(8,128)S(1)} custom-call(f32[296,128]{1,0:T(8,128)S(1)} %constant_dynamic-update-slice_fusion.2.packed), custom_call_target="tpu_custom_call" | custom-call | tf_op jit(solution)/shard_map/sum_statistics/pallas_call | solution.py:1054
  1003.8 12.0 %multiply_subtract_fusion.1 = f32[8000,256]{1,0:T(8,128)} fusion(f32[8000,256]{1,0:T(8,128)} %param.22, f32[8000,256]{1,0:T(8,128)} %get-tuple-element.395, f32[]{:T(128)} %bitcast.109, f32[256]{0:T(256)S(1)} %bitcast_add_fusion.4, f32[8000]{0:T(1024)S(1)} %fusion.85, f32[]{:T(128)} %bitcast.106), kind=kLoop, calls=%fused_computation.23 | loop fusion | flops 10240000 | bytes 24609032 | tf_op jit(solution)/shard_map/sub | solution.py:90
  (449 shorter events, 328.3 us)
Async XLA Ops:
  7.2 254.9 %all-gather.4.cloned.1.call-start = ((), (), s32[]{:S(2)}) async-start(), calls=%async_computation.2 | async-start | bytes 2703360 | tf_op jit(solution)/shard_map/all_gather | solution.py:1136
  10.3 287.8 %all-gather.6.cloned.1.call-start = ((), (), s32[]{:S(2)}) async-start(), calls=%async_computation.3 | async-start | bytes 17301504 | tf_op jit(solution)/shard_map/all_gather | solution.py:1140
  88.9 348.6 %all-gather.8.cloned.1.call-start = ((), (), s32[]{:S(2)}) async-start(), calls=%async_computation.4 | async-start | bytes 20480000 | tf_op jit(solution)/shard_map/all_gather | solution.py:1152
  91.0 11.0 %collective-permute-start = (s32[2560]{0:T(1024)S(1)}, s32[2560]{0:T(1024)S(1)}, u32[]{:S(2)}, u32[]{:S(2)}) collective-permute-start(s32[2560]{0:T(1024)S(1)} %reshape.557), channel_id=1, source_target_pairs={{0,8},{1,9},{2,10},{3,11},{4,12},{5,13},{6,14},{7,15},{8,0},{9,1},... | collective-permute-start | bytes 30728 | tf_op jit(solution)/shard_map/ppermute | solution.py:114
  91.0 11.0 %collective-permute-start.1 = (s32[2560]{0:T(1024)S(1)}, s32[2560]{0:T(1024)S(1)}, u32[]{:S(2)}, u32[]{:S(2)}) collective-permute-start(s32[2560]{0:T(1024)S(1)} %reshape.557), channel_id=1, source_target_pairs={{0,16},{1,17},{2,18},{3,19},{4,20},{5,21},{6,22},{7,23},{8,24},{9,... | collective-permute-start | bytes 30728 | tf_op jit(solution)/shard_map/ppermute | solution.py:114
  92.4 9.5 collective-permute-start.2
  113.3 21.2 %collective-permute-start.3 = (bf16[2560,256]{1,0:T(8,128)(2,1)}, bf16[2560,256]{1,0:T(8,128)(2,1)}, u32[]{:S(2)}, u32[]{:S(2)}) collective-permute-start(bf16[2560,256]{1,0:T(8,128)(2,1)} %select_convert_fusion.2), channel_id=1, source_target_pairs={{0,8},{1,9},{2,10},{3,11},{4,12},{5,13},{6,14},{7,15},{8,0},{9,1},... | collective-permute-start | bytes 3932168 | tf_op jit(solution)/shard_map/ppermute | solution.py:114
  253.7 608.3 %reduce-scatter.2.cloned.1.call-start = ((), (), s32[]{:S(2)}) async-start(), calls=%async_computation.5 | async-start | bytes 20480000 | tf_op jit(solution)/shard_map/reduce_scatter | solution.py:1268
  590.1 89.9 %collective-permute-start.8 = (bf16[4,2,64,2112]{3,2,0,1:T(8,128)(2,1)}, bf16[4,2,64,2112]{3,2,0,1:T(8,128)(2,1)}, u32[]{:S(2)}, u32[]{:S(2)}) collective-permute-start(bf16[4,2,64,2112]{3,2,0,1:T(8,128)(2,1)} %bitcast.274), channel_id=1, source_target_pairs={{0,16},{1,17},{2,18},{3,19},{4,20},{5,21},{6,22},{7,23},{8,24},{9,... | collective-permute-start | bytes 6488072 | tf_op jit(solution)/shard_map/ppermute | solution.py:114
  592.6 87.4 %collective-permute-start.9 = (bf16[2,4,64,2112]{3,2,1,0:T(8,128)(2,1)}, bf16[2,4,64,2112]{3,2,1,0:T(8,128)(2,1)}, u32[]{:S(2)}, u32[]{:S(2)}) collective-permute-start(bf16[2,4,64,2112]{3,2,1,0:T(8,128)(2,1)} %dynamic-slice_bitcast_fusion.2), channel_id=1, source_target_pairs={{0,1},{1,0},{2,3},{3,2},{4,5},{5,4},{6,7},{7,6},{8,9},{9,8},{10,11... | collective-permute-start | bytes 6488072 | tf_op jit(solution)/shard_map/ppermute | solution.py:114
  755.9 59.0 %all-to-all-start = ((bf16[320,8,256]{2,0,1:T(8,128)(2,1)}), bf16[320,8,256]{2,0,1:T(8,128)(2,1)}, u32[]{:S(2)}, u32[]{:S(2)}) async-start(bf16[320,8,256]{2,0,1:T(8,128)(2,1)} %pad_maximum_fusion.4), calls=%async_computation | async-start | bytes 2621440 | tf_op jit(solution)/shard_map/all_to_all | solution.py:1324
  762.4 36.5 %collective-permute-start.11 = (bf16[4,64,2112]{2,1,0:T(8,128)(2,1)}, bf16[4,64,2112]{2,1,0:T(8,128)(2,1)}, u32[]{:S(2)}, u32[]{:S(2)}) collective-permute-start(bf16[4,64,2112]{2,1,0:T(8,128)(2,1)} %fusion.54), channel_id=1, source_target_pairs={{0,1},{1,0},{2,3},{3,2},{4,5},{5,4},{6,7},{7,6},{8,9},{9,8},{10,11... | collective-permute-start | bytes 3244040 | tf_op jit(solution)/shard_map/ppermute | solution.py:114
  764.5 34.4 %collective-permute-start.12 = (bf16[4,64,2112]{2,1,0:T(8,128)(2,1)}, bf16[4,64,2112]{2,1,0:T(8,128)(2,1)}, u32[]{:S(2)}, u32[]{:S(2)}) collective-permute-start(bf16[4,64,2112]{2,1,0:T(8,128)(2,1)} %fusion.55), channel_id=1, source_target_pairs={{0,16},{1,17},{2,18},{3,19},{4,20},{5,21},{6,22},{7,23},{8,24},{9,... | collective-permute-start | bytes 3244040 | tf_op jit(solution)/shard_map/ppermute | solution.py:114
  767.9 47.3 %collective-permute-start.10 = (bf16[1024,640]{0,1:T(8,128)(2,1)}, bf16[1024,640]{0,1:T(8,128)(2,1)}, u32[]{:S(2)}, u32[]{:S(2)}) collective-permute-start(bf16[1024,640]{0,1:T(8,128)(2,1)} %fusion.53), channel_id=1, source_target_pairs={{0,8},{1,9},{2,10},{3,11},{4,12},{5,13},{6,14},{7,15},{8,0},{9,1},... | collective-permute-start | bytes 3932168 | tf_op jit(solution)/shard_map/ppermute | solution.py:114
  804.3 13.4 %collective-permute-start.13 = (bf16[4,64,2112]{2,1,0:T(8,128)(2,1)}, bf16[4,64,2112]{2,1,0:T(8,128)(2,1)}, u32[]{:S(2)}, u32[]{:S(2)}) collective-permute-start(bf16[4,64,2112]{2,1,0:T(8,128)(2,1)} %get-tuple-element.309), channel_id=1, source_target_pairs={{0,8},{1,9},{2,10},{3,11},{4,12},{5,13},{6,14},{7,15},{8,0},{9,1},... | collective-permute-start | bytes 3244040 | tf_op jit(solution)/shard_map/ppermute | solution.py:114
  812.0 32.1 %collective-permute-start.16 = (bf16[4,2,64,512]{3,2,0,1:T(8,128)(2,1)}, bf16[4,2,64,512]{3,2,0,1:T(8,128)(2,1)}, u32[]{:S(2)}, u32[]{:S(2)}) collective-permute-start(bf16[4,2,64,512]{3,2,0,1:T(8,128)(2,1)} %bitcast.278), channel_id=1, source_target_pairs={{0,16},{1,17},{2,18},{3,19},{4,20},{5,21},{6,22},{7,23},{8,24},{9,... | collective-permute-start | bytes 1572872 | tf_op jit(solution)/shard_map/ppermute | solution.py:114
  814.6 29.6 %collective-permute-start.17 = (bf16[2,4,64,512]{3,2,1,0:T(8,128)(2,1)}, bf16[2,4,64,512]{3,2,1,0:T(8,128)(2,1)}, u32[]{:S(2)}, u32[]{:S(2)}) collective-permute-start(bf16[2,4,64,512]{3,2,1,0:T(8,128)(2,1)} %dynamic-slice_bitcast_fusion.5), channel_id=1, source_target_pairs={{0,1},{1,0},{2,3},{3,2},{4,5},{5,4},{6,7},{7,6},{8,9},{9,8},{10,11... | collective-permute-start | bytes 1572872 | tf_op jit(solution)/shard_map/ppermute | solution.py:114
  814.9 55.5 %collective-permute-start.14 = (bf16[2560,256]{1,0:T(8,128)(2,1)}, bf16[2560,256]{1,0:T(8,128)(2,1)}, u32[]{:S(2)}, u32[]{:S(2)}) collective-permute-start(bf16[2560,256]{1,0:T(8,128)(2,1)} %bitcast.50), channel_id=1, source_target_pairs={{0,16},{1,17},{2,18},{3,19},{4,20},{5,21},{6,22},{7,23},{8,24},{9,... | collective-permute-start | bytes 3932168 | tf_op jit(solution)/shard_map/ppermute | solution.py:114
  820.7 49.7 %collective-permute-start.15 = (bf16[2,64,2112]{2,1,0:T(8,128)(2,1)}, bf16[2,64,2112]{2,1,0:T(8,128)(2,1)}, u32[]{:S(2)}, u32[]{:S(2)}) collective-permute-start(bf16[2,64,2112]{2,1,0:T(8,128)(2,1)} %get-tuple-element.305), channel_id=1, source_target_pairs={{0,6},{1,7},{2,0},{3,1},{4,2},{5,3},{6,4},{7,5},{8,14},{9,15},{10,... | collective-permute-start | bytes 1622024 | tf_op jit(solution)/shard_map/ppermute | solution.py:114
  844.2 17.8 %collective-permute-start.18 = (bf16[2,64,2112]{2,1,0:T(8,128)(2,1)}, bf16[2,64,2112]{2,1,0:T(8,128)(2,1)}, u32[]{:S(2)}, u32[]{:S(2)}) collective-permute-start(bf16[2,64,2112]{2,1,0:T(8,128)(2,1)} %get-tuple-element.306), channel_id=1, source_target_pairs={{0,2},{1,3},{2,4},{3,5},{4,6},{5,7},{6,0},{7,1},{8,10},{9,11},{10,... | collective-permute-start | bytes 1622024 | tf_op jit(solution)/shard_map/ppermute | solution.py:114
  845.3 51.4 %collective-permute-start.20 = (bf16[4,2,64,640]{3,2,0,1:T(8,128)(2,1)S(1)}, bf16[4,2,64,640]{3,2,0,1:T(8,128)(2,1)S(1)}, u32[]{:S(2)}, u32[]{:S(2)}) collective-permute-start(bf16[4,2,64,640]{3,2,0,1:T(8,128)(2,1)S(1)} %bitcast.345), channel_id=1, source_target_pairs={{0,16},{1,17},{2,18},{3,19},{4,20},{5,21},{6,22},{7,23},{8,24},{9,... | collective-permute-start | bytes 1966088 | tf_op jit(solution)/shard_map/ppermute | solution.py:114
  850.4 48.4 %collective-permute-start.19 = (bf16[2,64,2112]{2,1,0:T(8,128)(2,1)}, bf16[2,64,2112]{2,1,0:T(8,128)(2,1)}, u32[]{:S(2)}, u32[]{:S(2)}) collective-permute-start(bf16[2,64,2112]{2,1,0:T(8,128)(2,1)} %get-tuple-element.307), channel_id=1, source_target_pairs={{0,4},{1,5},{2,6},{3,7},{4,0},{5,1},{6,2},{7,3},{8,12},{9,13},{10,... | collective-permute-start | bytes 1622024 | tf_op jit(solution)/shard_map/ppermute | solution.py:114
  904.5 24.8 %collective-permute-start.21 = (bf16[8000,256]{1,0:T(8,128)(2,1)}, bf16[8000,256]{1,0:T(8,128)(2,1)}, u32[]{:S(2)}, u32[]{:S(2)}) collective-permute-start(bf16[8000,256]{1,0:T(8,128)(2,1)} %slice.418), channel_id=1, source_target_pairs={{0,8},{1,9},{2,10},{3,11},{4,12},{5,13},{6,14},{7,15},{8,0},{9,1},... | collective-permute-start | bytes 12288008 | tf_op jit(solution)/shard_map/ppermute | solution.py:114
  916.0 12.2 %collective-permute-start.24 = (bf16[4,64,640]{2,1,0:T(8,128)(2,1)S(1)}, bf16[4,64,640]{2,1,0:T(8,128)(2,1)}, u32[]{:S(2)}, u32[]{:S(2)}) collective-permute-start(bf16[4,64,640]{2,1,0:T(8,128)(2,1)S(1)} %fusion.73), channel_id=1, source_target_pairs={{0,1},{1,0},{2,3},{3,2},{4,5},{5,4},{6,7},{7,6},{8,9},{9,8},{10,11... | collective-permute-start | bytes 983048 | tf_op jit(solution)/shard_map/ppermute | solution.py:114
  (93 other events, 1867.1 us)
Sparse Core Ops, SparseCore 0:
  11.5 78.8 all-gather.3
  94.0 158.5 all-gather.5
  254.7 102.7 all-gather.7
  582.5 147.7 reduce-scatter.1

commit v4 on v3

--- a/solution.py
+++ b/solution.py
@@ -189,6 +189,43 @@
         cost_estimate=SMALL,
         name="line_place",
     )(*got)
+
+
+def assemble_body(line, over_x, over_y, far_a, far_b, out, sems):
+    dp, s = lax.axis_index("dp"), lax.axis_index("seq")
+    y, lo = dp // 2, s % 2
+    his = line.shape[1]
+    copies = []
+    for c in range(2):
+        for h in range(his):
+            for block, at_y, at_lo in (
+                (line.at[c, h], y, lo),
+                (over_x.at[c, h], y, 1 - lo),
+                (over_y.at[c, h], 1 - y, lo),
+                ((far_b if c else far_a).at[h], 1 - y, 1 - lo),
+            ):
+                copies.append(
+                    pltpu.make_async_copy(
+                        block, out.at[at_y, c, h, at_lo], sems.at[len(copies)]
+                    )
+                )
+                copies[-1].start()
+    for copy in copies:
+        copy.wait()
+
+
+def assemble(line, over_x, over_y, far_a, far_b):
+    two, his, rows, columns = line.shape
+    return pallas.pallas_call(
+        assemble_body,
+        out_shape=jax.ShapeDtypeStruct((2, two, his, 2, rows, columns), line.dtype),
+        in_specs=[pallas.BlockSpec(memory_space=pallas.ANY)] * 5,
+        out_specs=pallas.BlockSpec(memory_space=pltpu.VMEM),
+        scratch_shapes=[pltpu.SemaphoreType.DMA((8 * his,))],
+        cost_estimate=SMALL,
+        compiler_params=pltpu.CompilerParams(vmem_limit_bytes=32 * 2**20),
+        name="assemble",
+    )(line, over_x, over_y, far_a, far_b)
 
 
 def cross_start(pl, term):
@@ -862,99 +899,19 @@
     return raw, kv_grad, line_out
 
 
-def weights_body(
-    his, blocks, whole, came, local_sems, core_sems, core_sems_in, up_sems, up_sems_in, x_sems, x_sems_in, y_sems,
-    y_sems_in
-):
+def rows_body(his, far, near, start, got, looked, local_sem, y_sems, y_sems_in, seq_sems, seq_sems_in):
     core = Core(his)
     dp, s = lax.axis_index("dp"), lax.axis_index("seq")
-    y, c, hi, lo = dp // 2, core.c, core.hi, core.lo
-    core.ids["y"] = (dp + 2 - 4 * y, s)
-    core.meet("c", "y", "lo", "line")
-    swap = core.copy(blocks.at[pallas.ds((1 - c) * his, his)], came, (core_sems, core_sems_in), 0, "c")
-    swap.start()
-    here, climb, over_x, over_y = [], {}, {}, {}
-
-    def cross(source, slot, at):
-        over_x[at] = core.copy(source, slot, (x_sems, x_sems_in), at, "lo")
-        over_y[at] = core.copy(source, slot, (y_sems, y_sems_in), at, "y")
-        over_x[at].start()
-        over_y[at].start()
-
-    def leave(source, j, side):
-        slot = whole.at[y, side, hi, lo]
-        here.append(pltpu.make_async_copy(source(hi), slot, local_sems.at[j]))
-        here[-1].start()
-        for k in range(1, his):
-            climb[2 * k + j] = core.copy(
-                source(lax.rem(hi + k, his)), slot, (up_sems, up_sems_in), 2 * k + j - 2, k
-            )
-            climb[2 * k + j].start()
-        cross(source(hi), slot, j)
-
-    leave(lambda h: blocks.at[c * his + h], 0, c)
-    swap.wait_recv()
-    leave(lambda h: came.at[h], 1, 1 - c)
-    for k in sorted(range(1, his), key=lambda k: min(k, his - k)):
-        h = lax.rem(hi + his - k, his)
-        for j, side in enumerate((c, 1 - c)):
-            climb[2 * k + j].wait_recv()
-            slot = whole.at[y, side, h, lo]
-            cross(slot, slot, 2 * k + j)
-    for copy in [*over_x.values(), *over_y.values()]:
-        copy.wait_recv()
-    for copy in here:
-        copy.wait()
-    sent([swap, *climb.values(), *over_x.values(), *over_y.values()])
-
-
-def gather_weights(his, blocks):
-    line, block, wide = blocks.shape
-    dma = pltpu.SemaphoreType.DMA
-    counts = (1, 2 * his - 2, 2 * his, 2 * his)
-    return pallas.pallas_call(
-        functools.partial(weights_body, his),
-        out_shape=jax.ShapeDtypeStruct((2, 2, his, 2, block, wide), low),
-        in_specs=[pallas.BlockSpec(memory_space=pltpu.VMEM)],
-        out_specs=pallas.BlockSpec(memory_space=pallas.ANY),
-        scratch_shapes=[
-            pltpu.VMEM((his, block, wide), low),
-            dma((2,)),
-            *[dma((count,)) for count in counts for _ in range(2)],
-        ],
-        cost_estimate=SMALL,
-        compiler_params=pltpu.CompilerParams(
-            collective_id=8, has_side_effects=True, vmem_limit_bytes=32 * 2**20
-        ),
-        name="gather_weights",
-    )(blocks)
-
-
-def rows_body(
-    his, far, near, whole, start, far_a, far_b, got, looked, local_sem, y_sems, y_sems_in, seq_sems, seq_sems_in,
-    a_sems, a_sems_in, b_sems, b_sems_in
-):
-    core = Core(his)
-    dp, s = lax.axis_index("dp"), lax.axis_index("seq")
-    y, seqs = dp // 2, 2 * his
-    core.ids["y"] = (dp + 2 - 4 * y, s)
+    seqs = 2 * his
+    core.ids["y"] = (dp + 2 - 4 * (dp // 2), s)
     for i in range(1, seqs):
         core.ids[f"seq{i}"] = (dp, lax.rem(s + i, seqs))
-    core.meet("y", "lo", *(f"seq{i}" for i in range(1, seqs)))
-    over, spread, carried = [], [], []
+    core.meet("y", *(f"seq{i}" for i in range(1, seqs)))
+    over, spread = [], []
     for i in range(seqs):
         to = lax.rem(s + i, seqs)
         over.append(core.copy(far.at[to], got.at[to], (y_sems, y_sems_in), i, "y"))
         over[i].start()
-    for h in range(his):
-        carried.append(
-            core.copy(whole.at[y, 0, h, 1 - core.lo], far_a.at[h], (a_sems, a_sems_in), h, "y")
-        )
-        carried.append(
-            core.copy(whole.at[1 - y, 1, h, core.lo], far_b.at[h], (b_sems, b_sems_in), h, "lo")
-        )
-    for copy in carried:
-        copy.start()
     here = None
     for i in [*range(1, seqs), 0]:
         to = lax.rem(s + i, seqs)
@@ -972,40 +929,35 @@
         else:
             here = pltpu.make_async_copy(looked.at[s], start.at[s], local_sem)
             here.start()
-    for copy in spread + carried:
+    for copy in spread:
         copy.wait_recv()
     here.wait()
-    sent(over + spread + carried)
-
-
-def gather_rows(his, far, near, whole):
+    sent(over + spread)
+
+
+def gather_rows(his, far, near):
     seqs = 2 * his
     rows, columns = far.shape[0] // seqs, far.shape[1]
     far, near = (part.reshape(seqs, rows, columns) for part in (far, near))
     dma = pltpu.SemaphoreType.DMA
-    start, far_a, far_b = pallas.pallas_call(
+    start = pallas.pallas_call(
         functools.partial(rows_body, his),
-        out_shape=(
-            jax.ShapeDtypeStruct((seqs, rows, columns), low),
-            *[jax.ShapeDtypeStruct((his, *whole.shape[4:]), low)] * 2,
-        ),
-        in_specs=[pallas.BlockSpec(memory_space=pltpu.VMEM)] * 2
-        + [pallas.BlockSpec(memory_space=pallas.ANY)],
-        out_specs=(pallas.BlockSpec(memory_space=pallas.ANY),) * 3,
+        out_shape=jax.ShapeDtypeStruct((seqs, rows, columns), low),
+        in_specs=[pallas.BlockSpec(memory_space=pltpu.VMEM)] * 2,
+        out_specs=pallas.BlockSpec(memory_space=pallas.ANY),
         scratch_shapes=[
             pltpu.VMEM((seqs, rows, columns), low),
             pltpu.VMEM((seqs, rows, columns), low),
             dma,
-            *[dma((count,)) for count in (seqs, seqs, seqs - 1, seqs - 1, his, his, his, his)],
+            *[dma((count,)) for count in (seqs, seqs, seqs - 1, seqs - 1)],
         ],
         cost_estimate=SMALL,
         compiler_params=pltpu.CompilerParams(
             collective_id=11, has_side_effects=True, vmem_limit_bytes=32 * 2**20
         ),
         name="gather_rows",
-    )(far, near, whole)
-    start = jnp.transpose(start, (1, 0, 2)).reshape(rows, seqs * columns).astype(full)
-    return start, far_a, far_b
+    )(far, near)
+    return jnp.transpose(start, (1, 0, 2)).reshape(rows, seqs * columns).astype(full)
 
 
 def sum_body(his, rows, packed, out, bufs, got, send_sems, recv_sems):
@@ -1110,7 +1062,7 @@
     def swap_rows(rows, **way):
         return pl.send(rows.astype(low), **way)
 
-    mlp_whole = gather_weights(his, split_columns(mlp_w, line))
+    mlp_here, mlp_came = line_pairs(pl, split_columns(mlp_w, line))
     ids = jnp.concatenate([tok_ids.reshape(seqs, tokens), targets.reshape(seqs, picks)], 1)
     ids = ids.reshape(seqs * (tokens + picks))
     def look(wanted, *work):
@@ -1120,9 +1072,11 @@
 
     ids_y = pl.send(ids, dy=1)
     ids_c, ids_yc = pl.send(ids, dc=1), pl.send(ids, dy=1, dc=1)
-    near_own = look(ids, mlp_whole)
+    near_own = look(ids)
     ids_c, ids_y, ids_yc = after((ids_c, ids_y, ids_yc), near_own)
-    far_other = look(ids_yc)
+    mlp_came = after(mlp_came, near_own)
+    far_other = look(ids_yc, mlp_came)
+    mlp_got = line_sends(pl, mlp_here, mlp_came)
     far_got = pl.send(far_other, dc=1)
     near_other = look(ids_c, far_other)
     near_got = pl.send(near_other, dc=1)
@@ -1130,18 +1084,15 @@
     far_sum = far_own + after(far_got, far_own)
     near_sum = near_own + after(near_got, far_own)
 
-    kv_block = jnp.concatenate(
-        [attn_w[:, D:QKV], jnp.pad(gains.T, ((0, 0), (0, 125)))], 1
-    ).astype(low)
-    kv_full = lax.all_gather(kv_block, ("dp", "seq"), axis=0, tiled=True)
-    gain_float = kv_full[:, 2 * kv_width : 2 * kv_width + 3].astype(full).T
-    kv_full = kv_full[:, : 2 * kv_width]
-    rest_low = after(attn_w, mlp_whole).astype(low)
-    rest_full = lax.all_gather(
-        jnp.concatenate([rest_low[:, :D], rest_low[:, QKV:]], 1), ("dp", "seq"), axis=0, tiled=True
-    )
-    query_full, out_full = rest_full[:, :D], rest_full[:, D:]
-    start, far_a, far_b = gather_rows(his, far_sum, near_sum, mlp_whole)
+    attn_block = jnp.concatenate([attn_w, jnp.pad(gains.T, ((0, 0), (0, 125)))], 1).astype(low)
+    attn_full = lax.all_gather(attn_block, ("dp", "seq"), axis=0, tiled=True)
+    query_full, out_full = attn_full[:, :D], attn_full[:, QKV : QKV + D]
+    kv_full = attn_full[:, D:QKV]
+    gain_float = attn_full[:, QKV + D : QKV + D + 3].astype(full).T
+    start = gather_rows(his, far_sum, near_sum)
+    mlp_line = line_place(pl, after(mlp_got, start)).reshape(2, his, block, wide)
+    mlp_x, mlp_y = pl.send(mlp_line, dlo=1), pl.send(mlp_line, dy=1)
+    start = after(start, mlp_line)
     head_low = after(head, start).astype(low)
     emb_square_sum = jnp.sum(after(emb, start) ** 2)
 
@@ -1149,7 +1100,6 @@
     pick_pos = lax.dynamic_slice_in_dim(positions[0], pl.s * picks, picks)
     token_tables = turn_tables(*yarn_tables(token_pos.astype(full)))
     pick_tables = turn_tables(*yarn_tables(pick_pos.astype(full)))
-    head_rows = lax.all_gather(after(head_low, start), "dp", axis=1, tiled=True)
     normed = rms_norm(start, gain_float[0]).astype(low)
     normed_tok, normed_pick = normed[:tokens], normed[tokens:]
     start_pick = start[tokens:]
@@ -1164,16 +1114,13 @@
         gathers=1,
     )
     kv_all = kv_all.reshape(seqs * tokens, 2 * kv_width)
-    raw = matmul(normed_pick, query_full)
+    kv_all, mlp_x, mlp_y = lax.optimization_barrier((kv_all, mlp_x, mlp_y))
+    raw = matmul(after(normed_pick, kv_all), query_full)
+    mlp_far = (pl.send(mlp_x[0], dy=1), pl.send(mlp_y[1], dlo=1))
+    head_rows = lax.all_gather(after(head_low, kv_all), "dp", axis=1, tiled=True)
     queries, attended_low, attended, log_total, pick_line = attend_rows(
         his, raw, pick_tables, pick_pos, kv_all, normed_pick
     )
-    for c, block_far in enumerate((far_a, far_b)):
-        mlp_whole = lax.dynamic_update_slice(
-            mlp_whole, block_far[None, None, :, None], (1 - pl.y, c, 0, 1 - pl.lo, 0, 0)
-        )
-    mlp_full = mlp_whole.reshape(D, wide)
-
     def shares(rows):
         return jnp.transpose(rows.reshape(picks, line, D // line), (1, 0, 2))
 
@@ -1192,6 +1139,8 @@
         swap=(his, picks, D // line),
     )
     normed_two = normed_two.reshape(line * picks, D)
+    mlp_far = after(mlp_far, normed_two)
+    mlp_full = assemble(mlp_line, mlp_x, mlp_y, *mlp_far).reshape(D, wide)
     gate_up = matmul(normed_two, mlp_full[:, : 2 * part])
     gate = gate_up[:, :part]
     upward = gate_up[:, part:]

time: 1040 us -> 1010 us (0.971)
  Pallas kernels: 530 us -> 423 us
  waiting for transfers between devices: 32.2 us -> 85.2 us
  local copies, waits for them, and re-layouts: 128 us -> 110 us
  starting transfers between devices: 32 us -> 47.2 us
  other arithmetic: 185 us -> 200 us
    pallas_call x2, Pallas kernels: 176 us -> 58.3 us  [the longest x1 55.5 us: gather_rows(): pallas.pallas_call(functools.partial(rows_body, his), out_shape=jax.Shape...]
    all_gather x3 -> x2, waiting for transfers between devices: 0.01 us -> 47.4 us  [the longest x1 47.4 us: on_device(): attn_full = lax.all_gather(attn_block, ('dp', 'seq'), axis=0, tiled=True)]
    ppermute x23 -> x31, starting transfers between devices: 25.6 us -> 39.1 us  [send(): return lax.ppermute(value, ('dp', 'seq'), pairs)]
    unnamed x196 -> x210, local copies, waits for them, and re-layouts: 34.4 us -> 22.8 us
    ppermute x23 -> x31, waiting for transfers between devices: 29.1 us -> 35.4 us  [send(): return lax.ppermute(value, ('dp', 'seq'), pairs)]
  transfers between devices with their start and end apart: 30 -> 37, of which waited for: 6 -> 8; matrix products, arithmetic and copies ran while one was open for 26% -> 28% of each run, Pallas kernels for 41% -> 32%
where the time goes in v4:
time: 1010 us; the launch traced here: 996 us
  Pallas kernels  423 us (42%)
  other arithmetic  200 us (20%)
  local copies, waits for them, and re-layouts  110 us (11%)
  matrix products  104 us (10%)
  waiting for transfers between devices  85.2 us (8%)
  starting transfers between devices  47.2 us (5%)
  between operations  26.8 us (3%)
    pallas_call x6, Pallas kernels, move(): pallas.pallas_call(body, out_shape=tuple((jax.ShapeDtypeStruct(shape, dty...  252 us
    pallas_call x1, Pallas kernels, gather_rows(): pallas.pallas_call(functools.partial(rows_body, his), out_shape=jax.Shape...  55.5 us
    all_gather x1, waiting for transfers between devices, on_device(): attn_full = lax.all_gather(attn_block, ('dp', 'seq'), axis=0, tiled=True)  47.4 us
    ppermute x31, starting transfers between devices, send(): return lax.ppermute(value, ('dp', 'seq'), pairs)  39.1 us
    dot_general x6, matrix products, matmul(): return jnp.dot(left, right, preferred_element_type=jnp.float32)  38.5 us
    gather x4, local copies, waits for them, and re-layouts, look(): rows = jnp.take(emb, jnp.clip(at, 0, emb_n - 1), axis=0, mode='clip')  36.8 us
    dot_general x6, matrix products, matmul_nt(): lax.dot_general(left, right, (((1,), (1,)), ((), ())), preferred_element_...  36.5 us
    ppermute x31, waiting for transfers between devices, send(): return lax.ppermute(value, ('dp', 'seq'), pairs)  35.4 us
  transfers between devices with their start and end apart: 37, of which 8 were waited for; matrix products, arithmetic and copies ran while one was open for 28% of the time, Pallas kernels for 32%

profile of v4, /device:TPU:0, one launch (start us, length us, event | category | flops | bytes accessed | tf_op | source)
XLA Modules:
  0.0 995.6 jit_solution(13793545681411843980)
XLA Ops:
  21.3 9.6 gather_fusion
  51.9 9.1 gather_fusion.2
  77.6 55.5 %gather_rows.1 = bf16[8,320,256]{2,1,0:T(8,128)(2,1)S(1)} custom-call(bf16[8,320,256]{2,1,0:T(8,128)(2,1)S(1)} %bitcast.288, bf16[8,320,256]{2,1,0:T(8,128)(2,1)S(1)} %bitcast.289), custom_call_target="tpu_custom_call" | custom-call | flops 1024 | bytes 1024 | tf_op jit(solution)/shard_map/gather_rows/pallas_call | solution.py:943
  138.3 10.4 %collective-permute-start.9 = (bf16[2,4,64,2112]{3,2,1,0:T(8,128)(2,1)}, bf16[2,4,64,2112]{3,2,1,0:T(8,128)(2,1)S(1)}, u32[]{:S(2)}, u32[]{:S(2)}) collective-permute-start(bf16[2,4,64,2112]{3,2,1,0:T(8,128)(2,1)} %bitcast.278), channel_id=1, source_target_pairs={{0,1},{1,0},{2,3},{3,2},{4,5},{5,4},{6,7},{7,6},{8,9},{9,8},{10,11... | collective-permute-start | bytes 6488072 | tf_op jit(solution)/shard_map/ppermute | solution.py:114
  158.1 47.4 %all-gather.3.cloned.1.call-done = bf16[2048,4736]{1,0:T(8,128)(2,1)} async-done(((bf16[64,4736]{1,0:T(8,128)(2,1)}), bf16[2048,4736]{1,0:T(8,128)(2,1)}) %all-gather.3.cloned.1.call-update) | async-done | bytes 19398672 | tf_op jit(solution)/shard_map/all_gather | solution.py:1088
  214.5 37.7 %shard_map.337 = bf16[4,2,256,512]{3,2,1,0:T(8,128)(2,1)S(1)} custom-call(f32[256,512]{1,0:T(8,128)S(1)} %fusion.42.projected, f32[256,128]{1,0:T(8,128)S(1)} %get-tuple-element.387.cosine, f32[256,128]{1,0:T(8,128)S(1)} %get-tuple-element.388.sine), custom_call_target="tpu_custom_call" | custom-call | flops 1024 | bytes 1024 | tf_op jit(solution)/shard_map/pallas_call | solution.py:704
  268.4 25.2 %attend.1 = (bf16[8,256,64]{2,1,0:T(8,128)(2,1)}, bf16[64,2048]{1,0:T(8,128)(2,1)}, f32[8,256,64]{2,1,0:T(8,128)}, f32[8,256,128]{2,1,0:T(8,128)}, bf16[2,4,64,2048]{3,2,1,0:T(8,128)(2,1)}) custom-call(f32[64,2048]{1,0:T(8,128)} %fusion.12.raw, f32[64,128]{1,0:T(8,128)} %get-tuple-element.389.cosine, f32[64,128]{1,0:T(8,128)} %get-tuple-element.390.sine, ...), custom_call_target="tpu_custom_call" | custom-call | flops 1024 | bytes 1024 | tf_op jit(solution)/shard_map/attend/pallas_call | solution.py:801
  300.9 36.0 %shard_map.338 = (bf16[4,2,64,2048]{3,2,1,0:T(8,128)(2,1)S(1)}, bf16[8,64,256]{2,1,0:T(8,128)(2,1)S(1)}) custom-call(f32[64,2048]{1,0:T(8,128)S(1)} %fusion.34.values.middle, f32[1,2048]{1,0:T(1,128)S(1)} %get-tuple-element.357.gain, bf16[8,64,256]{2,1,0:T(8,128)(2,1)S(1)} %bitcast.296), custom_call_target="tpu_custom_call" | custom-call | flops 1024 | bytes 1024 | tf_op jit(solution)/shard_map/pallas_call | solution.py:704
  347.5 54.1 %shard_map.339 = (f32[64,2048]{1,0:T(8,128)S(1)}, bf16[4,2,64,2048]{3,2,1,0:T(8,128)(2,1)S(1)}) custom-call(f32[4,2,64,2048]{3,2,1,0:T(8,128)} %bitcast.327, f32[64,2048]{1,0:T(8,128)S(1)} %fusion.34.values.middle, f32[1,2048]{1,0:T(1,128)S(1)} %get-tuple-element.356.gain), custom_call_target="tpu_custom_call" | custom-call | flops 1024 | bytes 1024 | tf_op jit(solution)/shard_map/pallas_call | solution.py:704
  401.7 12.5 %fusion.117 = (f32[512]{0:T(512)S(1)}, f32[512,4000]{0,1:T(8,128)S(1)}) fusion(bf16[512,2048]{1,0:T(8,128)(2,1)S(1)} %bitcast.301, bf16[4000,2048]{1,0:T(8,128)(2,1)} %all-gather.5.cloned.1.call-done), kind=kOutput, calls=%fused_computation.333 | convolution fusion | flops 8390655488 | bytes 26675200 | tf_op jit(solution)/shard_map/dot_general | solution.py:78
  414.4 11.1 %exponential_reduce_fusion = (f32[512]{0:T(512)S(1)}, f32[512]{0:T(512)S(1)}) fusion(f32[512,4000]{0,1:T(8,128)S(1)} %get-tuple-element.386, f32[512]{0:T(512)S(1)} %get-tuple-element.385, s32[4000]{0:T(1024)S(1)} %copy-done.43, s32[512]{0:T(512)S(1)} %bitcast.356), kind=kLoop, calls=%fused_computation.28 | loop fusion | flops 10238976 | bytes 8216192 | tf_op jit(solution)/shard_map/reduce_sum | solution.py:1167
  443.8 15.5 %fusion.118 = f32[512,2048]{1,0:T(8,128)} fusion(bf16[512,4000]{0,1:T(8,128)(2,1)S(1)} %fusion.5, bf16[4000,2048]{1,0:T(8,128)(2,1)} %all-gather.5.cloned.1.call-done), kind=kOutput, calls=%fused_computation.334 | convolution fusion | flops 8388608000 | bytes 24674304 | tf_op jit(solution)/shard_map/dot_general | solution.py:74
  459.3 57.1 %shard_map.340 = (f32[64,2048]{1,0:T(8,128)S(1)}, f32[1,2048]{1,0:T(1,128)S(1)}, bf16[4,2,64,2048]{3,2,1,0:T(8,128)(2,1)S(1)}) custom-call(f32[4,2,64,2048]{3,2,1,0:T(8,128)} %bitcast.326, f32[64,2048]{1,0:T(8,128)S(1)} %get-tuple-element.132.ending, f32[1,2048]{1,0:T(1,128)S(1)} %get-tuple-element.356.gain), custom_call_target="tpu_custom_call" | custom-call | flops 1024 | bytes 1024 | tf_op jit(solution)/shard_map/pallas_call | solution.py:704
  541.4 11.5 %convolution_convert_fusion = bf16[4000,2048]{1,0:T(8,128)(2,1)} fusion(bf16[512,4000]{0,1:T(8,128)(2,1)S(1)} %copy-done.32, bf16[512,2048]{1,0:T(8,128)(2,1)S(1)} %bitcast.302), kind=kOutput, calls=%fused_computation.6 | convolution fusion | flops 8396800000 | bytes 22577152 | tf_op jit(solution)/shard_map/dot_general | solution.py:84
  578.7 27.2 %shard_map.341 = (f32[64,2048]{1,0:T(8,128)S(1)}, bf16[64,2048]{1,0:T(8,128)(2,1)S(1)}, f32[1,2048]{1,0:T(1,128)S(1)}) custom-call(f32[4,2,64,2048]{3,2,1,0:T(8,128)S(1)} %bitcast.290, f32[64,2048]{1,0:T(8,128)S(1)} %fusion.34.values.middle, f32[1,2048]{1,0:T(1,128)S(1)} %get-tuple-element.357.gain, f32[64,2048]{1,0:T(8,128)S(1)} %get-tuple-element.137.ending_grad), custom_call_target="tpu_custom_call" | custom-call | flops 1024 | bytes 1024 | tf_op jit(solution)/shard_map/pallas_call | solution.py:704
  611.7 27.2 %attend_back.1 = (bf16[64,2048]{1,0:T(8,128)(2,1)}, f32[2048,512]{1,0:T(8,128)}, bf16[2,4,64,2048]{3,2,1,0:T(8,128)(2,1)}) custom-call(bf16[64,2048]{1,0:T(8,128)(2,1)} %fusion.37.grad, f32[64,128]{1,0:T(8,128)} %get-tuple-element.389.cosine, f32[64,128]{1,0:T(8,128)} %get-tuple-element.390.sine, s32[64,1]{1,0:T(8,128)} %copy.146.places, ...), custom_call_target="tpu_custom_call" | custom-call | flops 1024 | bytes 1024 | tf_op jit(solution)/shard_map/attend_back/pallas_call | solution.py:874
  655.5 40.3 %shard_map.342 = (bf16[256,512]{1,0:T(8,128)(2,1)S(1)}, bf16[8,64,256]{2,1,0:T(8,128)(2,1)S(1)}) custom-call(f32[4,2,256,512]{3,2,1,0:T(8,128)S(1)} %bitcast.291, f32[256,128]{1,0:T(8,128)S(1)} %get-tuple-element.387.cosine, f32[256,128]{1,0:T(8,128)S(1)} %get-tuple-element.388.sine, bf16[8,64,256]{2,1,0:T(8,128)(2,1)S(1)} %bitcast.295), custom_call_target="tpu_custom_call" | custom-call | flops 1024 | bytes 1024 | tf_op jit(solution)/shard_map/pallas_call | solution.py:704
  744.2 13.3 %collective-permute-done.19 = bf16[4,64,2112]{2,1,0:T(8,128)(2,1)} collective-permute-done((bf16[4,64,2112]{2,1,0:T(8,128)(2,1)}, bf16[4,64,2112]{2,1,0:T(8,128)(2,1)}, u32[]{:S(2)}, u32[]{:S(2)}) %collective-permute-start.19) | collective-permute-done | bytes 1081376 | tf_op jit(solution)/shard_map/ppermute | solution.py:114
  785.6 20.1 %scatter_custom_fusion = f32[16008,256]{1,0:T(8,128)} fusion(s32[2560]{0:T(1024)} %get-tuple-element.309, f32[]{:T(128)} %constant.315.clone.1, bf16[2560,256]{1,0:T(8,128)(2,1)} %bitcast.55), kind=kCustom, calls=%fused_computation.14 | custom fusion | flops 1310720 | bytes 17703424 | tf_op jit(solution)/shard_map/scatter-add | solution.py:1339
  812.7 10.8 %collective-permute-done.26.refs_1_ = bf16[2,64,2112]{2,1,0:T(8,128)(2,1)} collective-permute-done((bf16[2,64,2112]{2,1,0:T(8,128)(2,1)}, bf16[2,64,2112]{2,1,0:T(8,128)(2,1)}, u32[]{:S(2)}, u32[]{:S(2)}) %collective-permute-start.26) | collective-permute-done | bytes 540704 | tf_op jit(solution)/shard_map/ppermute | solution.py:114
  831.9 26.2 %scatter_custom_fusion.1 = f32[16008,256]{1,0:T(8,128)} fusion(f32[16008,256]{1,0:T(8,128)} %scatter_custom_fusion, s32[2560]{0:T(1024)S(1)} %compare_select_fusion.2, bf16[2560,256]{1,0:T(8,128)(2,1)} %collective-permute-done.22), kind=kCustom, calls=%fused_computation.85 | custom fusion | flops 1310720 | bytes 17702912 | tf_op jit(solution)/shard_map/scatter-add | solution.py:1349
  901.7 28.9 %layer_gradient.1 = (f32[64,4608]{1,0:T(8,128)S(1)}, f32[64,128]{1,0:T(8,128)S(1)}, f32[64,1]{1,0:T(8,128)S(1)}, f32[1,4608]{1,0:T(1,128)S(1)}) custom-call(bf16[8,64,512]{2,1,0:T(8,128)(2,1)S(1)} %bitcast.294, f32[4,64,640]{2,1,0:T(8,128)S(1)} %bitcast_add_fusion.tokens), custom_call_target="tpu_custom_call" | custom-call | flops 1024 | bytes 1024 | tf_op jit(solution)/shard_map/layer_gradient/pallas_call | solution.py:611
  932.1 20.3 %sum_statistics.1 = f32[296,128]{1,0:T(8,128)S(1)} custom-call(f32[296,128]{1,0:T(8,128)S(1)} %constant_dynamic-update-slice_fusion.2.packed), custom_call_target="tpu_custom_call" | custom-call | tf_op jit(solution)/shard_map/sum_statistics/pallas_call | solution.py:1006
  966.8 12.0 %multiply_subtract_fusion.1 = f32[8000,256]{1,0:T(8,128)} fusion(f32[8000,256]{1,0:T(8,128)} %param.22, f32[8000,256]{1,0:T(8,128)} %get-tuple-element.414, f32[]{:T(128)} %bitcast.115, f32[256]{0:T(256)S(1)} %bitcast_add_fusion.4, f32[8000]{0:T(1024)S(1)} %fusion.85, f32[]{:T(128)} %bitcast.112), kind=kLoop, calls=%fused_computation.23 | loop fusion | flops 10240000 | bytes 24609032 | tf_op jit(solution)/shard_map/sub | solution.py:90
  (469 shorter events, 349.9 us)
Async XLA Ops:
  7.2 198.2 %all-gather.3.cloned.1.call-start = ((), (), s32[]{:S(2)}) async-start(), calls=%async_computation.2 | async-start | bytes 20004864 | tf_op jit(solution)/shard_map/all_gather | solution.py:1088
  11.0 390.7 %all-gather.5.cloned.1.call-start = ((), (), s32[]{:S(2)}) async-start(), calls=%async_computation.3 | async-start | bytes 20480000 | tf_op jit(solution)/shard_map/all_gather | solution.py:1120
  34.7 100.6 %collective-permute-start.6 = (bf16[2,64,2112]{2,1,0:T(8,128)(2,1)}, bf16[2,64,2112]{2,1,0:T(8,128)(2,1)}, u32[]{:S(2)}, u32[]{:S(2)}) collective-permute-start(bf16[2,64,2112]{2,1,0:T(8,128)(2,1)} %get-tuple-element.330), channel_id=1, source_target_pairs={{0,2},{1,3},{2,4},{3,5},{4,6},{5,7},{6,0},{7,1},{8,10},{9,11},{10,... | collective-permute-start | bytes 1622024 | tf_op jit(solution)/shard_map/ppermute | solution.py:114
  36.6 98.6 %collective-permute-start.7 = (bf16[2,64,2112]{2,1,0:T(8,128)(2,1)}, bf16[2,64,2112]{2,1,0:T(8,128)(2,1)}, u32[]{:S(2)}, u32[]{:S(2)}) collective-permute-start(bf16[2,64,2112]{2,1,0:T(8,128)(2,1)} %get-tuple-element.331), channel_id=1, source_target_pairs={{0,4},{1,5},{2,6},{3,7},{4,0},{5,1},{6,2},{7,3},{8,12},{9,13},{10,... | collective-permute-start | bytes 1622024 | tf_op jit(solution)/shard_map/ppermute | solution.py:114
  39.2 96.1 %collective-permute-start.8 = (bf16[2,64,2112]{2,1,0:T(8,128)(2,1)}, bf16[2,64,2112]{2,1,0:T(8,128)(2,1)}, u32[]{:S(2)}, u32[]{:S(2)}) collective-permute-start(bf16[2,64,2112]{2,1,0:T(8,128)(2,1)} %get-tuple-element.328), channel_id=1, source_target_pairs={{0,6},{1,7},{2,0},{3,1},{4,2},{5,3},{6,4},{7,5},{8,14},{9,15},{10,... | collective-permute-start | bytes 1622024 | tf_op jit(solution)/shard_map/ppermute | solution.py:114
  51.8 20.9 %collective-permute-start.4 = (bf16[2560,256]{1,0:T(8,128)(2,1)}, bf16[2560,256]{1,0:T(8,128)(2,1)}, u32[]{:S(2)}, u32[]{:S(2)}) collective-permute-start(bf16[2560,256]{1,0:T(8,128)(2,1)} %select_convert_fusion.2), channel_id=1, source_target_pairs={{0,8},{1,9},{2,10},{3,11},{4,12},{5,13},{6,14},{7,15},{8,0},{9,1},... | collective-permute-start | bytes 3932168 | tf_op jit(solution)/shard_map/ppermute | solution.py:114
  138.3 115.3 %collective-permute-start.9 = (bf16[2,4,64,2112]{3,2,1,0:T(8,128)(2,1)}, bf16[2,4,64,2112]{3,2,1,0:T(8,128)(2,1)S(1)}, u32[]{:S(2)}, u32[]{:S(2)}) collective-permute-start(bf16[2,4,64,2112]{3,2,1,0:T(8,128)(2,1)} %bitcast.278), channel_id=1, source_target_pairs={{0,1},{1,0},{2,3},{3,2},{4,5},{5,4},{6,7},{7,6},{8,9},{9,8},{10,11... | collective-permute-start | bytes 6488072 | tf_op jit(solution)/shard_map/ppermute | solution.py:114
  148.6 104.9 %collective-permute-start.10 = (bf16[2,4,64,2112]{3,2,1,0:T(8,128)(2,1)}, bf16[2,4,64,2112]{3,2,1,0:T(8,128)(2,1)}, u32[]{:S(2)}, u32[]{:S(2)}) collective-permute-start(bf16[2,4,64,2112]{3,2,1,0:T(8,128)(2,1)} %bitcast.279), channel_id=1, source_target_pairs={{0,16},{1,17},{2,18},{3,19},{4,20},{5,21},{6,22},{7,23},{8,24},{9,... | collective-permute-start | bytes 6488072 | tf_op jit(solution)/shard_map/ppermute | solution.py:114
  253.6 569.9 %reduce-scatter.2.cloned.1.call-start = ((), (), s32[]{:S(2)}) async-start(), calls=%async_computation.4 | async-start | bytes 20480000 | tf_op jit(solution)/shard_map/reduce_scatter | solution.py:1217
  258.0 78.9 %collective-permute-start.11 = (bf16[4,64,2112]{2,1,0:T(8,128)(2,1)S(1)}, bf16[4,64,2112]{2,1,0:T(8,128)(2,1)S(1)}, u32[]{:S(2)}, u32[]{:S(2)}) collective-permute-start(bf16[4,64,2112]{2,1,0:T(8,128)(2,1)S(1)} %slice_bitcast_fusion.1), channel_id=1, source_target_pairs={{0,16},{1,17},{2,18},{3,19},{4,20},{5,21},{6,22},{7,23},{8,24},{9,... | collective-permute-start | bytes 3244040 | tf_op jit(solution)/shard_map/ppermute | solution.py:114
  261.2 75.7 %collective-permute-start.12 = (bf16[4,64,2112]{2,1,0:T(8,128)(2,1)S(1)}, bf16[4,64,2112]{2,1,0:T(8,128)(2,1)S(1)}, u32[]{:S(2)}, u32[]{:S(2)}) collective-permute-start(bf16[4,64,2112]{2,1,0:T(8,128)(2,1)S(1)} %slice_bitcast_fusion), channel_id=1, source_target_pairs={{0,1},{1,0},{2,3},{3,2},{4,5},{5,4},{6,7},{7,6},{8,9},{9,8},{10,11... | collective-permute-start | bytes 3244040 | tf_op jit(solution)/shard_map/ppermute | solution.py:114
  560.7 86.1 %collective-permute-start.16 = (bf16[4,2,64,2112]{3,2,0,1:T(8,128)(2,1)}, bf16[4,2,64,2112]{3,2,0,1:T(8,128)(2,1)}, u32[]{:S(2)}, u32[]{:S(2)}) collective-permute-start(bf16[4,2,64,2112]{3,2,0,1:T(8,128)(2,1)} %bitcast.265), channel_id=1, source_target_pairs={{0,16},{1,17},{2,18},{3,19},{4,20},{5,21},{6,22},{7,23},{8,24},{9,... | collective-permute-start | bytes 6488072 | tf_op jit(solution)/shard_map/ppermute | solution.py:114
  564.1 82.7 %collective-permute-start.17 = (bf16[2,4,64,2112]{3,2,1,0:T(8,128)(2,1)}, bf16[2,4,64,2112]{3,2,1,0:T(8,128)(2,1)}, u32[]{:S(2)}, u32[]{:S(2)}) collective-permute-start(bf16[2,4,64,2112]{3,2,1,0:T(8,128)(2,1)} %dynamic-slice_bitcast_fusion.2), channel_id=1, source_target_pairs={{0,1},{1,0},{2,3},{3,2},{4,5},{5,4},{6,7},{7,6},{8,9},{9,8},{10,11... | collective-permute-start | bytes 6488072 | tf_op jit(solution)/shard_map/ppermute | solution.py:114
  714.9 58.8 %all-to-all-start = ((bf16[320,8,256]{2,0,1:T(8,128)(2,1)}), bf16[320,8,256]{2,0,1:T(8,128)(2,1)}, u32[]{:S(2)}, u32[]{:S(2)}) async-start(bf16[320,8,256]{2,0,1:T(8,128)(2,1)} %pad_maximum_fusion.4), calls=%async_computation | async-start | bytes 2621440 | tf_op jit(solution)/shard_map/all_to_all | solution.py:1273
  720.8 36.8 %collective-permute-start.19 = (bf16[4,64,2112]{2,1,0:T(8,128)(2,1)}, bf16[4,64,2112]{2,1,0:T(8,128)(2,1)}, u32[]{:S(2)}, u32[]{:S(2)}) collective-permute-start(bf16[4,64,2112]{2,1,0:T(8,128)(2,1)} %fusion.47), channel_id=1, source_target_pairs={{0,1},{1,0},{2,3},{3,2},{4,5},{5,4},{6,7},{7,6},{8,9},{9,8},{10,11... | collective-permute-start | bytes 3244040 | tf_op jit(solution)/shard_map/ppermute | solution.py:114
  722.9 34.7 %collective-permute-start.20 = (bf16[4,64,2112]{2,1,0:T(8,128)(2,1)}, bf16[4,64,2112]{2,1,0:T(8,128)(2,1)}, u32[]{:S(2)}, u32[]{:S(2)}) collective-permute-start(bf16[4,64,2112]{2,1,0:T(8,128)(2,1)} %fusion.48), channel_id=1, source_target_pairs={{0,16},{1,17},{2,18},{3,19},{4,20},{5,21},{6,22},{7,23},{8,24},{9,... | collective-permute-start | bytes 3244040 | tf_op jit(solution)/shard_map/ppermute | solution.py:114
  724.6 51.1 %collective-permute-start.18 = (bf16[1024,640]{0,1:T(8,128)(2,1)}, bf16[1024,640]{0,1:T(8,128)(2,1)}, u32[]{:S(2)}, u32[]{:S(2)}) collective-permute-start(bf16[1024,640]{0,1:T(8,128)(2,1)} %fusion.45), channel_id=1, source_target_pairs={{0,8},{1,9},{2,10},{3,11},{4,12},{5,13},{6,14},{7,15},{8,0},{9,1},... | collective-permute-start | bytes 3932168 | tf_op jit(solution)/shard_map/ppermute | solution.py:114
  772.3 33.4 %collective-permute-start.24 = (bf16[4,2,64,512]{3,2,0,1:T(8,128)(2,1)}, bf16[4,2,64,512]{3,2,0,1:T(8,128)(2,1)}, u32[]{:S(2)}, u32[]{:S(2)}) collective-permute-start(bf16[4,2,64,512]{3,2,0,1:T(8,128)(2,1)} %bitcast.268), channel_id=1, source_target_pairs={{0,16},{1,17},{2,18},{3,19},{4,20},{5,21},{6,22},{7,23},{8,24},{9,... | collective-permute-start | bytes 1572872 | tf_op jit(solution)/shard_map/ppermute | solution.py:114
  773.3 32.4 %collective-permute-start.25 = (bf16[2,4,64,512]{3,2,1,0:T(8,128)(2,1)}, bf16[2,4,64,512]{3,2,1,0:T(8,128)(2,1)}, u32[]{:S(2)}, u32[]{:S(2)}) collective-permute-start(bf16[2,4,64,512]{3,2,1,0:T(8,128)(2,1)} %dynamic-slice_bitcast_fusion.7), channel_id=1, source_target_pairs={{0,1},{1,0},{2,3},{3,2},{4,5},{5,4},{6,7},{7,6},{8,9},{9,8},{10,11... | collective-permute-start | bytes 1572872 | tf_op jit(solution)/shard_map/ppermute | solution.py:114
  773.6 58.3 %collective-permute-start.22 = (bf16[2560,256]{1,0:T(8,128)(2,1)}, bf16[2560,256]{1,0:T(8,128)(2,1)}, u32[]{:S(2)}, u32[]{:S(2)}) collective-permute-start(bf16[2560,256]{1,0:T(8,128)(2,1)} %bitcast.55), channel_id=1, source_target_pairs={{0,16},{1,17},{2,18},{3,19},{4,20},{5,21},{6,22},{7,23},{8,24},{9,... | collective-permute-start | bytes 3932168 | tf_op jit(solution)/shard_map/ppermute | solution.py:114
  782.5 49.5 %collective-permute-start.23 = (bf16[2,64,2112]{2,1,0:T(8,128)(2,1)}, bf16[2,64,2112]{2,1,0:T(8,128)(2,1)}, u32[]{:S(2)}, u32[]{:S(2)}) collective-permute-start(bf16[2,64,2112]{2,1,0:T(8,128)(2,1)} %get-tuple-element.323), channel_id=1, source_target_pairs={{0,6},{1,7},{2,0},{3,1},{4,2},{5,3},{6,4},{7,5},{8,14},{9,15},{10,... | collective-permute-start | bytes 1622024 | tf_op jit(solution)/shard_map/ppermute | solution.py:114
  806.8 51.4 %collective-permute-start.28 = (bf16[4,2,64,640]{3,2,0,1:T(8,128)(2,1)S(1)}, bf16[4,2,64,640]{3,2,0,1:T(8,128)(2,1)S(1)}, u32[]{:S(2)}, u32[]{:S(2)}) collective-permute-start(bf16[4,2,64,640]{3,2,0,1:T(8,128)(2,1)S(1)} %bitcast.337), channel_id=1, source_target_pairs={{0,16},{1,17},{2,18},{3,19},{4,20},{5,21},{6,22},{7,23},{8,24},{9,... | collective-permute-start | bytes 1966088 | tf_op jit(solution)/shard_map/ppermute | solution.py:114
  811.3 49.2 %collective-permute-start.27 = (bf16[2,64,2112]{2,1,0:T(8,128)(2,1)}, bf16[2,64,2112]{2,1,0:T(8,128)(2,1)S(1)}, u32[]{:S(2)}, u32[]{:S(2)}) collective-permute-start(bf16[2,64,2112]{2,1,0:T(8,128)(2,1)} %get-tuple-element.325), channel_id=1, source_target_pairs={{0,4},{1,5},{2,6},{3,7},{4,0},{5,1},{6,2},{7,3},{8,12},{9,13},{10,... | collective-permute-start | bytes 1622024 | tf_op jit(solution)/shard_map/ppermute | solution.py:114
  866.9 26.7 %collective-permute-start.29 = (bf16[8000,256]{1,0:T(8,128)(2,1)}, bf16[8000,256]{1,0:T(8,128)(2,1)}, u32[]{:S(2)}, u32[]{:S(2)}) collective-permute-start(bf16[8000,256]{1,0:T(8,128)(2,1)} %slice.403), channel_id=1, source_target_pairs={{0,8},{1,9},{2,10},{3,11},{4,12},{5,13},{6,14},{7,15},{8,0},{9,1},... | collective-permute-start | bytes 12288008 | tf_op jit(solution)/shard_map/ppermute | solution.py:114
  (108 other events, 1775.6 us)
Sparse Core Ops, SparseCore 0:
  11.5 193.9 all-gather.2
  253.7 118.5 all-gather.4
  553.0 147.7 reduce-scatter.1

commit v5 on v4

--- a/solution.py
+++ b/solution.py
@@ -1092,9 +1092,11 @@
     start = gather_rows(his, far_sum, near_sum)
     mlp_line = line_place(pl, after(mlp_got, start)).reshape(2, his, block, wide)
     mlp_x, mlp_y = pl.send(mlp_line, dlo=1), pl.send(mlp_line, dy=1)
-    start = after(start, mlp_line)
+    emb_square_sum, *other_squares = (
+        jnp.sum(after(w, mlp_line) ** 2) for w in (emb, attn_w, mlp_w, head)
+    )
+    start = after(start, mlp_line, emb_square_sum, other_squares)
     head_low = after(head, start).astype(low)
-    emb_square_sum = jnp.sum(after(emb, start) ** 2)
 
     token_pos = pl.s * tokens + jnp.arange(tokens, dtype=jnp.int32)
     pick_pos = lax.dynamic_slice_in_dim(positions[0], pl.s * picks, picks)
@@ -1304,7 +1306,6 @@
 
     token_got = pl.send(token_term(1 - pl.c).astype(low), dc=1)
     token_keep = token_term(pl.c)
-    other_squares = [jnp.sum(after(w, token_keep) ** 2) for w in (attn_w, mlp_w, head)]
     early = [
         loss_part,
         jnp.sum(attn_row),
@@ -1317,10 +1318,10 @@
     ]
     slot = jnp.arange(128, dtype=jnp.int32)
     early = sum(jnp.where(slot == i, value, 0.0) for i, value in enumerate(early))
-    mlp_term = cross_end(pl, mlp_state, early)
+    back_rows, early = lax.optimization_barrier((back_rows, early))
+    back_got = pl.send(back_rows, dy=1)
+    mlp_term = cross_end(pl, mlp_state, back_rows)
     mlp_here, mlp_came = line_pairs(pl, mlp_term)
-    back_rows, early = lax.optimization_barrier((back_rows, early, mlp_term, query_term))[:2]
-    back_got = pl.send(back_rows, dy=1)
     token_sum = grid(token_keep + after(token_got, back_rows).astype(full))
     token_got = pl.send(pick(token_sum, 1 - pl.y, 0), dy=1)
 
@@ -1336,20 +1337,20 @@
     chip_grad = (
         jnp.zeros((2 * emb_n + 8, emb_m), full)
         .at[places_in[0]]
-        .add(after(back_rows, token_sum, mlp_came).astype(full))
+        .add(after(back_rows, token_sum, mlp_came, query_term).astype(full))
     )
     mlp_got = line_sends(pl, mlp_here, after(mlp_came, token_sum))
     near, far = mlp_got[1:2] + mlp_got[-1:], mlp_got[2:-1]
     query_state = cross_send(pl, *cross_next(pl, query_state, chip_grad))
-    head_grad = after(head_grad, query_state[:2], near[0]).astype(full)
+    head_grad = after(head_grad, query_state[:2]).astype(full)
     head_square = head_grad * head_grad + eps_square
     head_rows_sum = jnp.sum(head_square, 1)
     head_cols_sum = jnp.sum(head_square, 0)
-    back_got = after(back_got, near[1:], head_rows_sum, head_cols_sum)
+    back_got = after(back_got, near[0], head_rows_sum, head_cols_sum)
     chip_grad = chip_grad.at[places_in[1]].add(back_got.astype(full))
     token_sum = pick(token_sum, pl.y, 0).astype(full) + after(token_got, chip_grad).astype(full)
     token_got = pl.send(pick(token_sum, 1 - pl.lo, 1).astype(low), dlo=1)
-    emb_part = after(chip_grad, far, token_sum)[emb_n : 2 * emb_n].astype(low)
+    emb_part = after(chip_grad, near[1:], far, token_sum)[emb_n : 2 * emb_n].astype(low)
     emb_got = pl.send(emb_part, dc=1)
     query_term = cross_end(pl, query_state, emb_part)
     token_sum = pick(token_sum, pl.lo, 1) + after(token_got, emb_part).astype(full)

time: 1010 us -> 945 us (0.936)
  waiting for transfers between devices: 85.2 us -> 60.6 us
  other arithmetic: 200 us -> 183 us
    ppermute x31, waiting for transfers between devices: 35.4 us -> 22.8 us  [send(): return lax.ppermute(value, ('dp', 'seq'), pairs)]
    all_gather x1, waiting for transfers between devices: 47.4 us -> 35.6 us  [on_device(): attn_full = lax.all_gather(attn_block, ('dp', 'seq'), axis=0, tiled=True)]
    unnamed x210 -> x178, local copies, waits for them, and re-layouts: 22.8 us -> 26.9 us
  transfers between devices with their start and end apart: 37 -> 37, of which waited for: 8 -> 9; matrix products, arithmetic and copies ran while one was open for 28% -> 28% of each run, Pallas kernels for 32% -> 33%
where the time goes in v5:
time: 945 us; the launch traced here: 940 us
  Pallas kernels  414 us (44%)
  other arithmetic  183 us (19%)
  local copies, waits for them, and re-layouts  109 us (12%)
  matrix products  103 us (11%)
  waiting for transfers between devices  60.6 us (6%)
  starting transfers between devices  44 us (5%)
  between operations  26.6 us (3%)
    pallas_call x6, Pallas kernels, move(): pallas.pallas_call(body, out_shape=tuple((jax.ShapeDtypeStruct(shape, dty...  250 us
    pallas_call x1, Pallas kernels, gather_rows(): pallas.pallas_call(functools.partial(rows_body, his), out_shape=jax.Shape...  55.4 us
    dot_general x6, matrix products, matmul(): return jnp.dot(left, right, preferred_element_type=jnp.float32)  38.5 us
    gather x4, local copies, waits for them, and re-layouts, look(): rows = jnp.take(emb, jnp.clip(at, 0, emb_n - 1), axis=0, mode='clip')  36.8 us
    dot_general x6, matrix products, matmul_nt(): lax.dot_general(left, right, (((1,), (1,)), ((), ())), preferred_element_...  36.6 us
    ppermute x31, starting transfers between devices, send(): return lax.ppermute(value, ('dp', 'seq'), pairs)  35.9 us
    all_gather x1, waiting for transfers between devices, on_device(): attn_full = lax.all_gather(attn_block, ('dp', 'seq'), axis=0, tiled=True)  35.6 us
    dot_general x7, matrix products, matmul_tn(): lax.dot_general(left, right, (((0,), (0,)), ((), ())), preferred_element_...  28.4 us
  transfers between devices with their start and end apart: 37, of which 9 were waited for; matrix products, arithmetic and copies ran while one was open for 28% of the time, Pallas kernels for 33%

profile of v5, /device:TPU:0, one launch (start us, length us, event | category | flops | bytes accessed | tf_op | source)
XLA Modules:
  0.0 939.9 jit_solution(13421101444239566299)
XLA Ops:
  21.0 9.6 %gather_fusion = bf16[2560,256]{1,0:T(8,128)(2,1)S(1)} fusion(f32[8000,256]{1,0:T(8,128)} %param.22, s32[3072]{0:T(1024)S(1)} %pad_clamp_fusion.3), kind=kCustom, calls=%fused_computation | custom fusion | bytes 2631680 | tf_op jit(solution)/shard_map/jit(_take)/gather | solution.py:1070
  40.4 9.1 gather_fusion.1
  51.6 9.1 gather_fusion.2
  63.4 9.1 gather_fusion.3
  77.4 55.4 %gather_rows.1 = bf16[8,320,256]{2,1,0:T(8,128)(2,1)S(1)} custom-call(bf16[8,320,256]{2,1,0:T(8,128)(2,1)S(1)} %bitcast.288, bf16[8,320,256]{2,1,0:T(8,128)(2,1)S(1)} %bitcast.289), custom_call_target="tpu_custom_call" | custom-call | flops 1024 | bytes 1024 | tf_op jit(solution)/shard_map/gather_rows/pallas_call | solution.py:943
  170.9 35.6 %all-gather.3.cloned.1.call-done = bf16[2048,4736]{1,0:T(8,128)(2,1)} async-done(((bf16[64,4736]{1,0:T(8,128)(2,1)}), bf16[2048,4736]{1,0:T(8,128)(2,1)}) %all-gather.3.cloned.1.call-update) | async-done | bytes 19398672 | tf_op jit(solution)/shard_map/all_gather | solution.py:1088
  214.9 37.3 %shard_map.337 = bf16[4,2,256,512]{3,2,1,0:T(8,128)(2,1)S(1)} custom-call(f32[256,512]{1,0:T(8,128)S(1)} %fusion.44.projected, f32[256,128]{1,0:T(8,128)S(1)} %get-tuple-element.387.cosine, f32[256,128]{1,0:T(8,128)S(1)} %get-tuple-element.388.sine), custom_call_target="tpu_custom_call" | custom-call | flops 1024 | bytes 1024 | tf_op jit(solution)/shard_map/pallas_call | solution.py:704
  270.0 24.5 %attend.1 = (bf16[8,256,64]{2,1,0:T(8,128)(2,1)}, bf16[64,2048]{1,0:T(8,128)(2,1)}, f32[8,256,64]{2,1,0:T(8,128)}, f32[8,256,128]{2,1,0:T(8,128)}, bf16[2,4,64,2048]{3,2,1,0:T(8,128)(2,1)}) custom-call(f32[64,2048]{1,0:T(8,128)} %fusion.12.raw, f32[64,128]{1,0:T(8,128)} %get-tuple-element.389.cosine, f32[64,128]{1,0:T(8,128)} %get-tuple-element.390.sine, ...), custom_call_target="tpu_custom_call" | custom-call | flops 1024 | bytes 1024 | tf_op jit(solution)/shard_map/attend/pallas_call | solution.py:801
  301.8 35.6 %shard_map.338 = (bf16[4,2,64,2048]{3,2,1,0:T(8,128)(2,1)S(1)}, bf16[8,64,256]{2,1,0:T(8,128)(2,1)S(1)}) custom-call(f32[64,2048]{1,0:T(8,128)S(1)} %fusion.36.values.middle, f32[1,2048]{1,0:T(1,128)S(1)} %get-tuple-element.357.gain, bf16[8,64,256]{2,1,0:T(8,128)(2,1)S(1)} %bitcast.296), custom_call_target="tpu_custom_call" | custom-call | flops 1024 | bytes 1024 | tf_op jit(solution)/shard_map/pallas_call | solution.py:704
  348.1 55.4 %shard_map.339 = (f32[64,2048]{1,0:T(8,128)S(1)}, bf16[4,2,64,2048]{3,2,1,0:T(8,128)(2,1)S(1)}) custom-call(f32[4,2,64,2048]{3,2,1,0:T(8,128)} %bitcast.325, f32[64,2048]{1,0:T(8,128)S(1)} %fusion.36.values.middle, f32[1,2048]{1,0:T(1,128)S(1)} %get-tuple-element.356.gain), custom_call_target="tpu_custom_call" | custom-call | flops 1024 | bytes 1024 | tf_op jit(solution)/shard_map/pallas_call | solution.py:704
  403.6 12.6 %fusion.119 = (f32[512]{0:T(512)S(1)}, f32[512,4000]{0,1:T(8,128)S(1)}) fusion(bf16[512,2048]{1,0:T(8,128)(2,1)S(1)} %bitcast.301, bf16[4000,2048]{1,0:T(8,128)(2,1)} %all-gather.5.cloned.1.call-done), kind=kOutput, calls=%fused_computation.334 | convolution fusion | flops 8390655488 | bytes 26675200 | tf_op jit(solution)/shard_map/dot_general | solution.py:78
  438.1 15.2 %fusion.120 = f32[512,2048]{1,0:T(8,128)} fusion(bf16[512,4000]{0,1:T(8,128)(2,1)S(1)} %fusion.5, bf16[4000,2048]{1,0:T(8,128)(2,1)} %all-gather.5.cloned.1.call-done), kind=kOutput, calls=%fused_computation.335 | convolution fusion | flops 8388608000 | bytes 24674304 | tf_op jit(solution)/shard_map/dot_general | solution.py:74
  453.3 58.9 %shard_map.340 = (f32[64,2048]{1,0:T(8,128)S(1)}, f32[1,2048]{1,0:T(1,128)S(1)}, bf16[4,2,64,2048]{3,2,1,0:T(8,128)(2,1)S(1)}) custom-call(f32[4,2,64,2048]{3,2,1,0:T(8,128)} %bitcast.324, f32[64,2048]{1,0:T(8,128)S(1)} %get-tuple-element.136.ending, f32[1,2048]{1,0:T(1,128)S(1)} %get-tuple-element.356.gain), custom_call_target="tpu_custom_call" | custom-call | flops 1024 | bytes 1024 | tf_op jit(solution)/shard_map/pallas_call | solution.py:704
  537.1 11.5 %convolution_convert_fusion = bf16[4000,2048]{1,0:T(8,128)(2,1)} fusion(bf16[512,4000]{0,1:T(8,128)(2,1)S(1)} %copy-done.28, bf16[512,2048]{1,0:T(8,128)(2,1)S(1)} %bitcast.302), kind=kOutput, calls=%fused_computation.6 | convolution fusion | flops 8396800000 | bytes 22577152 | tf_op jit(solution)/shard_map/dot_general | solution.py:84
  563.2 26.5 %shard_map.341 = (f32[64,2048]{1,0:T(8,128)S(1)}, bf16[64,2048]{1,0:T(8,128)(2,1)S(1)}, f32[1,2048]{1,0:T(1,128)S(1)}) custom-call(f32[4,2,64,2048]{3,2,1,0:T(8,128)S(1)} %bitcast.290, f32[64,2048]{1,0:T(8,128)S(1)} %fusion.36.values.middle, f32[1,2048]{1,0:T(1,128)S(1)} %get-tuple-element.357.gain, f32[64,2048]{1,0:T(8,128)S(1)} %get-tuple-element.141.ending_grad), custom_call_target="tpu_custom_call" | custom-call | flops 1024 | bytes 1024 | tf_op jit(solution)/shard_map/pallas_call | solution.py:704
  595.5 26.5 %attend_back.1 = (bf16[64,2048]{1,0:T(8,128)(2,1)}, f32[2048,512]{1,0:T(8,128)}, bf16[2,4,64,2048]{3,2,1,0:T(8,128)(2,1)}) custom-call(bf16[64,2048]{1,0:T(8,128)(2,1)} %fusion.39.grad, f32[64,128]{1,0:T(8,128)} %get-tuple-element.389.cosine, f32[64,128]{1,0:T(8,128)} %get-tuple-element.390.sine, s32[64,1]{1,0:T(8,128)} %copy.146.places, ...), custom_call_target="tpu_custom_call" | custom-call | flops 1024 | bytes 1024 | tf_op jit(solution)/shard_map/attend_back/pallas_call | solution.py:874
  643.7 36.2 %shard_map.342 = (bf16[256,512]{1,0:T(8,128)(2,1)S(1)}, bf16[8,64,256]{2,1,0:T(8,128)(2,1)S(1)}) custom-call(f32[4,2,256,512]{3,2,1,0:T(8,128)S(1)} %bitcast.291, f32[256,128]{1,0:T(8,128)S(1)} %get-tuple-element.387.cosine, f32[256,128]{1,0:T(8,128)S(1)} %get-tuple-element.388.sine, bf16[8,64,256]{2,1,0:T(8,128)(2,1)S(1)} %bitcast.295), custom_call_target="tpu_custom_call" | custom-call | flops 1024 | bytes 1024 | tf_op jit(solution)/shard_map/pallas_call | solution.py:704
  750.9 20.3 %scatter_custom_fusion = f32[16008,256]{1,0:T(8,128)} fusion(s32[2560]{0:T(1024)} %get-tuple-element.309, f32[]{:T(128)} %constant.315.clone.1, bf16[2560,256]{1,0:T(8,128)(2,1)} %bitcast.55), kind=kCustom, calls=%fused_computation.14 | custom fusion | flops 1310720 | bytes 17703424 | tf_op jit(solution)/shard_map/scatter-add | solution.py:1340
  777.4 8.4 fusion.14
  785.8 26.3 %scatter_custom_fusion.1 = f32[16008,256]{1,0:T(8,128)} fusion(f32[16008,256]{1,0:T(8,128)} %scatter_custom_fusion, s32[2560]{0:T(1024)S(1)} %compare_select_fusion.2, bf16[2560,256]{1,0:T(8,128)(2,1)} %collective-permute-done.22), kind=kCustom, calls=%fused_computation.87 | custom fusion | flops 1310720 | bytes 17702912 | tf_op jit(solution)/shard_map/scatter-add | solution.py:1350
  842.9 8.2 fusion.17
  851.1 22.2 %layer_gradient.1 = (f32[64,4608]{1,0:T(8,128)S(1)}, f32[64,128]{1,0:T(8,128)S(1)}, f32[64,1]{1,0:T(8,128)S(1)}, f32[1,4608]{1,0:T(1,128)S(1)}) custom-call(bf16[8,64,512]{2,1,0:T(8,128)(2,1)S(1)} %bitcast.294, f32[4,64,640]{2,1,0:T(8,128)S(1)} %bitcast_add_fusion.tokens), custom_call_target="tpu_custom_call" | custom-call | flops 1024 | bytes 1024 | tf_op jit(solution)/shard_map/layer_gradient/pallas_call | solution.py:611
  874.8 21.9 %sum_statistics.1 = f32[296,128]{1,0:T(8,128)S(1)} custom-call(f32[296,128]{1,0:T(8,128)S(1)} %constant_dynamic-update-slice_fusion.2.packed), custom_call_target="tpu_custom_call" | custom-call | tf_op jit(solution)/shard_map/sum_statistics/pallas_call | solution.py:1006
  911.2 12.0 %multiply_subtract_fusion.1 = f32[8000,256]{1,0:T(8,128)} fusion(f32[8000,256]{1,0:T(8,128)} %param.22, f32[8000,256]{1,0:T(8,128)} %get-tuple-element.414, f32[]{:T(128)} %bitcast.115, f32[256]{0:T(256)S(1)} %bitcast_add_fusion.4, f32[8000]{0:T(1024)S(1)} %fusion.87, f32[]{:T(128)} %bitcast.112), kind=kLoop, calls=%fused_computation.23 | loop fusion | flops 10240000 | bytes 24609032 | tf_op jit(solution)/shard_map/sub | solution.py:90
  (437 shorter events, 326.1 us)
Async XLA Ops:
  7.2 199.2 %all-gather.3.cloned.1.call-start = ((), (), s32[]{:S(2)}) async-start(), calls=%async_computation.2 | async-start | bytes 20004864 | tf_op jit(solution)/shard_map/all_gather | solution.py:1088
  11.0 392.6 %all-gather.5.cloned.1.call-start = ((), (), s32[]{:S(2)}) async-start(), calls=%async_computation.3 | async-start | bytes 20480000 | tf_op jit(solution)/shard_map/all_gather | solution.py:1122
  34.3 100.7 %collective-permute-start.6 = (bf16[2,64,2112]{2,1,0:T(8,128)(2,1)}, bf16[2,64,2112]{2,1,0:T(8,128)(2,1)S(1)}, u32[]{:S(2)}, u32[]{:S(2)}) collective-permute-start(bf16[2,64,2112]{2,1,0:T(8,128)(2,1)} %get-tuple-element.330), channel_id=1, source_target_pairs={{0,2},{1,3},{2,4},{3,5},{4,6},{5,7},{6,0},{7,1},{8,10},{9,11},{10,... | collective-permute-start | bytes 1622024 | tf_op jit(solution)/shard_map/ppermute | solution.py:114
  36.3 98.7 %collective-permute-start.7 = (bf16[2,64,2112]{2,1,0:T(8,128)(2,1)}, bf16[2,64,2112]{2,1,0:T(8,128)(2,1)}, u32[]{:S(2)}, u32[]{:S(2)}) collective-permute-start(bf16[2,64,2112]{2,1,0:T(8,128)(2,1)} %get-tuple-element.331), channel_id=1, source_target_pairs={{0,4},{1,5},{2,6},{3,7},{4,0},{5,1},{6,2},{7,3},{8,12},{9,13},{10,... | collective-permute-start | bytes 1622024 | tf_op jit(solution)/shard_map/ppermute | solution.py:114
  38.8 96.2 %collective-permute-start.8 = (bf16[2,64,2112]{2,1,0:T(8,128)(2,1)}, bf16[2,64,2112]{2,1,0:T(8,128)(2,1)}, u32[]{:S(2)}, u32[]{:S(2)}) collective-permute-start(bf16[2,64,2112]{2,1,0:T(8,128)(2,1)} %get-tuple-element.328), channel_id=1, source_target_pairs={{0,6},{1,7},{2,0},{3,1},{4,2},{5,3},{6,4},{7,5},{8,14},{9,15},{10,... | collective-permute-start | bytes 1622024 | tf_op jit(solution)/shard_map/ppermute | solution.py:114
  138.7 114.8 %collective-permute-start.9 = (bf16[2,4,64,2112]{3,2,1,0:T(8,128)(2,1)}, bf16[2,4,64,2112]{3,2,1,0:T(8,128)(2,1)S(1)}, u32[]{:S(2)}, u32[]{:S(2)}) collective-permute-start(bf16[2,4,64,2112]{3,2,1,0:T(8,128)(2,1)} %bitcast.278), channel_id=1, source_target_pairs={{0,1},{1,0},{2,3},{3,2},{4,5},{5,4},{6,7},{7,6},{8,9},{9,8},{10,11... | collective-permute-start | bytes 6488072 | tf_op jit(solution)/shard_map/ppermute | solution.py:114
  146.2 107.4 %collective-permute-start.10 = (bf16[2,4,64,2112]{3,2,1,0:T(8,128)(2,1)}, bf16[2,4,64,2112]{3,2,1,0:T(8,128)(2,1)}, u32[]{:S(2)}, u32[]{:S(2)}) collective-permute-start(bf16[2,4,64,2112]{3,2,1,0:T(8,128)(2,1)} %bitcast.279), channel_id=1, source_target_pairs={{0,16},{1,17},{2,18},{3,19},{4,20},{5,21},{6,22},{7,23},{8,24},{9,... | collective-permute-start | bytes 6488072 | tf_op jit(solution)/shard_map/ppermute | solution.py:114
  253.6 523.8 %reduce-scatter.2.cloned.1.call-start = ((), (), s32[]{:S(2)}) async-start(), calls=%async_computation.4 | async-start | bytes 20480000 | tf_op jit(solution)/shard_map/reduce_scatter | solution.py:1219
  258.6 78.9 %collective-permute-start.11 = (bf16[4,64,2112]{2,1,0:T(8,128)(2,1)}, bf16[4,64,2112]{2,1,0:T(8,128)(2,1)S(1)}, u32[]{:S(2)}, u32[]{:S(2)}) collective-permute-start(bf16[4,64,2112]{2,1,0:T(8,128)(2,1)} %slice_bitcast_fusion.1), channel_id=1, source_target_pairs={{0,16},{1,17},{2,18},{3,19},{4,20},{5,21},{6,22},{7,23},{8,24},{9,... | collective-permute-start | bytes 3244040 | tf_op jit(solution)/shard_map/ppermute | solution.py:114
  262.6 74.9 %collective-permute-start.12 = (bf16[4,64,2112]{2,1,0:T(8,128)(2,1)}, bf16[4,64,2112]{2,1,0:T(8,128)(2,1)S(1)}, u32[]{:S(2)}, u32[]{:S(2)}) collective-permute-start(bf16[4,64,2112]{2,1,0:T(8,128)(2,1)} %slice_bitcast_fusion), channel_id=1, source_target_pairs={{0,1},{1,0},{2,3},{3,2},{4,5},{5,4},{6,7},{7,6},{8,9},{9,8},{10,11... | collective-permute-start | bytes 3244040 | tf_op jit(solution)/shard_map/ppermute | solution.py:114
  556.9 78.2 %collective-permute-start.16 = (bf16[4,2,64,2112]{3,2,0,1:T(8,128)(2,1)}, bf16[4,2,64,2112]{3,2,0,1:T(8,128)(2,1)}, u32[]{:S(2)}, u32[]{:S(2)}) collective-permute-start(bf16[4,2,64,2112]{3,2,0,1:T(8,128)(2,1)} %bitcast.265), channel_id=1, source_target_pairs={{0,16},{1,17},{2,18},{3,19},{4,20},{5,21},{6,22},{7,23},{8,24},{9,... | collective-permute-start | bytes 6488072 | tf_op jit(solution)/shard_map/ppermute | solution.py:114
  560.0 75.1 %collective-permute-start.17 = (bf16[2,4,64,2112]{3,2,1,0:T(8,128)(2,1)}, bf16[2,4,64,2112]{3,2,1,0:T(8,128)(2,1)}, u32[]{:S(2)}, u32[]{:S(2)}) collective-permute-start(bf16[2,4,64,2112]{3,2,1,0:T(8,128)(2,1)} %dynamic-slice_bitcast_fusion.2), channel_id=1, source_target_pairs={{0,1},{1,0},{2,3},{3,2},{4,5},{5,4},{6,7},{7,6},{8,9},{9,8},{10,11... | collective-permute-start | bytes 6488072 | tf_op jit(solution)/shard_map/ppermute | solution.py:114
  685.5 37.4 %all-to-all-start = ((bf16[320,8,256]{2,0,1:T(8,128)(2,1)}), bf16[320,8,256]{2,0,1:T(8,128)(2,1)}, u32[]{:S(2)}, u32[]{:S(2)}) async-start(bf16[320,8,256]{2,0,1:T(8,128)(2,1)} %pad_maximum_fusion.4), calls=%async_computation | async-start | bytes 2621440 | tf_op jit(solution)/shard_map/all_to_all | solution.py:1275
  699.8 30.1 %collective-permute-start.19 = (bf16[4,64,2112]{2,1,0:T(8,128)(2,1)}, bf16[4,64,2112]{2,1,0:T(8,128)(2,1)}, u32[]{:S(2)}, u32[]{:S(2)}) collective-permute-start(bf16[4,64,2112]{2,1,0:T(8,128)(2,1)} %fusion.49), channel_id=1, source_target_pairs={{0,1},{1,0},{2,3},{3,2},{4,5},{5,4},{6,7},{7,6},{8,9},{9,8},{10,11... | collective-permute-start | bytes 3244040 | tf_op jit(solution)/shard_map/ppermute | solution.py:114
  701.8 28.1 %collective-permute-start.20 = (bf16[4,64,2112]{2,1,0:T(8,128)(2,1)}, bf16[4,64,2112]{2,1,0:T(8,128)(2,1)}, u32[]{:S(2)}, u32[]{:S(2)}) collective-permute-start(bf16[4,64,2112]{2,1,0:T(8,128)(2,1)} %fusion.50), channel_id=1, source_target_pairs={{0,16},{1,17},{2,18},{3,19},{4,20},{5,21},{6,22},{7,23},{8,24},{9,... | collective-permute-start | bytes 3244040 | tf_op jit(solution)/shard_map/ppermute | solution.py:114
  712.5 28.7 %collective-permute-start.18 = (bf16[1024,640]{0,1:T(8,128)(2,1)}, bf16[1024,640]{0,1:T(8,128)(2,1)}, u32[]{:S(2)}, u32[]{:S(2)}) collective-permute-start(bf16[1024,640]{0,1:T(8,128)(2,1)} %fusion.47), channel_id=1, source_target_pairs={{0,8},{1,9},{2,10},{3,11},{4,12},{5,13},{6,14},{7,15},{8,0},{9,1},... | collective-permute-start | bytes 3932168 | tf_op jit(solution)/shard_map/ppermute | solution.py:114
  737.8 33.5 %collective-permute-start.24 = (bf16[4,2,64,512]{3,2,0,1:T(8,128)(2,1)}, bf16[4,2,64,512]{3,2,0,1:T(8,128)(2,1)}, u32[]{:S(2)}, u32[]{:S(2)}) collective-permute-start(bf16[4,2,64,512]{3,2,0,1:T(8,128)(2,1)} %bitcast.268), channel_id=1, source_target_pairs={{0,16},{1,17},{2,18},{3,19},{4,20},{5,21},{6,22},{7,23},{8,24},{9,... | collective-permute-start | bytes 1572872 | tf_op jit(solution)/shard_map/ppermute | solution.py:114
  740.1 31.1 %collective-permute-start.25 = (bf16[2,4,64,512]{3,2,1,0:T(8,128)(2,1)}, bf16[2,4,64,512]{3,2,1,0:T(8,128)(2,1)}, u32[]{:S(2)}, u32[]{:S(2)}) collective-permute-start(bf16[2,4,64,512]{3,2,1,0:T(8,128)(2,1)} %dynamic-slice_bitcast_fusion.7), channel_id=1, source_target_pairs={{0,1},{1,0},{2,3},{3,2},{4,5},{5,4},{6,7},{7,6},{8,9},{9,8},{10,11... | collective-permute-start | bytes 1572872 | tf_op jit(solution)/shard_map/ppermute | solution.py:114
  740.6 45.1 %collective-permute-start.22 = (bf16[2560,256]{1,0:T(8,128)(2,1)}, bf16[2560,256]{1,0:T(8,128)(2,1)}, u32[]{:S(2)}, u32[]{:S(2)}) collective-permute-start(bf16[2560,256]{1,0:T(8,128)(2,1)} %bitcast.55), channel_id=1, source_target_pairs={{0,16},{1,17},{2,18},{3,19},{4,20},{5,21},{6,22},{7,23},{8,24},{9,... | collective-permute-start | bytes 3932168 | tf_op jit(solution)/shard_map/ppermute | solution.py:114
  744.8 67.3 %collective-permute-start.28 = (bf16[4,2,64,640]{3,2,0,1:T(8,128)(2,1)S(1)}, bf16[4,2,64,640]{3,2,0,1:T(8,128)(2,1)S(1)}, u32[]{:S(2)}, u32[]{:S(2)}) collective-permute-start(bf16[4,2,64,640]{3,2,0,1:T(8,128)(2,1)S(1)} %bitcast.335), channel_id=1, source_target_pairs={{0,16},{1,17},{2,18},{3,19},{4,20},{5,21},{6,22},{7,23},{8,24},{9,... | collective-permute-start | bytes 1966088 | tf_op jit(solution)/shard_map/ppermute | solution.py:114
  749.0 36.8 %collective-permute-start.23 = (bf16[2,64,2112]{2,1,0:T(8,128)(2,1)}, bf16[2,64,2112]{2,1,0:T(8,128)(2,1)}, u32[]{:S(2)}, u32[]{:S(2)}) collective-permute-start(bf16[2,64,2112]{2,1,0:T(8,128)(2,1)} %get-tuple-element.323), channel_id=1, source_target_pairs={{0,2},{1,3},{2,4},{3,5},{4,6},{5,7},{6,0},{7,1},{8,10},{9,11},{10,... | collective-permute-start | bytes 1622024 | tf_op jit(solution)/shard_map/ppermute | solution.py:114
  775.5 36.7 %collective-permute-start.26 = (bf16[2,64,2112]{2,1,0:T(8,128)(2,1)}, bf16[2,64,2112]{2,1,0:T(8,128)(2,1)}, u32[]{:S(2)}, u32[]{:S(2)}) collective-permute-start(bf16[2,64,2112]{2,1,0:T(8,128)(2,1)} %get-tuple-element.324), channel_id=1, source_target_pairs={{0,6},{1,7},{2,0},{3,1},{4,2},{5,3},{6,4},{7,5},{8,14},{9,15},{10,... | collective-permute-start | bytes 1622024 | tf_op jit(solution)/shard_map/ppermute | solution.py:114
  777.4 36.0 %collective-permute-start.27 = (bf16[2,64,2112]{2,1,0:T(8,128)(2,1)}, bf16[2,64,2112]{2,1,0:T(8,128)(2,1)}, u32[]{:S(2)}, u32[]{:S(2)}) collective-permute-start(bf16[2,64,2112]{2,1,0:T(8,128)(2,1)} %get-tuple-element.325), channel_id=1, source_target_pairs={{0,4},{1,5},{2,6},{3,7},{4,0},{5,1},{6,2},{7,3},{8,12},{9,13},{10,... | collective-permute-start | bytes 1622024 | tf_op jit(solution)/shard_map/ppermute | solution.py:114
  819.1 23.8 %collective-permute-start.29 = (bf16[8000,256]{1,0:T(8,128)(2,1)}, bf16[8000,256]{1,0:T(8,128)(2,1)}, u32[]{:S(2)}, u32[]{:S(2)}) collective-permute-start(bf16[8000,256]{1,0:T(8,128)(2,1)} %slice.403), channel_id=1, source_target_pairs={{0,8},{1,9},{2,10},{3,11},{4,12},{5,13},{6,14},{7,15},{8,0},{9,1},... | collective-permute-start | bytes 12288008 | tf_op jit(solution)/shard_map/ppermute | solution.py:114
  (93 other events, 1643.1 us)
Sparse Core Ops, SparseCore 0:
  11.5 194.9 all-gather.2
  253.7 119.2 all-gather.4
  548.6 148.3 reduce-scatter.1
